TPU v7x, 128 devices: a whole 4x4x4 slice. The times are simulated.
128 devices in a mesh: dp: 16 (over x, z), fsdp: 8 (over y, core).
Axes of the slice: x: 4, y: 4, z: 4, core: 2. Of those that a mesh axis runs over, the one named last changes fastest.
Arguments:
- points: bfloat16 [262144, 512], P(('dp', 'fsdp')), may hold values from -8 to 8
- cotangent: bfloat16 [262144, 512], P(('dp', 'fsdp')), may hold values from -6 to 6
- destination: int32 [262144], P(('dp', 'fsdp')), may hold values from 0 to 127, as said below
- curve_slot: int32 [262144], P(('dp', 'fsdp')), may hold values from 0 to 1023, as said below
- point_counts: int32 [128], P(('dp', 'fsdp')), may hold values from 0 to 2048, as said below
- shift_offset: int32 [1], replicated, may hold values from 1 to 1023
- project_in: bfloat16 [512, 1536], P('fsdp'), may hold values from -8 to 8
- project_out: bfloat16 [512, 512], P('fsdp'), may hold values from -0.5 to 0.5
- norm_gain: bfloat16 [512], P('fsdp'), may hold values from 0.099609375 to 1.8984375
Outputs:
- block_out: bfloat16 [262144, 512], P(('dp', 'fsdp'))
- point_grad: bfloat16 [262144, 512], P(('dp', 'fsdp'))
- grad_in: float32 [512, 1536], P('fsdp')
- grad_out: float32 [512, 512], P('fsdp')
- grad_gain: float32 [512], P('fsdp')
Inputs may be any that keep to these rules, and one draw needn't show every extreme that they name: Rows at or past their device's count carry no meaning. Among the counting rows of one device at most 16 name one destination, and some device sends exactly 16 to every destination. Over the counting rows of all devices every pair of destination and curve_slot occurs exactly once. `point_counts`: they sum to 131072; some device holds exactly 2048.
All inputs are finite; a program needn't handle non-finite values.
Results may differ from a plain program's by a relative error of at most 0.006.
The roundings to bfloat16 on the way count: a program that leaves them out, or rounds other values in their place, can miss the bound.
Values may be sent and summed in bfloat16 or wider, within the bound.
No kernel may reach another device: no remote copies, remote signals or barrier semaphores. Data moves between devices by JAX's collectives and lax.ppermute only.
A program may use at most 128 MiB of HBM per device.

v0:
```python
import math

import jax
import jax.numpy as jnp
from jax import lax
from jax.sharding import PartitionSpec as P

HEADS = 16
PATCH = 1024


EPS = 1e-05


def extended_2(cells, sides, width):
    for axis, dim in sides:
        count = lax.axis_size(axis)
        ends = count - 1
        head = lax.slice_in_dim(cells, 0, width, axis=dim)
        tail = lax.slice_in_dim(cells, cells.shape[dim] - width, cells.shape[dim], axis=dim)
        cells = jnp.concatenate(
            [
                lax.ppermute(tail, axis, [(i, (i + 1) % count) for i in range(ends)]),
                cells,
                lax.ppermute(head, axis, [((i + 1) % count, i) for i in range(ends)]),
            ],
            axis=dim,
        )
    return cells


def layer_stats(values_in):
    values = values_in.astype(jnp.float32)
    center = values - jnp.mean(values, axis=-1, keepdims=True)
    inverse = lax.rsqrt(jnp.mean(center * center, axis=-1, keepdims=True) + EPS)
    return (center * inverse, inverse)


def split_heads(block, blocks, heads):
    length = block.shape[0] // blocks
    head_width = block.shape[1] // heads
    group = math.gcd(heads, 4)
    shaped = block.reshape(blocks, length, heads // group, group, head_width)
    return jnp.transpose(shaped, (0, 2, 1, 3, 4)).reshape(
        blocks * (heads // group), length, group, head_width
    )


def join_heads(items, blocks):
    total_items, length, group, head_width = items.shape
    groups = total_items // blocks
    shaped = items.reshape(blocks, groups, length, group, head_width)
    return jnp.transpose(shaped, (0, 2, 1, 3, 4)).reshape(
        blocks * length, groups * group * head_width
    )


def probabilities(query, keys, query_code, key_code):
    scale = query.shape[-1] ** (-0.5)
    scores = jnp.einsum("qhe,khe->hqk", query, keys, preferred_element_type=jnp.float32) * scale
    allowed = query_code[:, None] == key_code[None, :]
    scores = jnp.where(allowed[None, :, :], scores, -1e30)
    top = jnp.max(scores, axis=-1, keepdims=True)
    weights = jnp.exp(scores - top)
    return weights / jnp.sum(weights, axis=-1, keepdims=True)


def forward_item(item):
    query, keys, values, query_code, key_code = item
    probs_b = probabilities(query, keys, query_code, key_code).astype(jnp.bfloat16)
    return jnp.einsum("hqk,khe->qhe", probs_b, values, preferred_element_type=jnp.float32).astype(
        jnp.bfloat16
    )


def backward_item(item):
    query, keys, values, output, upstream, query_code, key_code = item
    scale = query.shape[-1] ** (-0.5)
    probs = probabilities(query, keys, query_code, key_code)
    probs_b = probs.astype(jnp.bfloat16)
    along = jnp.einsum("qhe,khe->hqk", upstream, values, preferred_element_type=jnp.float32)
    offset = jnp.sum(upstream.astype(jnp.float32) * output.astype(jnp.float32), axis=-1)
    slopes = (probs * (along - jnp.transpose(offset)[:, :, None]) * scale).astype(jnp.bfloat16)
    query_grad = jnp.einsum("hqk,khe->qhe", slopes, keys, preferred_element_type=jnp.float32)
    key_grad = jnp.einsum("hqk,qhe->khe", slopes, query, preferred_element_type=jnp.float32)
    value_grad = jnp.einsum("hqk,qhe->khe", probs_b, upstream, preferred_element_type=jnp.float32)
    return (query_grad, key_grad, value_grad)


def regroup(rows_buffer, marks):
    moved_rows, moved_marks = (
        lax.all_to_all(rows_buffer, ("dp", "fsdp"), split_axis=0, concat_axis=0, tiled=True),
        lax.all_to_all(marks, ("dp", "fsdp"), split_axis=0, concat_axis=0, tiled=True),
    )
    return (moved_rows, moved_marks)


def patch_work(
    rows_in,
    cot_in,
    query_codes,
    key_codes,
    blocks,
    own_start,
    own_rows,
    full_in,
    full_out,
    full_gain,
):
    width = rows_in.shape[1]
    heads = HEADS
    patch = rows_in.shape[0] // blocks
    groups = heads // math.gcd(heads, 4)
    query_items = jnp.repeat(query_codes.reshape(blocks, patch), groups, axis=0)
    key_items = jnp.repeat(key_codes.reshape(blocks, patch), groups, axis=0)
    normed, inv_std = layer_stats(rows_in)
    gain = full_gain.astype(jnp.float32)
    hidden = (normed * gain).astype(jnp.bfloat16)
    projected = jnp.dot(hidden, full_in, preferred_element_type=jnp.float32).astype(jnp.bfloat16)
    queries = split_heads(projected[:, :width], blocks, heads)
    keyset = split_heads(projected[:, width : 2 * width], blocks, heads)
    valueset = split_heads(projected[:, 2 * width :], blocks, heads)
    att_items = lax.map(forward_item, (queries, keyset, valueset, query_items, key_items))
    attended = join_heads(att_items, blocks)
    attended_own = lax.dynamic_slice_in_dim(attended, own_start, own_rows, 0)
    rows_own = lax.dynamic_slice_in_dim(rows_in, own_start, own_rows, 0)
    cot_own = lax.dynamic_slice_in_dim(cot_in, own_start, own_rows, 0)
    curve_out = (
        rows_own.astype(jnp.float32)
        + jnp.dot(attended_own, full_out, preferred_element_type=jnp.float32)
    ).astype(jnp.bfloat16)
    grad_att = lax.dot_general(
        cot_in, full_out, (((1,), (1,)), ((), ())), preferred_element_type=jnp.float32
    ).astype(jnp.bfloat16)
    grad_items = split_heads(grad_att, blocks, heads)
    query_grad, key_grad, value_grad = lax.map(
        backward_item, (queries, keyset, valueset, att_items, grad_items, query_items, key_items)
    )
    grad_rows = jnp.concatenate(
        [
            join_heads(query_grad, blocks),
            join_heads(key_grad, blocks),
            join_heads(value_grad, blocks),
        ],
        axis=1,
    ).astype(jnp.bfloat16)
    grad_rows_own = lax.dynamic_slice_in_dim(grad_rows, own_start, own_rows, 0)
    hidden_own = lax.dynamic_slice_in_dim(hidden, own_start, own_rows, 0)
    normed_own = lax.dynamic_slice_in_dim(normed, own_start, own_rows, 0)
    inv_own = lax.dynamic_slice_in_dim(inv_std, own_start, own_rows, 0)
    grad_hidden = lax.dot_general(
        grad_rows_own, full_in, (((1,), (1,)), ((), ())), preferred_element_type=jnp.float32
    )
    part_in = lax.dot_general(
        hidden_own, grad_rows_own, (((0,), (0,)), ((), ())), preferred_element_type=jnp.float32
    )
    part_out = lax.dot_general(
        attended_own, cot_own, (((0,), (0,)), ((), ())), preferred_element_type=jnp.float32
    )
    part_gain = jnp.sum(grad_hidden * normed_own, axis=0)
    scaled = grad_hidden * gain
    curve_grad = (
        cot_own.astype(jnp.float32)
        + inv_own
        * (
            scaled
            - jnp.mean(scaled, axis=-1, keepdims=True)
            - normed_own * jnp.mean(scaled * normed_own, axis=-1, keepdims=True)
        )
    ).astype(jnp.bfloat16)
    return (curve_out, curve_grad, part_in, part_out, part_gain)


def body(
    points,
    cotangent,
    destination,
    curve_slot,
    point_counts,
    shift_offset,
    project_in,
    project_out,
    norm_gain,
):
    devices = lax.axis_size(("dp", "fsdp"))
    arrived, width = points.shape
    capacity = arrived // devices
    slots = devices * capacity
    own_rows = arrived // 2
    patch = PATCH
    order = jnp.arange(arrived, dtype=jnp.int32)
    valid = order < point_counts[0]
    earlier = (
        (destination[None, :] == destination[:, None])
        & valid[None, :]
        & (order[None, :] < order[:, None])
    )
    ranking = jnp.sum(earlier.astype(jnp.int32), axis=1)
    target = jnp.where(valid, destination * capacity + ranking, slots)
    source_row = jnp.full((slots,), arrived, jnp.int32).at[target].set(order, mode="drop")
    digits = jnp.stack([curve_slot // 64 + 1, curve_slot % 64], axis=1).astype(jnp.bfloat16)
    paired = jnp.stack([points, cotangent], axis=1)
    padded_rows = jnp.concatenate([paired, jnp.zeros((1, 2, width), jnp.bfloat16)], axis=0)
    padded_marks = jnp.concatenate([digits, jnp.zeros((1, 2), jnp.bfloat16)], axis=0)
    send_rows = padded_rows[source_row]
    send_marks = padded_marks[source_row]
    got_rows, got_marks = regroup(
        send_rows.reshape(devices, capacity, 2, width), send_marks.reshape(devices, capacity, 2)
    )
    got_rows = got_rows.reshape(slots, 2, width)
    mark_values = got_marks.reshape(slots, 2).astype(jnp.int32)
    present = mark_values[:, 0] > 0
    landing = jnp.where(present, (mark_values[:, 0] - 1) * 64 + mark_values[:, 1], own_rows)
    slot_order = jnp.arange(slots, dtype=jnp.int32)
    curve_source = jnp.zeros((own_rows,), jnp.int32).at[landing].set(slot_order, mode="drop")
    curve = got_rows[curve_source]
    full_in, full_out, full_gain = (
        lax.all_gather(project_in, "fsdp", axis=0, tiled=True),
        lax.all_gather(project_out, "fsdp", axis=0, tiled=True),
        lax.all_gather(norm_gain, "fsdp", axis=0, tiled=True),
    )
    shift = shift_offset[0]
    extended = extended_2(curve, ((("dp", "fsdp"), 0),), patch)
    span = own_rows + patch
    blocks = span // patch
    window = lax.dynamic_slice_in_dim(extended, shift, span, axis=0)
    location = (
        lax.axis_index(("dp", "fsdp")) * own_rows
        + shift
        - patch
        + jnp.arange(span, dtype=jnp.int32)
    )
    keep = ((location >= 0) & (location < devices * own_rows)).astype(jnp.int32)
    ones = jnp.ones((span,), jnp.int32)
    curve_out, curve_grad, part_in, part_out, part_gain = patch_work(
        window[:, 0],
        window[:, 1],
        ones,
        keep,
        blocks,
        patch - shift,
        own_rows,
        full_in,
        full_out,
        full_gain,
    )
    results = jnp.stack([curve_out, curve_grad], axis=1)
    shares = (
        lax.psum_scatter(part_in, "fsdp", scatter_dimension=0, tiled=True),
        lax.psum_scatter(part_out, "fsdp", scatter_dimension=0, tiled=True),
        lax.psum_scatter(part_gain, "fsdp", scatter_dimension=0, tiled=True),
    )
    totals = lax.psum((shares[0], shares[1], shares[2]), "dp")
    picked = results[jnp.minimum(landing, own_rows - 1)]
    back_rows, back_marks = regroup(picked.reshape(devices, capacity, 2, width), got_marks)
    flat_rows = back_rows.reshape(slots, 2, width)
    safe = jnp.minimum(target, slots - 1)
    returned = flat_rows[safe]
    echo = back_marks.reshape(slots, 2)[safe, 0].astype(jnp.int32)
    landed = valid & (echo > 0)
    returned = jnp.where(landed[:, None, None], returned, jnp.zeros((), jnp.bfloat16))
    return (returned[:, 0], returned[:, 1], totals[0], totals[1], totals[2])


def solution(mesh):
    in_specs = (
        P(("dp", "fsdp"), None),
        P(("dp", "fsdp"), None),
        P(("dp", "fsdp")),
        P(("dp", "fsdp")),
        P(("dp", "fsdp")),
        P(),
        P("fsdp", None),
        P("fsdp", None),
        P("fsdp"),
    )
    out_specs = (
        P(("dp", "fsdp"), None),
        P(("dp", "fsdp"), None),
        P("fsdp", None),
        P("fsdp", None),
        P("fsdp"),
    )
    return jax.shard_map(body, mesh=mesh, in_specs=in_specs, out_specs=out_specs, check_vma=False)
```

profile of v0, /device:TPU:0, one launch (start us, length us, event | category | flops | bytes accessed | tf_op | source)
XLA Modules:
  0.0 1038.1 jit_solution(236634763954339619)
XLA Ops:
  33.2 11.7 %all-to-all-start = ((bf16[128,16,2]{1,2,0:T(2,128)(2,1)}), bf16[128,16,2]{1,2,0:T(2,128)(2,1)}, u32[]{:S(2)}, u32[]{:S(2)}) async-start(bf16[128,16,2]{1,2,0:T(2,128)(2,1)} %copy.140), calls=%async_computation | async-start | bytes 131072 | tf_op jit(solution)/shard_map/all_to_all | solution.py:93
  44.9 15.6 %copy.142 = bf16[2048,1,512]{2,1,0:T(2,128)(2,1)S(1)} copy(bf16[2048,1,512]{2,0,1:T(8,128)(2,1)S(1)} %bitcast.260) | data formatting | bytes 4194304 | tf_op jit(solution)/shard_map/stack | solution.py:202
  60.5 15.6 %copy.143 = bf16[2048,1,512]{2,1,0:T(2,128)(2,1)S(1)} copy(bf16[2048,1,512]{2,0,1:T(8,128)(2,1)S(1)} %bitcast.261) | data formatting | bytes 4194304 | tf_op jit(solution)/shard_map/stack | solution.py:202
  76.1 15.7 %fusion.99 = bf16[2049,2,512]{2,1,0:T(2,128)(2,1)} fusion(bf16[2048,1,512]{2,1,0:T(2,128)(2,1)S(1)} %copy.143, bf16[2048,1,512]{2,1,0:T(2,128)(2,1)S(1)} %copy.142), kind=kLoop, calls=%fused_computation.102 | loop fusion | flops 14687232 | bytes 8390656 | tf_op jit(solution)/shard_map/stack | solution.py:202
  91.8 23.6 %gather_fusion.2 = bf16[2048,2,512]{2,1,0:T(2,128)(2,1)} fusion(bf16[2049,2,512]{2,1,0:T(2,128)(2,1)} %fusion.99, s32[2048]{0:T(1024)S(1)} %fusion.125), kind=kCustom, calls=%fused_computation.2 | custom fusion | bytes 8396800 | tf_op jit(solution)/shard_map/gather | solution.py:205
  135.0 43.3 %all-to-all-done.2 = bf16[128,16,2,512]{3,2,1,0:T(2,128)(2,1)} async-done(((bf16[128,16,2,512]{3,2,1,0:T(2,128)(2,1)}), bf16[128,16,2,512]{3,2,1,0:T(2,128)(2,1)}, u32[]{:S(2)}, u32[]{:S(2)}) %all-to-all-start.2) | async-done | bytes 4194336 | tf_op jit(solution)/shard_map/all_to_all | solution.py:92
  196.0 34.3 %all-reduce.3 = bf16[512]{0:T(512)(128)(2,1)S(1)} all-reduce(bf16[512]{0:T(512)(128)(2,1)S(1)} %dynamic-update-slice), channel_id=1, replica_groups=mesh['dp'=16,'fsdp'=8] {'fsdp'}, use_global_device_ids=true, to_apply=%add.3 | all-reduce | flops 512 | bytes 2048
  230.4 13.1 %all_gather.11 = bf16[512,512]{1,0:T(8,128)(2,1)S(1)} all-gather(bf16[64,512]{1,0:T(8,128)(2,1)S(1)} %copy-done.18), channel_id=1, replica_groups=mesh['dp'=16,'fsdp'=8] {'fsdp'}, dimensions={0}, use_global_device_ids=true | all-gather | bytes 589824 | tf_op jit(solution)/shard_map/all_gather | solution.py:219
  317.7 146.3 %while.24 = (s32[]{:T(128)}, bf16[8,1024,4,32]{1,3,2,0:T(8,128)(2,1)S(1)}, bf16[8,1024,4,32]{1,3,2,0:T(8,128)(2,1)}, s32[8,1024]{1,0:T(8,128)S(1)}, bf16[8,1024,...) while((s32[]{:T(128)}, bf16[8,1024,4,32]{1,3,2,0:T(8,128)(2,1)S(1)}, ...), condition=%wide.region_8.9_spmd, body=%wide.region_5.8_spmd.sunk | while | flops 562169856 | bytes 34644056 | solution.py:123
  317.7 10.9 %fusion.193 = (f32[4,1024]{1,0:T(4,128)S(1)}, f32[4,1024,1024]{1,2,0:T(8,128)}) fusion(pred[1024]{0:T(1024)(128)(4,1)S(1)} %compare_reduce_fusion.4, bf16[8,1024,4,32]{1,3,2,0:T(8,128)(2,1)} %get-tuple-element.283, s32[]{:T(128)S(6)} %copy.187, bf16[8,1024,4,32]{1,3,2,0:T(8,128)(2,1)} %get-tuple-element.282), kind=kOutput, calls=%fused_computation.175.clone.1 | convolution fusion | flops 285213696 | bytes 17319936 | tf_op jit(solution)/shard_map/while/body/eval_jaxpr/sub | solution.py:64
  336.0 10.8 %fusion.193 = (f32[4,1024]{1,0:T(4,128)S(1)}, f32[4,1024,1024]{1,2,0:T(8,128)}) fusion(pred[1024]{0:T(1024)(128)(4,1)S(1)} %compare_reduce_fusion.4, bf16[8,1024,4,32]{1,3,2,0:T(8,128)(2,1)} %get-tuple-element.283, s32[]{:T(128)S(6)} %copy.187, bf16[8,1024,4,32]{1,3,2,0:T(8,128)(2,1)} %get-tuple-element.282), kind=kOutput, calls=%fused_computation.175.clone.1 | convolution fusion | flops 285213696 | bytes 17319936 | tf_op jit(solution)/shard_map/while/body/eval_jaxpr/sub | solution.py:64
  354.3 10.8 %fusion.193 = (f32[4,1024]{1,0:T(4,128)S(1)}, f32[4,1024,1024]{1,2,0:T(8,128)}) fusion(pred[1024]{0:T(1024)(128)(4,1)S(1)} %compare_reduce_fusion.4, bf16[8,1024,4,32]{1,3,2,0:T(8,128)(2,1)} %get-tuple-element.283, s32[]{:T(128)S(6)} %copy.187, bf16[8,1024,4,32]{1,3,2,0:T(8,128)(2,1)} %get-tuple-element.282), kind=kOutput, calls=%fused_computation.175.clone.1 | convolution fusion | flops 285213696 | bytes 17319936 | tf_op jit(solution)/shard_map/while/body/eval_jaxpr/sub | solution.py:64
  372.6 10.8 %fusion.193 = (f32[4,1024]{1,0:T(4,128)S(1)}, f32[4,1024,1024]{1,2,0:T(8,128)}) fusion(pred[1024]{0:T(1024)(128)(4,1)S(1)} %compare_reduce_fusion.4, bf16[8,1024,4,32]{1,3,2,0:T(8,128)(2,1)} %get-tuple-element.283, s32[]{:T(128)S(6)} %copy.187, bf16[8,1024,4,32]{1,3,2,0:T(8,128)(2,1)} %get-tuple-element.282), kind=kOutput, calls=%fused_computation.175.clone.1 | convolution fusion | flops 285213696 | bytes 17319936 | tf_op jit(solution)/shard_map/while/body/eval_jaxpr/sub | solution.py:64
  390.9 10.8 %fusion.193 = (f32[4,1024]{1,0:T(4,128)S(1)}, f32[4,1024,1024]{1,2,0:T(8,128)}) fusion(pred[1024]{0:T(1024)(128)(4,1)S(1)} %compare_reduce_fusion.4, bf16[8,1024,4,32]{1,3,2,0:T(8,128)(2,1)} %get-tuple-element.283, s32[]{:T(128)S(6)} %copy.187, bf16[8,1024,4,32]{1,3,2,0:T(8,128)(2,1)} %get-tuple-element.282), kind=kOutput, calls=%fused_computation.175.clone.1 | convolution fusion | flops 285213696 | bytes 17319936 | tf_op jit(solution)/shard_map/while/body/eval_jaxpr/sub | solution.py:64
  470.0 288.5 %while.25 = (s32[]{:T(128)}, bf16[8,1024,4,32]{1,3,2,0:T(8,128)(2,1)}, bf16[8,1024,4,32]{1,3,2,0:T(8,128)(2,1)}, bf16[8,1024,4,32]{1,3,2,0:T(8,128)(2,1)}, bf16[...) while((s32[]{:T(128)}, ...), condition=%wide.region_13.14_spmd, body=%wide.region_9.13_spmd.sunk | while | flops 1388836864 | bytes 79522944 | solution.py:136
  471.3 10.9 %fusion.206 = (f32[4,1024]{1,0:T(4,128)S(1)}, f32[4,1024,1024]{1,2,0:T(8,128)}) fusion(pred[1024]{0:T(1024)(128)(4,1)S(1)} %compare_reduce_fusion.5, bf16[8,1024,4,32]{1,3,2,0:T(8,128)(2,1)} %get-tuple-element.313, s32[]{:T(128)S(6)} %copy.195, bf16[8,1024,4,32]{1,3,2,0:T(8,128)(2,1)} %get-tuple-element.311), kind=kOutput, calls=%fused_computation.176.clone.1 | convolution fusion | flops 285213696 | bytes 17319936 | tf_op jit(solution)/shard_map/while/body/eval_jaxpr/sub | solution.py:64
  579.5 10.9 %fusion.206 = (f32[4,1024]{1,0:T(4,128)S(1)}, f32[4,1024,1024]{1,2,0:T(8,128)}) fusion(pred[1024]{0:T(1024)(128)(4,1)S(1)} %compare_reduce_fusion.5, bf16[8,1024,4,32]{1,3,2,0:T(8,128)(2,1)} %get-tuple-element.313, s32[]{:T(128)S(6)} %copy.195, bf16[8,1024,4,32]{1,3,2,0:T(8,128)(2,1)} %get-tuple-element.311), kind=kOutput, calls=%fused_computation.176.clone.1 | convolution fusion | flops 285213696 | bytes 17319936 | tf_op jit(solution)/shard_map/while/body/eval_jaxpr/sub | solution.py:64
  651.5 10.8 %fusion.206 = (f32[4,1024]{1,0:T(4,128)S(1)}, f32[4,1024,1024]{1,2,0:T(8,128)}) fusion(pred[1024]{0:T(1024)(128)(4,1)S(1)} %compare_reduce_fusion.5, bf16[8,1024,4,32]{1,3,2,0:T(8,128)(2,1)} %get-tuple-element.313, s32[]{:T(128)S(6)} %copy.195, bf16[8,1024,4,32]{1,3,2,0:T(8,128)(2,1)} %get-tuple-element.311), kind=kOutput, calls=%fused_computation.176.clone.1 | convolution fusion | flops 285213696 | bytes 17319936 | tf_op jit(solution)/shard_map/while/body/eval_jaxpr/sub | solution.py:64
  786.8 21.3 %gather_fusion.4 = bf16[2048,2,512]{2,1,0:T(2,128)(2,1)} fusion(bf16[1024,2,512]{2,1,0:T(2,128)(2,1)S(1)} %copy.162, s32[2048]{0:T(1024)S(1)} %copy-done.22), kind=kCustom, calls=%fused_computation.4 | custom fusion | bytes 8396800 | tf_op jit(solution)/shard_map/gather | solution.py:254
  820.8 17.5 %gather_fusion.1 = bf16[2048]{0:T(1024)(128)(2,1)S(1)} fusion(bf16[2048,2]{1,0:T(8,128)(2,1)S(1)} %bitcast.242, s32[2048]{0:T(1024)S(1)} %copy-done), kind=kCustom, calls=%fused_computation.1 | custom fusion | bytes 24576 | tf_op jit(solution)/shard_map/gather | solution.py:259
  838.4 34.1 %all-reduce.4 = f32[512]{0:T(512)S(1)} all-reduce(f32[512]{0:T(512)S(1)} %get-tuple-element.95), channel_id=4, replica_groups=mesh['dp'=16,'fsdp'=8] {'fsdp'}, use_global_device_ids=true, to_apply=%region_21.22.clone | all-reduce | flops 512 | bytes 4096
  872.6 40.7 %psum.23 = f32[64]{0:T(128)} all-reduce(f32[64]{0:T(128)S(1)} %dynamic-slice.8), channel_id=1, replica_groups=mesh['dp'=16,'fsdp'=8] {'dp'}, use_global_device_ids=true, to_apply=%region_22.23 | all-reduce | flops 64 | bytes 512 | tf_op jit(solution)/shard_map/psum | solution.py:253
  913.3 23.6 %gather_fusion.5 = bf16[2048,2,512]{2,1,0:T(2,128)(2,1)} fusion(bf16[2048,2,512]{2,1,0:T(2,128)(2,1)} %bitcast.51, s32[2048]{0:T(1024)S(1)} %copy-done.21), kind=kCustom, calls=%fused_computation.5 | custom fusion | bytes 8396800 | tf_op jit(solution)/shard_map/gather | solution.py:258
  958.8 69.0 %all-reduce.8.cloned.1.call-done = (f32[64,1536]{1,0:T(8,128)}, f32[64,512]{1,0:T(8,128)}) async-done(((f32[64,1536]{1,0:T(8,128)}, f32[64,512]{1,0:T(8,128)}), (f32[64,1536]{1,0:T(8,128)}, f32[64,512]{1,0:T(8,128)})) %all-reduce.8.cloned.1.call-update) | async-done | bytes 524304 | tf_op jit(solution)/shard_map/psum | solution.py:253
  (234 shorter events, 554.0 us)
Async XLA Ops:
  25.4 19.5 %copy-start.7 = (bf16[2048,512]{1,0:T(8,128)(2,1)S(1)}, bf16[2048,512]{1,0:T(8,128)(2,1)}, u32[]{:S(2)}) copy-start(bf16[2048,512]{1,0:T(8,128)(2,1)} %param.13) | copy-start | bytes 6291460
  33.2 82.3 %all-to-all-start = ((bf16[128,16,2]{1,2,0:T(2,128)(2,1)}), bf16[128,16,2]{1,2,0:T(2,128)(2,1)}, u32[]{:S(2)}, u32[]{:S(2)}) async-start(bf16[128,16,2]{1,2,0:T(2,128)(2,1)} %copy.140), calls=%async_computation | async-start | bytes 131072 | tf_op jit(solution)/shard_map/all_to_all | solution.py:93
  44.9 15.6 %copy-start.8 = (bf16[2048,512]{1,0:T(8,128)(2,1)S(1)}, bf16[2048,512]{1,0:T(8,128)(2,1)}, u32[]{:S(2)}) copy-start(bf16[2048,512]{1,0:T(8,128)(2,1)} %param.14) | copy-start | bytes 6291460
  115.5 62.9 %all-to-all-start.2 = ((bf16[128,16,2,512]{3,2,1,0:T(2,128)(2,1)}), bf16[128,16,2,512]{3,2,1,0:T(2,128)(2,1)}, u32[]{:S(2)}, u32[]{:S(2)}) async-start(bf16[128,16,2,512]{3,2,1,0:T(2,128)(2,1)} %bitcast.243), calls=%async_computation.2 | async-start | bytes 8388608 | tf_op jit(solution)/shard_map/all_to_all | solution.py:92
  125.7 155.0 %all-gather.2.cloned.1.call-start = ((), (), s32[]{:S(2)}) async-start(), calls=%async_computation.6 | async-start | bytes 1769472 | tf_op jit(solution)/shard_map/all_gather | solution.py:218
  186.4 8.1 copy-start.25
  186.4 9.4 copy-start.26
  186.4 44.0 %copy-start.18 = (bf16[64,512]{1,0:T(8,128)(2,1)S(1)}, bf16[64,512]{1,0:T(8,128)(2,1)}, u32[]{:S(2)}) copy-start(bf16[64,512]{1,0:T(8,128)(2,1)} %param.20) | copy-start | bytes 196612
  188.1 64.0 %collective-permute-start.1 = (bf16[1024,2,512]{2,0,1:T(8,128)(2,1)}, bf16[1024,2,512]{2,0,1:T(8,128)(2,1)S(1)}, u32[]{:S(2)}, u32[]{:S(2)}) collective-permute-start(bf16[1024,2,512]{2,0,1:T(8,128)(2,1)} %copy.146), channel_id=1, source_target_pairs={{1,0},{2,1},{3,2},{4,3},{5,4},{6,5},{7,6},{8,7},{9,8},{10,9},{11,1... | collective-permute-start | bytes 6291464 | tf_op jit(solution)/shard_map/ppermute | solution.py:25
  189.4 62.7 %collective-permute-start = (bf16[1024,2,512]{2,0,1:T(8,128)(2,1)}, bf16[1024,2,512]{2,0,1:T(8,128)(2,1)}, u32[]{:S(2)}, u32[]{:S(2)}) collective-permute-start(bf16[1024,2,512]{2,0,1:T(8,128)(2,1)} %copy.146), channel_id=1, source_target_pairs={{0,1},{1,2},{2,3},{3,4},{4,5},{5,6},{6,7},{7,8},{8,9},{9,10},{10,1... | collective-permute-start | bytes 6291464 | tf_op jit(solution)/shard_map/ppermute | solution.py:23
  230.3 48.0 %copy-start.23 = (f32[512]{0:T(512)}, f32[512]{0:T(512)S(1)}, u32[]{:S(2)}) copy-start(f32[512]{0:T(512)S(1)} %convert_element_type.87) | copy-start | bytes 6148
  243.5 17.1 %copy-start.16 = (bf16[512,512]{1,0:T(8,128)(2,1)}, bf16[512,512]{1,0:T(8,128)(2,1)S(1)}, u32[]{:S(2)}) copy-start(bf16[512,512]{1,0:T(8,128)(2,1)S(1)} %all_gather.11) | copy-start | bytes 1572868
  243.5 564.6 %all-to-all-start.1 = ((bf16[128,16,2]{1,2,0:T(2,128)(2,1)}), bf16[128,16,2]{1,2,0:T(2,128)(2,1)}, u32[]{:S(2)}, u32[]{:S(2)}) async-start(bf16[128,16,2]{1,2,0:T(2,128)(2,1)} %all-to-all-done), calls=%async_computation.1 | async-start | bytes 131072 | tf_op jit(solution)/shard_map/all_to_all | solution.py:93
  251.5 694.6 %reduce-scatter.5.cloned.1.call-start = ((), (), s32[]{:S(2)}) async-start(), calls=%async_computation.8 | async-start | bytes 1179648 | tf_op jit(solution)/shard_map/reduce_scatter | solution.py:250
  280.7 5.8 copy-start.9
  470.0 476.1 %reduce-scatter.3.cloned.1.call-start = ((), (), s32[]{:S(2)}) async-start(), calls=%async_computation.7 | async-start | bytes 3538944 | tf_op jit(solution)/shard_map/reduce_scatter | solution.py:249
  777.2 4.7 copy-start.14
  777.2 4.7 copy-start.15
  777.2 4.7 copy-start.17
  777.2 6.1 copy-start.3
  808.2 12.6 %copy-start = (s32[2048]{0:T(1024)S(1)}, s32[2048]{0:T(1024)}, u32[]{:S(2)}) copy-start(s32[2048]{0:T(1024)} %get-tuple-element.132) | copy-start | bytes 24580
  808.2 105.1 %all-to-all-start.3 = ((bf16[128,16,2,512]{3,2,1,0:T(2,128)(2,1)}), bf16[128,16,2,512]{3,2,1,0:T(2,128)(2,1)}, u32[]{:S(2)}, u32[]{:S(2)}) async-start(bf16[128,16,2,512]{3,2,1,0:T(2,128)(2,1)} %bitcast.244), calls=%async_computation.3 | async-start | bytes 8388608 | tf_op jit(solution)/shard_map/all_to_all | solution.py:92
  818.4 94.9 %copy-start.21 = (s32[2048]{0:T(1024)S(1)}, s32[2048]{0:T(1024)}, u32[]{:S(2)}) copy-start(s32[2048]{0:T(1024)} %get-tuple-element.149) | copy-start | bytes 24580
  818.4 209.4 %all-reduce.8.cloned.1.call-start = ((), (), s32[]{:S(2)}) async-start(), calls=%async_computation.9 | async-start | bytes 1048576 | tf_op jit(solution)/shard_map/psum | solution.py:253
  (13 other events, 29.4 us)
Sparse Core Ops, SparseCore 0:
  193.9 33.1 all-gather.1
  470.1 32.8 reduce-scatter.4
  776.7 36.7 reduce-scatter.2
  946.3 81.4 all-reduce.7
where the time goes:
time: 1050 us; the launch traced here: 1040 us
  matrix products  445 us (42%)
  local copies, waits for them, and re-layouts  235 us (22%)
  blocking collectives  122 us (12%)
  waiting for transfers between devices  112 us (11%)
  other arithmetic  59.4 us (6%)
  starting transfers between devices  45.9 us (4%)
  between operations  17.6 us (2%)
    sub x16, matrix products, probabilities(): weights = jnp.exp(scores - top)  174 us
    dot_general x8, matrix products, backward_item(): jnp.einsum('hqk,qhe->khe', probs_b, upstream, preferred_element_type=jnp....  73.3 us
    psum x1, waiting for transfers between devices, body(): totals = lax.psum((shares[0], shares[1], shares[2]), 'dp')  69 us
    unnamed x2, blocking collectives  68.4 us
    dot_general x8, matrix products, backward_item(): jnp.einsum('qhe,khe->hqk', upstream, values, preferred_element_type=jnp.f...  59.7 us
    dot_general x8, matrix products, forward_item(): jnp.einsum('hqk,khe->qhe', probs_b, values, preferred_element_type=jnp.fl...  59.3 us
    all_to_all x2, waiting for transfers between devices, regroup(): lax.all_to_all(rows_buffer, ('dp', 'fsdp'), split_axis=0, concat_axis=0,...  43.3 us
    psum x1, blocking collectives, body(): totals = lax.psum((shares[0], shares[1], shares[2]), 'dp')  40.7 us
  transfers between devices with their start and end apart: 10, of which 2 were waited for; matrix products, arithmetic and copies ran while one was open for 67% of the time, Pallas kernels for 0%

commit v1 on v0

v1 whole, which is shorter than its diff:
```python
import jax
import jax.numpy as jnp
from jax import lax
from jax.experimental import pallas as pl
from jax.experimental.pallas import tpu as pltpu
from jax.sharding import PartitionSpec as P

HEADS = 16
PATCH = 1024
EPS = 1e-05
BOTH = ("dp", "fsdp")
GAIN_COLS = 128
FAR = -1e30
LOG2E = 1.4426950408889634
F32 = jnp.float32
BF16 = jnp.bfloat16
VMEM_BYTES = 60 * 1024 * 1024


def params(steps=1):
    return pltpu.CompilerParams(
        vmem_limit_bytes=VMEM_BYTES, dimension_semantics=("arbitrary",) * steps
    )


def whole(shape):
    zeros = (0,) * len(shape)
    return pl.BlockSpec(shape, lambda *_: zeros)


SMEM = pl.BlockSpec(memory_space=pltpu.SMEM)


def ones_where(mask, dtype=BF16):
    return jnp.where(mask, 1.0, 0.0).astype(dtype)


def iota(shape, dim):
    return lax.broadcasted_iota(jnp.int32, shape, dim)


def nt(a, b):
    return lax.dot_general(a, b, (((1,), (1,)), ((), ())), preferred_element_type=F32)


def nn(a, b):
    return jnp.dot(a, b, preferred_element_type=F32)


def pick_rows(index_row, rows, first, count):
    slots = index_row.shape[1]
    chosen = ones_where(iota((count, slots), 0) + first == index_row)
    return nn(chosen, rows).astype(BF16)


def send_plan(shift, count, dest_ref, slot_ref, target_ref, marks_ref):
    devices, capacity = marks_ref.shape
    arrived = dest_ref.shape[1]
    chunk = 256
    before = ones_where(iota((chunk, chunk), 0) < iota((chunk, chunk), 1))
    base = jnp.zeros((devices, 1), F32)
    marks = jnp.zeros((devices, capacity), F32)
    for start in range(0, arrived, chunk):
        cols = pl.ds(start, chunk)
        dest = dest_ref[:, cols]
        valid = iota((1, chunk), 1) + start < count
        here = jnp.where(
            (iota((devices, chunk), 0) == dest) & valid, 1.0, 0.0
        )
        ahead = nn(here.astype(BF16), before) + base
        rank = jnp.sum(here * ahead, axis=0, keepdims=True).astype(jnp.int32)
        base = base + jnp.sum(here, axis=1, keepdims=True)
        target_ref[:, cols] = jnp.where(valid, dest * capacity + rank, -1)
        code = jnp.where(slot_ref[:, cols] < shift, 2.0, 1.0)
        at_rank = ones_where(iota((capacity, chunk), 0) == rank)
        marks = marks + nt((here * code).astype(BF16), at_rank)
    marks_ref[...] = marks.astype(BF16)


def send_first_kernel(
    shift_ref, count_ref, dest_ref, slot_ref, rows_ref, send_ref, target_ref, marks_ref
):
    step = pl.program_id(0)

    @pl.when(step == 0)
    def _():
        send_plan(shift_ref[0], count_ref[0], dest_ref, slot_ref, target_ref, marks_ref)

    block = send_ref.shape[0]
    send_ref[...] = pick_rows(target_ref[...], rows_ref[...], step * block, block)


def send_first(shift, count, dest, slot, rows, devices, block=512):
    arrived, width = rows.shape
    return pl.pallas_call(
        send_first_kernel,
        grid=(arrived // block,),
        in_specs=[
            SMEM,
            SMEM,
            whole((1, arrived)),
            whole((1, arrived)),
            whole((arrived, width)),
        ],
        out_specs=[
            pl.BlockSpec((block, width), lambda i: (i, 0)),
            whole((1, arrived)),
            whole((devices, arrived // devices)),
        ],
        out_shape=[
            jax.ShapeDtypeStruct((arrived, width), BF16),
            jax.ShapeDtypeStruct((1, arrived), jnp.int32),
            jax.ShapeDtypeStruct((devices, arrived // devices), BF16),
        ],
        compiler_params=params(),
        name="send_first",
    )(shift, count, dest, slot, rows)


def pick_kernel(index_ref, rows_ref, out_ref):
    block = out_ref.shape[0]
    out_ref[...] = pick_rows(index_ref[...], rows_ref[...], pl.program_id(0) * block, block)


def pick(index, rows, out_rows, name, block=512):
    arrived, width = rows.shape
    return pl.pallas_call(
        pick_kernel,
        grid=(out_rows // block,),
        in_specs=[whole((1, arrived)), whole((arrived, width))],
        out_specs=pl.BlockSpec((block, width), lambda i: (i, 0)),
        out_shape=jax.ShapeDtypeStruct((out_rows, width), BF16),
        compiler_params=params(),
        name=name,
    )(index, rows)


def place_kernel(shift_ref, marks_ref, place_ref):
    devices, capacity = marks_ref.shape
    slots = devices * capacity
    marks = marks_ref[...].astype(F32)
    lower = ones_where(iota((devices, devices), 1) < iota((devices, devices), 0))
    before = ones_where(iota((capacity, capacity), 0) < iota((capacity, capacity), 1))
    place = jnp.full((devices, capacity), -1.0, F32)
    for code, first in ((1.0, 0), (2.0, PATCH - shift_ref[0])):
        mine = marks == code
        flags = ones_where(mine)
        earlier = jnp.sum(nn(lower, flags), axis=1, keepdims=True) + nn(flags, before)
        place = jnp.where(mine, earlier + lax.convert_element_type(first, F32), place)
    place = place.astype(jnp.int32)
    high = lax.shift_right_arithmetic(place, 5)
    low = lax.bitwise_and(place, 31)
    spread = ones_where(
        iota((capacity, slots), 0) == lax.rem(iota((capacity, slots), 1), capacity)
    )
    own = iota((devices, slots), 0) == lax.div(iota((devices, slots), 1), capacity)

    def flat(part):
        wide = nn(part.astype(F32).astype(BF16), spread)
        return jnp.sum(jnp.where(own, wide, 0.0), axis=0, keepdims=True).astype(jnp.int32)

    place_ref[...] = flat(high) * 32 + flat(low)


def place_of(shift, marks):
    devices, capacity = marks.shape
    return pl.pallas_call(
        place_kernel,
        in_specs=[SMEM, whole((devices, capacity))],
        out_specs=whole((1, devices * capacity)),
        out_shape=jax.ShapeDtypeStruct((1, devices * capacity), jnp.int32),
        compiler_params=params(0),
        grid=(),
        name="place",
    )(shift, marks)


def column_of(row):
    length = row.shape[1]
    return jnp.transpose(jnp.broadcast_to(row, (128, length)))


def spread_rows(index_row, rows):
    wide = column_of(index_row)
    count = wide.shape[0]
    lanes = iota((count, 128), 1)
    chosen = jnp.concatenate(
        [ones_where(wide == lanes + start) for start in range(0, rows.shape[0], 128)], axis=1
    )
    return nn(chosen, rows).astype(BF16)


def spread_kernel(index_ref, rows_ref, out_ref):
    out_ref[...] = spread_rows(index_ref[...], rows_ref[...])


def spread(index, rows, name, block=512):
    slots = index.shape[1]
    source, width = rows.shape
    return pl.pallas_call(
        spread_kernel,
        grid=(slots // block,),
        in_specs=[pl.BlockSpec((1, block), lambda i: (0, i)), whole((source, width))],
        out_specs=pl.BlockSpec((block, width), lambda i: (i, 0)),
        out_shape=jax.ShapeDtypeStruct((slots, width), BF16),
        compiler_params=params(),
        name=name,
    )(index, rows)


def spread_pair_kernel(shift_ref, index_ref, own_ref, back_ref, ahead_ref, out_ref, rows):
    @pl.when(pl.program_id(0) == 0)
    def _():
        rows[...] = joined(shift_ref[0], own_ref, back_ref, ahead_ref)

    out_ref[...] = spread_rows(index_ref[...], rows[...])


def spread_pair(shift, index, own, back, ahead, name, block=512):
    slots = index.shape[1]
    half, width = back.shape
    return pl.pallas_call(
        spread_pair_kernel,
        grid=(slots // block,),
        in_specs=[
            SMEM,
            pl.BlockSpec((1, block), lambda i: (0, i)),
            whole((2 * half, width)),
            whole((half, width)),
            whole((half, width)),
        ],
        out_specs=pl.BlockSpec((block, width), lambda i: (i, 0)),
        out_shape=jax.ShapeDtypeStruct((slots, width), BF16),
        scratch_shapes=[pltpu.VMEM((2 * half, width), BF16)],
        compiler_params=params(),
        name=name,
    )(shift, index, own, back, ahead)


def joined(shift, own_ref, top_ref, bottom_ref):
    half, width = top_ref.shape
    edge = PATCH - shift
    row = iota((half, width), 0)
    top = jnp.where((2 * shift > PATCH) & (row < edge), top_ref[...], own_ref[:half, :])
    bottom = jnp.where((2 * shift <= PATCH) & (row + half >= edge), bottom_ref[...], own_ref[half:, :])
    return jnp.concatenate([top, bottom], axis=0)


def forward_kernel(
    shift_ref,
    wrap_ref,
    own_ref,
    top_ref,
    bottom_ref,
    in_t_ref,
    out_t_ref,
    gain_ref,
    probs_ref,
    block_ref,
    hidden_ref,
    normed_ref,
    inverse_ref,
    queries_ref,
    keys_ref,
    values_ref,
    attended_ref,
    x_t,
    query_x,
    key_x,
):
    head = pl.program_id(0)
    heads, head_width, length = queries_ref.shape
    width = heads * head_width
    extra = query_x.shape[1] - head_width

    @pl.when(head == 0)
    def _():
        rows = joined(shift_ref[0], own_ref, top_ref, bottom_ref)
        values_in = jnp.transpose(rows.astype(F32))
        x_t[...] = values_in
        center = values_in - jnp.mean(values_in, axis=0, keepdims=True)
        inverse = lax.rsqrt(jnp.mean(center * center, axis=0, keepdims=True) + EPS)
        normed = center * inverse
        normed_ref[...] = normed
        inverse_ref[...] = inverse
        hidden = (normed * gain_ref[:, :1].astype(F32)).astype(BF16)
        hidden_ref[...] = hidden
        for part, ref in enumerate((queries_ref, keys_ref, values_ref)):
            rows_of = in_t_ref[part * width : (part + 1) * width, :]
            ref[...] = nn(rows_of, hidden).astype(BF16).reshape(heads, head_width, length)
        side = iota((extra, length), 1) >= PATCH - shift_ref[0]
        line = iota((extra, length), 0)
        query_side = jnp.where(((line == 0) & ~side) | ((line == 1) & side), 1.0, 0.0)
        key_side = jnp.where(((line == 0) & side) | ((line == 1) & ~side), FAR, 0.0)
        key_side = jnp.where(wrap_ref[0] > 0, key_side, 0.0)
        query_x[:, :head_width, :] = queries_ref[...]
        key_x[:, :head_width, :] = keys_ref[...]
        for h in range(heads):
            query_x[h, head_width:, :] = query_side.astype(BF16)
            key_x[h, head_width:, :] = key_side.astype(BF16)

    scale = head_width ** (-0.5) * LOG2E
    key_rows = jnp.transpose(key_x[head])
    query = query_x.at[head]
    value = values_ref[head]
    chunk = 256
    for start in range(0, length, chunk):
        cols = pl.ds(start, chunk)
        scores = nn(key_rows, query[:, cols])
        top = jnp.max(scores, axis=0, keepdims=True)
        weights = jnp.exp2((scores - top) * scale)
        probs = weights * (1.0 / jnp.sum(weights, axis=0, keepdims=True))
        probs_ref[0, :, cols] = probs
        attended_ref[head, :, cols] = nn(value, probs.astype(BF16)).astype(BF16)

    @pl.when(head == heads - 1)
    def _():
        attended = attended_ref[...].reshape(width, length)
        block = x_t[...] + nn(out_t_ref[...], attended)
        block_ref[...] = jnp.transpose(block).astype(BF16)


def forward(shift, wrap, own, top, bottom, weights, weights_t):
    length, width = own.shape
    head_width = width // HEADS
    half = length // 2
    split = jax.ShapeDtypeStruct((HEADS, head_width, length), BF16)
    return pl.pallas_call(
        forward_kernel,
        grid=(HEADS,),
        in_specs=[
            SMEM,
            SMEM,
            whole((length, width)),
            whole((half, width)),
            whole((half, width)),
            pl.BlockSpec((3 * width, width), lambda h: (0, 0)),
            pl.BlockSpec((width, width), lambda h: (3, 0)),
            pl.BlockSpec((width, GAIN_COLS), lambda h: (0, 4 * width // GAIN_COLS)),
        ],
        out_specs=[
            pl.BlockSpec((1, length, length), lambda h: (h, 0, 0)),
            whole((length, width)),
            whole((width, length)),
            whole((width, length)),
            whole((1, length)),
            whole((HEADS, head_width, length)),
            whole((HEADS, head_width, length)),
            whole((HEADS, head_width, length)),
            whole((HEADS, head_width, length)),
        ],
        out_shape=[
            jax.ShapeDtypeStruct((HEADS, length, length), F32),
            jax.ShapeDtypeStruct((length, width), BF16),
            jax.ShapeDtypeStruct((width, length), BF16),
            jax.ShapeDtypeStruct((width, length), F32),
            jax.ShapeDtypeStruct((1, length), F32),
            split,
            split,
            split,
            split,
        ],
        scratch_shapes=[
            pltpu.VMEM((width, length), F32),
            pltpu.VMEM((HEADS, head_width + 16, length), BF16),
            pltpu.VMEM((HEADS, head_width + 16, length), BF16),
        ],
        compiler_params=params(),
        name="forward",
    )(shift, wrap, own, top, bottom, weights_t, weights_t, weights)


def backward_kernel(
    shift_ref,
    own_ref,
    top_ref,
    bottom_ref,
    in_ref,
    out_ref,
    gain_ref,
    probs_ref,
    hidden_ref,
    normed_ref,
    inverse_ref,
    queries_ref,
    keys_ref,
    values_ref,
    attended_ref,
    grad_ref,
    parts_ref,
    cot,
    grad_att,
    grad_rows,
):
    head = pl.program_id(0)
    heads, head_width, length = queries_ref.shape
    width = heads * head_width

    @pl.when(head == 0)
    def _():
        rows = joined(shift_ref[0], own_ref, top_ref, bottom_ref)
        cot[...] = rows
        grad_att[...] = nt(out_ref[...], rows).astype(BF16).reshape(heads, head_width, length)

    scale = head_width ** (-0.5)
    query, key, value = queries_ref[head], keys_ref[head], values_ref[head]
    value_rows = jnp.transpose(value)
    upstream = grad_att[head]
    offset = jnp.sum(upstream.astype(F32) * attended_ref[head].astype(F32), axis=0, keepdims=True)
    chunk = 256
    key_grad = jnp.zeros((head_width, length), F32)
    value_grad = jnp.zeros((head_width, length), F32)
    for start in range(0, length, chunk):
        cols = pl.ds(start, chunk)
        probs = probs_ref[0, :, cols]
        along = nn(value_rows, upstream[:, start : start + chunk])
        slopes = (probs * (along - offset[:, start : start + chunk]) * scale).astype(BF16)
        grad_rows[0, head, :, cols] = nn(key, slopes).astype(BF16)
        key_grad = key_grad + nt(query[:, start : start + chunk], slopes)
        value_grad = value_grad + nt(upstream[:, start : start + chunk], probs.astype(BF16))
    grad_rows[1, head] = key_grad.astype(BF16)
    grad_rows[2, head] = value_grad.astype(BF16)

    @pl.when(head == heads - 1)
    def _():
        grads = grad_rows[...].reshape(3 * width, length)
        normed = normed_ref[...]
        grad_hidden = nn(in_ref[...], grads)
        parts_ref[:, : 3 * width] = nt(hidden_ref[...], grads)
        parts_ref[:, 3 * width : 4 * width] = nn(
            attended_ref[...].reshape(width, length), cot[...]
        )
        part_gain = jnp.sum(grad_hidden * normed, axis=1, keepdims=True)
        parts_ref[:, 4 * width :] = jnp.broadcast_to(part_gain, (width, GAIN_COLS))
        scaled = grad_hidden * gain_ref[:, :1].astype(F32)
        middle = jnp.mean(scaled, axis=0, keepdims=True)
        slope = jnp.mean(scaled * normed, axis=0, keepdims=True)
        change = inverse_ref[...] * (scaled - middle - normed * slope)
        grad_ref[...] = (cot[...].astype(F32) + jnp.transpose(change)).astype(BF16)


def backward(shift, own, top, bottom, weights, saved):
    length, width = own.shape
    head_width = width // HEADS
    half = length // 2
    split = (HEADS, head_width, length)
    return pl.pallas_call(
        backward_kernel,
        grid=(HEADS,),
        in_specs=[
            SMEM,
            whole((length, width)),
            whole((half, width)),
            whole((half, width)),
            pl.BlockSpec((width, 3 * width), lambda h: (0, 0)),
            pl.BlockSpec((width, width), lambda h: (0, 3)),
            pl.BlockSpec((width, GAIN_COLS), lambda h: (0, 4 * width // GAIN_COLS)),
            pl.BlockSpec((1, length, length), lambda h: (h, 0, 0)),
            whole((width, length)),
            whole((width, length)),
            whole((1, length)),
            whole(split),
            whole(split),
            whole(split),
            whole(split),
        ],
        out_specs=[whole((length, width)), whole((width, 4 * width + GAIN_COLS))],
        out_shape=[
            jax.ShapeDtypeStruct((length, width), BF16),
            jax.ShapeDtypeStruct((width, 4 * width + GAIN_COLS), F32),
        ],
        scratch_shapes=[
            pltpu.VMEM((length, width), BF16),
            pltpu.VMEM(split, BF16),
            pltpu.VMEM((3,) + split, BF16),
        ],
        compiler_params=params(),
        name="backward",
    )(shift, own, top, bottom, weights, weights, weights, *saved)


def exchange(rows, devices):
    moved = lax.all_to_all(
        rows.reshape(devices, rows.shape[0] // devices, rows.shape[1]),
        BOTH,
        split_axis=0,
        concat_axis=0,
        tiled=True,
    )
    return moved.reshape(rows.shape)


def neighbours(rows, devices):
    half = rows.shape[0] // 2
    onward = [(i, (i + 1) % devices) for i in range(devices)]
    back = [((i + 1) % devices, i) for i in range(devices)]
    return lax.ppermute(rows[:half], BOTH, onward), lax.ppermute(rows[half:], BOTH, back)


def neighbours_back(rows, devices):
    half = rows.shape[0] // 2
    onward = [(i, (i + 1) % devices) for i in range(devices)]
    back = [((i + 1) % devices, i) for i in range(devices)]
    return lax.ppermute(rows[:half], BOTH, back), lax.ppermute(rows[half:], BOTH, onward)


def body(
    points,
    cotangent,
    destination,
    curve_slot,
    point_counts,
    shift_offset,
    project_in,
    project_out,
    norm_gain,
):
    devices = lax.axis_size(BOTH)
    groups = lax.axis_size("dp")
    arrived, width = points.shape
    share = project_in.shape[0]
    packed = jnp.concatenate(
        [project_in, project_out, jnp.broadcast_to(norm_gain[:, None], (share, GAIN_COLS))], axis=1
    )
    weights = lax.all_gather(packed, "fsdp", axis=0, tiled=True)
    weights_t = jnp.transpose(weights)
    device = lax.axis_index(BOTH)
    edge_device = jnp.where(2 * shift_offset <= PATCH, devices - 1, 0)
    wrap = (device == edge_device).astype(jnp.int32)

    send_points, target, marks = send_first(
        shift_offset,
        point_counts,
        destination.reshape(1, arrived),
        curve_slot.reshape(1, arrived),
        points,
        devices,
    )
    got_marks = lax.all_to_all(marks, BOTH, split_axis=0, concat_axis=0, tiled=True)
    got_points = exchange(send_points, devices)
    place = place_of(shift_offset, got_marks)
    send_cot = pick(target, cotangent, arrived, "send_cot")
    got_cot = exchange(send_cot, devices)

    own_points = pick(place, got_points, PATCH, "curve_points")
    points_top, points_bottom = neighbours(own_points, devices)
    own_cot = pick(place, got_cot, PATCH, "curve_cot")
    cot_top, cot_bottom = neighbours(own_cot, devices)

    probs, block, *saved = forward(
        shift_offset, wrap, own_points, points_top, points_bottom, weights, weights_t
    )
    block_top, block_bottom = neighbours_back(block, devices)
    back_block = exchange(
        spread_pair(shift_offset, place, block, block_top, block_bottom, "back_block"), devices
    )

    grad, parts = backward(
        shift_offset, own_cot, cot_top, cot_bottom, weights, (probs, *saved)
    )
    grad_top, grad_bottom = neighbours_back(grad, devices)
    back_grad = exchange(
        spread_pair(shift_offset, place, grad, grad_top, grad_bottom, "back_grad"), devices
    )

    shares = lax.psum_scatter(parts, "fsdp", scatter_dimension=0, tiled=True)
    terms = lax.all_to_all(
        shares.reshape(groups, share // groups, shares.shape[1]),
        "dp",
        split_axis=0,
        concat_axis=0,
        tiled=True,
    )
    total = jnp.sum(terms, axis=0)
    totals = lax.all_to_all(
        jnp.broadcast_to(total[None], terms.shape), "dp", split_axis=0, concat_axis=0, tiled=True
    ).reshape(shares.shape)

    block_out = spread(target, back_block, "block_out")
    point_grad = spread(target, back_grad, "point_grad")
    return (
        block_out,
        point_grad,
        totals[:, : 3 * width],
        totals[:, 3 * width : 4 * width],
        totals[:, 4 * width],
    )


def solution(mesh):
    in_specs = (
        P(BOTH, None),
        P(BOTH, None),
        P(BOTH),
        P(BOTH),
        P(BOTH),
        P(),
        P("fsdp", None),
        P("fsdp", None),
        P("fsdp"),
    )
    out_specs = (
        P(BOTH, None),
        P(BOTH, None),
        P("fsdp", None),
        P("fsdp", None),
        P("fsdp"),
    )
    return jax.shard_map(body, mesh=mesh, in_specs=in_specs, out_specs=out_specs, check_vma=False)
```

time: 1050 us -> 405 us (0.39)
  matrix products: 445 us -> 0 us
  local copies, waits for them, and re-layouts: 235 us -> 22.9 us
  Pallas kernels: 0 us -> 178 us
  blocking collectives: 122 us -> 20.3 us
  other arithmetic: 59.4 us -> 0.82 us
  starting transfers between devices: 45.9 us -> 62.5 us
    dot_general x46 -> x0, matrix products: 272 us -> none  [the longest x8 73.3 us: backward_item(): jnp.einsum('hqk,qhe->khe', probs_b, upstream, preferred_element_type=jnp....]
    pallas_call x0 -> x11, Pallas kernels: none -> 178 us  [the longest x1 67.1 us: forward(): pl.pallas_call(forward_kernel, grid=(HEADS,), in_specs=[SMEM, SMEM, whole...]
    sub x16 -> x0, matrix products: 174 us -> none  [probabilities(): weights = jnp.exp(scores - top)]
    gather x7 -> x0, local copies, waits for them, and re-layouts: 102 us -> none  [the longest x1 23.6 us: body(): send_rows = padded_rows[source_row]]
    psum x1 -> x0, waiting for transfers between devices: 69 us -> none  [body(): totals = lax.psum((shares[0], shares[1], shares[2]), 'dp')]
    unnamed x2 -> x0, blocking collectives: 68.4 us -> none
    psum x1 -> x0, blocking collectives: 40.7 us -> none  [body(): totals = lax.psum((shares[0], shares[1], shares[2]), 'dp')]
    another operation x7 -> x0, local copies, waits for them, and re-layouts: 33.9 us -> none  [the longest x2 31.2 us: body(): paired = jnp.stack([points, cotangent], axis=1)]
  transfers between devices with their start and end apart: 10 -> 16, of which waited for: 2 -> 6; matrix products, arithmetic and copies ran while one was open for 67% -> 3% of each run, Pallas kernels for 0% -> 28%
where the time goes in v1:
time: 405 us; the launch traced here: 403 us
  Pallas kernels  178 us (44%)
  waiting for transfers between devices  104 us (26%)
  starting transfers between devices  62.5 us (15%)
  local copies, waits for them, and re-layouts  22.9 us (6%)
  blocking collectives  20.3 us (5%)
  between operations  15.5 us (4%)
    pallas_call x1, Pallas kernels, forward(): pl.pallas_call(forward_kernel, grid=(HEADS,), in_specs=[SMEM, SMEM, whole...  67.1 us
    all_to_all x4, waiting for transfers between devices, exchange(): lax.all_to_all(rows.reshape(devices, rows.shape[0] // devices, rows.shape...  66.2 us
    pallas_call x1, Pallas kernels, backward(): pl.pallas_call(backward_kernel, grid=(HEADS,), in_specs=[SMEM, whole((len...  56.4 us
    all_to_all x4, starting transfers between devices, exchange(): lax.all_to_all(rows.reshape(devices, rows.shape[0] // devices, rows.shape...  27.5 us
    reduce_scatter x1, waiting for transfers between devices, body(): shares = lax.psum_scatter(parts, 'fsdp', scatter_dimension=0, tiled=True)  26.7 us
    all_to_all x1, blocking collectives, body(): lax.all_to_all(marks, BOTH, split_axis=0, concat_axis=0, tiled=True)  20.3 us
    pallas_call x3, Pallas kernels, pick(): pl.pallas_call(pick_kernel, grid=(out_rows // block,), in_specs=[whole((1...  17.3 us
    pallas_call x2, Pallas kernels, spread(): pl.pallas_call(spread_kernel, grid=(slots // block,), in_specs=[pl.BlockS...  15.2 us
  transfers between devices with their start and end apart: 16, of which 6 were waited for; matrix products, arithmetic and copies ran while one was open for 3% of the time, Pallas kernels for 28%

profile of v1, /device:TPU:0, one launch (start us, length us, event | category | flops | bytes accessed | tf_op | source)
XLA Modules:
  0.0 403.2 jit_solution(4435756755398738112)
XLA Ops:
  8.5 8.3 %send_first.1 = (bf16[2048,512]{1,0:T(8,128)(2,1)}, s32[1,2048]{1,0:T(1,128)}, bf16[128,16]{1,0:T(8,128)(2,1)}) custom-call(s32[1]{0:T(128)S(6)} %copy.30.shift_ref, s32[1]{0:T(128)S(6)} %copy.29.count_ref, s32[1,2048]{1,0:T(1,128)} %bitcast.27, s32[1,2048]{1,0:T(1,128)} %bitcast.28, bf16[2048,512]{1,0:T(8,128)(2,1)} %rows_ref.2), custom_call_target="tpu_custom_call" | custom-call | tf_op jit(solution)/shard_map/send_first/pallas_call | solution.py:95
  17.6 20.3 %all_to_all.41 = bf16[128,1,16]{2,1,0:T(2,128)(2,1)S(1)} all-to-all(bf16[128,1,16]{2,1,0:T(2,128)(2,1)S(1)} %copy.21), channel_id=1, replica_groups=mesh['dp'=16,'fsdp'=8] {'dp','fsdp'}, dimensions={0} | all-to-all | bytes 8192 | tf_op jit(solution)/shard_map/all_to_all | solution.py:539
  37.9 4.8 %all-to-all-start.1 = ((bf16[128,16,512]{2,1,0:T(8,128)(2,1)}), bf16[128,16,512]{2,1,0:T(8,128)(2,1)S(1)}, u32[]{:S(2)}, u32[]{:S(2)}) async-start(bf16[128,16,512]{2,1,0:T(8,128)(2,1)} %bitcast.24), calls=%async_computation.1 | async-start | bytes 4194304 | tf_op jit(solution)/shard_map/all_to_all | solution.py:483
  43.6 7.5 %send_cot.1 = bf16[2048,512]{1,0:T(8,128)(2,1)} custom-call(s32[1,2048]{1,0:T(1,128)} %get-tuple-element.19.index_ref, bf16[2048,512]{1,0:T(8,128)(2,1)} %rows_ref.3), custom_call_target="tpu_custom_call" | custom-call | tf_op jit(solution)/shard_map/send_cot/pallas_call | solution.py:127
  51.0 22.1 %all-to-all-done.1 = bf16[128,16,512]{2,1,0:T(8,128)(2,1)S(1)} async-done(((bf16[128,16,512]{2,1,0:T(8,128)(2,1)}), bf16[128,16,512]{2,1,0:T(8,128)(2,1)S(1)}, u32[]{:S(2)}, u32[]{:S(2)}) %all-to-all-start.1) | async-done | bytes 2097184 | tf_op jit(solution)/shard_map/all_to_all | solution.py:483
  74.5 6.9 %all-to-all-start.3 = ((bf16[128,16,512]{2,1,0:T(8,128)(2,1)}), bf16[128,16,512]{2,1,0:T(8,128)(2,1)}, u32[]{:S(2)}, u32[]{:S(2)}) async-start(bf16[128,16,512]{2,1,0:T(8,128)(2,1)} %bitcast.20), calls=%async_computation.3 | async-start | bytes 4194304 | tf_op jit(solution)/shard_map/all_to_all | solution.py:483
  84.1 4.9 %curve_points.1.own_ref = bf16[1024,512]{1,0:T(8,128)(2,1)} custom-call(s32[1,2048]{1,0:T(1,128)} %place.1.index_ref, bf16[2048,512]{1,0:T(8,128)(2,1)} %bitcast.19), custom_call_target="tpu_custom_call" | custom-call | tf_op jit(solution)/shard_map/curve_points/pallas_call | solution.py:127
  91.2 7.0 %collective-permute-start.1 = (bf16[512,512]{1,0:T(8,128)(2,1)}, bf16[512,512]{1,0:T(8,128)(2,1)S(1)}, u32[]{:S(2)}, u32[]{:S(2)}) collective-permute-start(bf16[512,512]{1,0:T(8,128)(2,1)} %get-tuple-element.39), channel_id=1, source_target_pairs={{1,0},{2,1},{3,2},{4,3},{5,4},{6,5},{7,6},{8,7},{9,8},{10,9},{11,1... | collective-permute-start | bytes 1572872 | tf_op jit(solution)/shard_map/ppermute | solution.py:497
  98.2 13.8 %all-to-all-done.3 = bf16[128,16,512]{2,1,0:T(8,128)(2,1)} async-done(((bf16[128,16,512]{2,1,0:T(8,128)(2,1)}), bf16[128,16,512]{2,1,0:T(8,128)(2,1)}, u32[]{:S(2)}, u32[]{:S(2)}) %all-to-all-start.3) | async-done | bytes 2097184 | tf_op jit(solution)/shard_map/all_to_all | solution.py:483
  112.0 5.0 %curve_cot.1.own_ref = bf16[1024,512]{1,0:T(8,128)(2,1)} custom-call(s32[1,2048]{1,0:T(1,128)} %place.1.index_ref, bf16[2048,512]{1,0:T(8,128)(2,1)} %bitcast.12.rows_ref), custom_call_target="tpu_custom_call" | custom-call | tf_op jit(solution)/shard_map/curve_cot/pallas_call | solution.py:127
  124.9 67.1 %forward.1 = (f32[16,1024,1024]{2,1,0:T(8,128)}, bf16[1024,512]{1,0:T(8,128)(2,1)}, bf16[512,1024]{1,0:T(8,128)(2,1)}, f32[512,1024]{1,0:T(8,128)}, f32[1,1024]{...) custom-call(s32[1]{0:T(128)S(6)} %copy.30.shift_ref, ...), custom_call_target="tpu_custom_call" | custom-call | tf_op jit(solution)/shard_map/forward/pallas_call | solution.py:328
  193.0 56.4 %backward.1 = (bf16[1024,512]{1,0:T(8,128)(2,1)}, f32[512,2176]{1,0:T(8,128)}) custom-call(s32[1]{0:T(128)S(6)} %copy.30.shift_ref, bf16[1024,512]{1,0:T(8,128)(2,1)} %curve_cot.1.own_ref, bf16[512,512]{1,0:T(8,128)(2,1)} %copy-done.6, bf16[512,512]{1,0:T(8,128)(2,1)} %copy-done.5, bf16[512,2176]{1,0:T(8,128)(2,1)} %all-gather.2.cloned.1.call-done.gain_ref.in_ref.out_ref, ...), custom_call_target="tpu_custom_call" | custom-call | tf_op jit(solution)/shard_map/backward/pallas_call | solution.py:447
  251.0 6.9 %collective-permute-start.6 = (bf16[512,512]{1,0:T(8,128)(2,1)S(1)}, bf16[512,512]{1,0:T(8,128)(2,1)S(1)}, u32[]{:S(2)}, u32[]{:S(2)}) collective-permute-start(bf16[512,512]{1,0:T(8,128)(2,1)S(1)} %get-tuple-element.34), channel_id=1, source_target_pairs={{1,0},{2,1},{3,2},{4,3},{5,4},{6,5},{7,6},{8,7},{9,8},{10,9},{11,1... | collective-permute-start | bytes 1572872 | tf_op jit(solution)/shard_map/ppermute | solution.py:504
  258.0 6.8 %collective-permute-done.7.ahead_ref = bf16[512,512]{1,0:T(8,128)(2,1)S(1)} collective-permute-done((bf16[512,512]{1,0:T(8,128)(2,1)S(1)}, bf16[512,512]{1,0:T(8,128)(2,1)S(1)}, u32[]{:S(2)}, u32[]{:S(2)}) %collective-permute-start.7) | collective-permute-done | bytes 524320 | tf_op jit(solution)/shard_map/ppermute | solution.py:504
  266.4 5.7 %back_grad.1 = bf16[2048,512]{1,0:T(8,128)(2,1)} custom-call(s32[1]{0:T(128)S(6)} %copy.30.shift_ref, s32[1,2048]{1,0:T(1,128)} %place.1.index_ref, bf16[1024,512]{1,0:T(8,128)(2,1)} %get-tuple-element.31.own_ref, bf16[512,512]{1,0:T(8,128)(2,1)} %copy-done.11, bf16[512,512]{1,0:T(8,128)(2,1)} %copy-done.10), custom_call_target="tpu_custom_call" | custom-call | tf_op jit(solution)/shard_map/back_grad/pallas_call | solution.py:222
  272.0 10.6 %all-to-all-start.4 = ((bf16[128,16,512]{2,1,0:T(8,128)(2,1)}), bf16[128,16,512]{2,1,0:T(8,128)(2,1)S(1)}, u32[]{:S(2)}, u32[]{:S(2)}) async-start(bf16[128,16,512]{2,1,0:T(8,128)(2,1)} %bitcast.21), calls=%async_computation.4 | async-start | bytes 4194304 | tf_op jit(solution)/shard_map/all_to_all | solution.py:483
  283.7 7.2 %collective-permute-start.2 = (bf16[512,512]{1,0:T(8,128)(2,1)}, bf16[512,512]{1,0:T(8,128)(2,1)}, u32[]{:S(2)}, u32[]{:S(2)}) collective-permute-start(bf16[512,512]{1,0:T(8,128)(2,1)} %get-tuple-element.38), channel_id=1, source_target_pairs={{1,0},{2,1},{3,2},{4,3},{5,4},{6,5},{7,6},{8,7},{9,8},{10,9},{11,1... | collective-permute-start | bytes 1572872 | tf_op jit(solution)/shard_map/ppermute | solution.py:504
  290.9 26.7 %reduce-scatter.2.cloned.1.call-done = f32[64,2176]{1,0:T(8,128)} async-done(((f32[512,2176]{1,0:T(8,128)}), f32[64,2176]{1,0:T(8,128)}) %reduce-scatter.2.cloned.1.call-update) | async-done | bytes 557072 | tf_op jit(solution)/shard_map/reduce_scatter | solution.py:566
  319.6 8.8 %all-to-all-start.5 = ((f32[16,4,2176]{2,1,0:T(4,128)}), f32[16,4,2176]{2,1,0:T(4,128)S(1)}, u32[]{:S(2)}, u32[]{:S(2)}) async-start(f32[16,4,2176]{2,1,0:T(4,128)} %reshape.60), calls=%async_computation.6 | async-start | bytes 1114112 | tf_op jit(solution)/shard_map/all_to_all | solution.py:567
  329.3 5.6 %back_block.1 = bf16[2048,512]{1,0:T(8,128)(2,1)} custom-call(s32[1]{0:T(128)S(6)} %copy.30.shift_ref, s32[1,2048]{1,0:T(1,128)} %place.1.index_ref, bf16[1024,512]{1,0:T(8,128)(2,1)} %get-tuple-element.22.own_ref, bf16[512,512]{1,0:T(8,128)(2,1)} %collective-permute-done.2.back_ref, bf16[512,512]{1,0:T(8,128)(2,1)} %copy-done.9), custom_call_target="tpu_custom_call" | custom-call | tf_op jit(solution)/shard_map/back_block/pallas_call | solution.py:222
  338.8 5.1 %all-to-all-start.2 = ((bf16[128,16,512]{2,1,0:T(8,128)(2,1)}), bf16[128,16,512]{2,1,0:T(8,128)(2,1)S(1)}, u32[]{:S(2)}, u32[]{:S(2)}) async-start(bf16[128,16,512]{2,1,0:T(8,128)(2,1)} %bitcast.23), calls=%async_computation.2 | async-start | bytes 4194304 | tf_op jit(solution)/shard_map/all_to_all | solution.py:483
  344.0 30.3 %all-to-all-done.2 = bf16[128,16,512]{2,1,0:T(8,128)(2,1)S(1)} async-done(((bf16[128,16,512]{2,1,0:T(8,128)(2,1)}), bf16[128,16,512]{2,1,0:T(8,128)(2,1)S(1)}, u32[]{:S(2)}, u32[]{:S(2)}) %all-to-all-start.2) | async-done | bytes 2097184 | tf_op jit(solution)/shard_map/all_to_all | solution.py:483
  378.9 7.6 %point_grad.1 = bf16[2048,512]{1,0:T(8,128)(2,1)} custom-call(s32[1,2048]{1,0:T(1,128)} %get-tuple-element.19.index_ref, bf16[2048,512]{1,0:T(8,128)(2,1)} %bitcast.18), custom_call_target="tpu_custom_call" | custom-call | tf_op jit(solution)/shard_map/point_grad/pallas_call | solution.py:200
  386.5 7.6 %block_out.1 = bf16[2048,512]{1,0:T(8,128)(2,1)} custom-call(s32[1,2048]{1,0:T(1,128)} %get-tuple-element.19.index_ref, bf16[2048,512]{1,0:T(8,128)(2,1)} %bitcast.22), custom_call_target="tpu_custom_call" | custom-call | tf_op jit(solution)/shard_map/block_out/pallas_call | solution.py:200
  (68 shorter events, 34.7 us)
Async XLA Ops:
  37.9 4.9 %copy-start.14 = (bf16[64]{0:T(256)(128)(2,1)S(1)}, bf16[64]{0:T(256)(128)(2,1)}, u32[]{:S(2)}) copy-start(bf16[64]{0:T(256)(128)(2,1)} %param.17) | copy-start | bytes 388
  37.9 5.0 %copy-start.12 = (bf16[64,1536]{1,0:T(8,128)(2,1)S(1)}, bf16[64,1536]{1,0:T(8,128)(2,1)}, u32[]{:S(2)}) copy-start(bf16[64,1536]{1,0:T(8,128)(2,1)} %param.15) | copy-start | bytes 589828
  37.9 5.0 %copy-start.13 = (bf16[64,512]{1,0:T(8,128)(2,1)S(1)}, bf16[64,512]{1,0:T(8,128)(2,1)}, u32[]{:S(2)}) copy-start(bf16[64,512]{1,0:T(8,128)(2,1)} %param.16) | copy-start | bytes 196612
  37.9 35.3 %all-to-all-start.1 = ((bf16[128,16,512]{2,1,0:T(8,128)(2,1)}), bf16[128,16,512]{2,1,0:T(8,128)(2,1)S(1)}, u32[]{:S(2)}, u32[]{:S(2)}) async-start(bf16[128,16,512]{2,1,0:T(8,128)(2,1)} %bitcast.24), calls=%async_computation.1 | async-start | bytes 4194304 | tf_op jit(solution)/shard_map/all_to_all | solution.py:483
  42.7 76.5 %all-gather.2.cloned.1.call-start = ((), (), s32[]{:S(2)}) async-start(), calls=%async_computation.8 | async-start | bytes 2506752 | tf_op jit(solution)/shard_map/all_gather | solution.py:525
  73.2 1.3 copy-start.1
  74.5 37.5 %all-to-all-start.3 = ((bf16[128,16,512]{2,1,0:T(8,128)(2,1)}), bf16[128,16,512]{2,1,0:T(8,128)(2,1)}, u32[]{:S(2)}, u32[]{:S(2)}) async-start(bf16[128,16,512]{2,1,0:T(8,128)(2,1)} %bitcast.20), calls=%async_computation.3 | async-start | bytes 4194304 | tf_op jit(solution)/shard_map/all_to_all | solution.py:483
  81.4 236.2 %reduce-scatter.2.cloned.1.call-start = ((), (), s32[]{:S(2)}) async-start(), calls=%async_computation.9 | async-start | bytes 5013504 | tf_op jit(solution)/shard_map/reduce_scatter | solution.py:566
  91.2 32.1 %collective-permute-start.1 = (bf16[512,512]{1,0:T(8,128)(2,1)}, bf16[512,512]{1,0:T(8,128)(2,1)S(1)}, u32[]{:S(2)}, u32[]{:S(2)}) collective-permute-start(bf16[512,512]{1,0:T(8,128)(2,1)} %get-tuple-element.39), channel_id=1, source_target_pairs={{1,0},{2,1},{3,2},{4,3},{5,4},{6,5},{7,6},{8,7},{9,8},{10,9},{11,1... | collective-permute-start | bytes 1572872 | tf_op jit(solution)/shard_map/ppermute | solution.py:497
  98.2 25.1 %collective-permute-start = (bf16[512,512]{1,0:T(8,128)(2,1)}, bf16[512,512]{1,0:T(8,128)(2,1)S(1)}, u32[]{:S(2)}, u32[]{:S(2)}) collective-permute-start(bf16[512,512]{1,0:T(8,128)(2,1)} %get-tuple-element.40), channel_id=1, source_target_pairs={{0,1},{1,2},{2,3},{3,4},{4,5},{5,6},{6,7},{7,8},{8,9},{9,10},{10,1... | collective-permute-start | bytes 1572872 | tf_op jit(solution)/shard_map/ppermute | solution.py:497
  118.2 73.8 %collective-permute-start.5 = (bf16[512,512]{1,0:T(8,128)(2,1)S(1)}, bf16[512,512]{1,0:T(8,128)(2,1)S(1)}, u32[]{:S(2)}, u32[]{:S(2)}) collective-permute-start(bf16[512,512]{1,0:T(8,128)(2,1)S(1)} %get-tuple-element.35), channel_id=1, source_target_pairs={{1,0},{2,1},{3,2},{4,3},{5,4},{6,5},{7,6},{8,7},{9,8},{10,9},{11,1... | collective-permute-start | bytes 1572872 | tf_op jit(solution)/shard_map/ppermute | solution.py:497
  119.2 72.8 %collective-permute-start.4 = (bf16[512,512]{1,0:T(8,128)(2,1)S(1)}, bf16[512,512]{1,0:T(8,128)(2,1)S(1)}, u32[]{:S(2)}, u32[]{:S(2)}) collective-permute-start(bf16[512,512]{1,0:T(8,128)(2,1)S(1)} %get-tuple-element.36), channel_id=1, source_target_pairs={{0,1},{1,2},{2,3},{3,4},{4,5},{5,6},{6,7},{7,8},{8,9},{9,10},{10,1... | collective-permute-start | bytes 1572872 | tf_op jit(solution)/shard_map/ppermute | solution.py:497
  249.4 1.2 copy-start.4
  250.7 14.1 %collective-permute-start.7 = (bf16[512,512]{1,0:T(8,128)(2,1)S(1)}, bf16[512,512]{1,0:T(8,128)(2,1)S(1)}, u32[]{:S(2)}, u32[]{:S(2)}) collective-permute-start(bf16[512,512]{1,0:T(8,128)(2,1)S(1)} %get-tuple-element.33), channel_id=1, source_target_pairs={{0,1},{1,2},{2,3},{3,4},{4,5},{5,6},{6,7},{7,8},{8,9},{9,10},{10,1... | collective-permute-start | bytes 1572872 | tf_op jit(solution)/shard_map/ppermute | solution.py:504
  251.0 13.7 %collective-permute-start.6 = (bf16[512,512]{1,0:T(8,128)(2,1)S(1)}, bf16[512,512]{1,0:T(8,128)(2,1)S(1)}, u32[]{:S(2)}, u32[]{:S(2)}) collective-permute-start(bf16[512,512]{1,0:T(8,128)(2,1)S(1)} %get-tuple-element.34), channel_id=1, source_target_pairs={{1,0},{2,1},{3,2},{4,3},{5,4},{6,5},{7,6},{8,7},{9,8},{10,9},{11,1... | collective-permute-start | bytes 1572872 | tf_op jit(solution)/shard_map/ppermute | solution.py:504
  272.0 10.6 %copy-start.3 = (bf16[1024,512]{1,0:T(8,128)(2,1)S(1)}, bf16[1024,512]{1,0:T(8,128)(2,1)}, u32[]{:S(2)}) copy-start(bf16[1024,512]{1,0:T(8,128)(2,1)} %get-tuple-element.22.own_ref) | copy-start | bytes 3145732
  272.0 47.6 %all-to-all-start.4 = ((bf16[128,16,512]{2,1,0:T(8,128)(2,1)}), bf16[128,16,512]{2,1,0:T(8,128)(2,1)S(1)}, u32[]{:S(2)}, u32[]{:S(2)}) async-start(bf16[128,16,512]{2,1,0:T(8,128)(2,1)} %bitcast.21), calls=%async_computation.4 | async-start | bytes 4194304 | tf_op jit(solution)/shard_map/all_to_all | solution.py:483
  283.7 44.8 %collective-permute-start.3 = (bf16[512,512]{1,0:T(8,128)(2,1)}, bf16[512,512]{1,0:T(8,128)(2,1)S(1)}, u32[]{:S(2)}, u32[]{:S(2)}) collective-permute-start(bf16[512,512]{1,0:T(8,128)(2,1)} %get-tuple-element.37), channel_id=1, source_target_pairs={{0,1},{1,2},{2,3},{3,4},{4,5},{5,6},{6,7},{7,8},{8,9},{9,10},{10,1... | collective-permute-start | bytes 1572872 | tf_op jit(solution)/shard_map/ppermute | solution.py:504
  283.7 44.8 %collective-permute-start.2 = (bf16[512,512]{1,0:T(8,128)(2,1)}, bf16[512,512]{1,0:T(8,128)(2,1)}, u32[]{:S(2)}, u32[]{:S(2)}) collective-permute-start(bf16[512,512]{1,0:T(8,128)(2,1)} %get-tuple-element.38), channel_id=1, source_target_pairs={{1,0},{2,1},{3,2},{4,3},{5,4},{6,5},{7,6},{8,7},{9,8},{10,9},{11,1... | collective-permute-start | bytes 1572872 | tf_op jit(solution)/shard_map/ppermute | solution.py:504
  319.6 15.3 %copy-start = (bf16[128,16,512]{2,1,0:T(8,128)(2,1)}, bf16[128,16,512]{2,1,0:T(8,128)(2,1)S(1)}, u32[]{:S(2)}) copy-start(bf16[128,16,512]{2,1,0:T(8,128)(2,1)S(1)} %all-to-all-done.4) | copy-start | bytes 6291460
  319.6 19.1 %all-to-all-start.5 = ((f32[16,4,2176]{2,1,0:T(4,128)}), f32[16,4,2176]{2,1,0:T(4,128)S(1)}, u32[]{:S(2)}, u32[]{:S(2)}) async-start(f32[16,4,2176]{2,1,0:T(4,128)} %reshape.60), calls=%async_computation.6 | async-start | bytes 1114112 | tf_op jit(solution)/shard_map/all_to_all | solution.py:567
  338.8 35.6 %all-to-all-start.2 = ((bf16[128,16,512]{2,1,0:T(8,128)(2,1)}), bf16[128,16,512]{2,1,0:T(8,128)(2,1)S(1)}, u32[]{:S(2)}, u32[]{:S(2)}) async-start(bf16[128,16,512]{2,1,0:T(8,128)(2,1)} %bitcast.23), calls=%async_computation.2 | async-start | bytes 4194304 | tf_op jit(solution)/shard_map/all_to_all | solution.py:483
  374.3 12.2 %copy-start.2 = (bf16[128,16,512]{2,1,0:T(8,128)(2,1)}, bf16[128,16,512]{2,1,0:T(8,128)(2,1)S(1)}, u32[]{:S(2)}) copy-start(bf16[128,16,512]{2,1,0:T(8,128)(2,1)S(1)} %all-to-all-done.2) | copy-start | bytes 6291460
  375.3 18.8 %all-to-all-start.6 = ((f32[16,4,2176]{2,1,0:T(4,128)}), f32[16,4,2176]{2,1,0:T(4,128)S(1)}, u32[]{:S(2)}, u32[]{:S(2)}) async-start(f32[16,4,2176]{2,1,0:T(4,128)} %broadcast_in_dim.9), calls=%async_computation.7 | async-start | bytes 1114112 | tf_op jit(solution)/shard_map/all_to_all | solution.py:575
  (7 other events, 5.8 us)
Sparse Core Ops, SparseCore 0:
  45.8 34.3 all-gather.1
  249.5 68.0 reduce-scatter.1

commit v2 on v1

v2 whole, which is shorter than its diff:
```python
import functools

import jax
import jax.numpy as jnp
from jax import lax
from jax.experimental import pallas as pl
from jax.experimental.pallas import tpu as pltpu
from jax.sharding import PartitionSpec as P

HEADS = 16
PATCH = 1024
EPS = 1e-05
BOTH = ("dp", "fsdp")
GAIN_COLS = 128
MARK_COLS = 128
LANES = 128
TILE_ROWS = 16
FAR = -1e30
LOG2E = 1.4426950408889634
F32 = jnp.float32
BF16 = jnp.bfloat16
FORWARD_HEADS, FORWARD_CHUNK = 2, 1024
BACKWARD_HEADS, BACKWARD_CHUNK = 1, 512
PROBS = F32
VMEM_BYTES = 63 * 1024 * 1024


def params(steps=1):
    return pltpu.CompilerParams(
        vmem_limit_bytes=VMEM_BYTES, dimension_semantics=("arbitrary",) * steps
    )


def whole(shape):
    zeros = (0,) * len(shape)
    return pl.BlockSpec(shape, lambda *_: zeros)


SMEM = pl.BlockSpec(memory_space=pltpu.SMEM)
ANY = pl.BlockSpec(memory_space=pl.ANY)


def lasting(us):
    return pl.CostEstimate(flops=int(us * 1e9), bytes_accessed=0, transcendentals=0)


def ones_where(mask, dtype=BF16):
    return jnp.where(mask, 1.0, 0.0).astype(dtype)


def iota(shape, dim):
    return lax.broadcasted_iota(jnp.int32, shape, dim)


def nt(a, b):
    return lax.dot_general(a, b, (((1,), (1,)), ((), ())), preferred_element_type=F32)


def nn(a, b):
    return jnp.dot(a, b, preferred_element_type=F32)


def pick_rows(index_row, rows, first, count):
    slots = index_row.shape[1]
    chosen = ones_where(iota((count, slots), 0) + first == index_row)
    return nn(chosen, rows).astype(BF16)


def slot_targets(count, dest_ref, target_ref, devices):
    arrived = dest_ref.shape[1]
    capacity = arrived // devices
    chunk = 256
    before = ones_where(iota((chunk, chunk), 0) < iota((chunk, chunk), 1))
    base = jnp.zeros((devices, 1), F32)
    for start in range(0, arrived, chunk):
        cols = pl.ds(start, chunk)
        dest = dest_ref[:, cols]
        valid = iota((1, chunk), 1) + start < count
        here = jnp.where((iota((devices, chunk), 0) == dest) & valid, 1.0, 0.0)
        ahead = nn(here.astype(BF16), before) + base
        rank = jnp.sum(here * ahead, axis=0, keepdims=True).astype(jnp.int32)
        base = base + jnp.sum(here, axis=1, keepdims=True)
        target_ref[:, cols] = jnp.where(valid, dest * capacity + rank, -1)


def send_first_kernel(devices, shift_ref, count_ref, dest_ref, slot_ref, rows_ref, send_ref, target_ref):
    step = pl.program_id(0)

    @pl.when(step == 0)
    def _():
        slot_targets(count_ref[0], dest_ref, target_ref, devices)

    block = send_ref.shape[0]
    arrived, width = rows_ref.shape
    chosen = ones_where(iota((block, arrived), 0) + step * block == target_ref[...])
    send_ref[:, :width] = nn(chosen, rows_ref[...]).astype(BF16)
    code = jnp.where(slot_ref[...] < shift_ref[0], 2.0, 1.0)
    send_ref[:, width:] = nt(chosen, jnp.broadcast_to(code, (MARK_COLS, arrived)).astype(BF16)).astype(BF16)


def send_first(shift, count, dest, slot, rows, devices, block=512):
    arrived, width = rows.shape
    wide = width + MARK_COLS
    return pl.pallas_call(
        functools.partial(send_first_kernel, devices),
        grid=(arrived // block,),
        in_specs=[SMEM, SMEM, whole((1, arrived)), whole((1, arrived)), whole((arrived, width))],
        out_specs=[pl.BlockSpec((block, wide), lambda i: (i, 0)), whole((1, arrived))],
        out_shape=[
            jax.ShapeDtypeStruct((arrived, wide), BF16),
            jax.ShapeDtypeStruct((1, arrived), jnp.int32),
        ],
        compiler_params=params(),
        cost_estimate=lasting(9),
        name="send_points",
    )(shift, count, dest, slot, rows)


def pick_kernel(index_ref, rows_ref, *refs):
    out_ref = refs[-1]
    block = out_ref.shape[0]
    out_ref[...] = pick_rows(index_ref[...], rows_ref[...], pl.program_id(0) * block, block)


def pick(index, rows, out_rows, name, after=(), block=512):
    arrived, width = rows.shape
    return pl.pallas_call(
        pick_kernel,
        grid=(out_rows // block,),
        in_specs=[whole((1, arrived)), whole((arrived, width))] + [ANY] * len(after),
        out_specs=pl.BlockSpec((block, width), lambda i: (i, 0)),
        out_shape=jax.ShapeDtypeStruct((out_rows, width), BF16),
        compiler_params=params(),
        cost_estimate=lasting(8),
        name=name,
    )(index, rows, *after)


def places(shift, marks_ref, place_ref):
    slots = marks_ref.shape[0]
    marks = jnp.transpose(marks_ref[...].astype(F32))[:1, :]
    chunk = 256
    before = ones_where(iota((chunk, chunk), 0) < iota((chunk, chunk), 1))
    line = iota((8, 1), 0)
    first = lax.convert_element_type(PATCH - shift, F32)
    base = jnp.where(line == 1, first, 0.0)
    for start in range(0, slots, chunk):
        here = marks[:, start : start + chunk]
        flags = jnp.where(here == (line + 1).astype(F32), 1.0, 0.0)
        flags = jnp.where(line < 2, flags, 0.0)
        earlier = nn(flags.astype(BF16), before) + base
        base = base + jnp.sum(flags, axis=1, keepdims=True)
        place = jnp.sum(flags * earlier, axis=0, keepdims=True).astype(jnp.int32)
        place_ref[:, start : start + chunk] = jnp.where(here > 0.0, place, -1)


def land_first_kernel(shift_ref, marks_ref, rows_ref, *refs):
    own_ref, place_ref = refs[-2:]
    places(shift_ref[0], marks_ref, place_ref)
    own_ref[...] = pick_rows(place_ref[...], rows_ref[...], 0, PATCH)


def land_first(shift, got, width, after):
    slots, wide = got.shape
    return pl.pallas_call(
        land_first_kernel,
        grid=(1,),
        in_specs=[
            SMEM,
            pl.BlockSpec((slots, MARK_COLS), lambda i: (0, width // MARK_COLS)),
            pl.BlockSpec((slots, width), lambda i: (0, 0)),
        ]
        + [ANY] * len(after),
        out_specs=[whole((PATCH, width)), whole((1, slots))],
        out_shape=[
            jax.ShapeDtypeStruct((PATCH, width), BF16),
            jax.ShapeDtypeStruct((1, slots), jnp.int32),
        ],
        compiler_params=params(),
        cost_estimate=lasting(7),
        name="land_points",
    )(shift, got, got, *after)


def pack_kernel(in_ref, out_ref, gain_ref, *refs):
    packed_ref = refs[-1]
    inner, outer = in_ref.shape[1], out_ref.shape[1]
    packed_ref[:, :inner] = in_ref[...]
    packed_ref[:, inner : inner + outer] = out_ref[...]
    column = jnp.transpose(jnp.broadcast_to(gain_ref[...].astype(F32), (GAIN_COLS, gain_ref.shape[1])))
    packed_ref[:, inner + outer :] = column.astype(BF16)


def pack(project_in, project_out, gain, after):
    share = project_in.shape[0]
    columns = project_in.shape[1] + project_out.shape[1] + GAIN_COLS
    return pl.pallas_call(
        pack_kernel,
        grid=(1,),
        in_specs=[whole(project_in.shape), whole(project_out.shape), whole((1, share))]
        + [ANY] * len(after),
        out_specs=whole((share, columns)),
        out_shape=jax.ShapeDtypeStruct((share, columns), BF16),
        compiler_params=params(),
        cost_estimate=lasting(1),
        name="pack_weights",
    )(project_in, project_out, gain.reshape(1, share), *after)


def column_of(row):
    length = row.shape[1]
    return jnp.transpose(jnp.broadcast_to(row, (128, length)))


def spread_rows(index_row, rows):
    wide = column_of(index_row)
    count = wide.shape[0]
    lanes = iota((count, 128), 1)
    chosen = jnp.concatenate(
        [ones_where(wide == lanes + start) for start in range(0, rows.shape[0], 128)], axis=1
    )
    return nn(chosen, rows).astype(BF16)


def spread_kernel(index_ref, rows_ref, *refs):
    out_ref = refs[-1]
    out_ref[...] = spread_rows(index_ref[...], rows_ref[...])


def spread(index, rows, width, name, after=(), block=512):
    slots, source = index.shape[1], rows.shape[0]
    return pl.pallas_call(
        spread_kernel,
        grid=(slots // block,),
        in_specs=[pl.BlockSpec((1, block), lambda i: (0, i)), whole((source, width))]
        + [ANY] * len(after),
        out_specs=pl.BlockSpec((block, width), lambda i: (i, 0)),
        out_shape=jax.ShapeDtypeStruct((slots, width), BF16),
        compiler_params=params(),
        cost_estimate=lasting(8),
        name=name,
    )(index, rows, *after)


def spread_pair_kernel(groups, shift_ref, index_ref, own_ref, other_ref, *refs):
    out_ref, rows = refs[-2:]
    step = pl.program_id(0)

    @pl.when(step == 0)
    def _():
        rows[...] = joined(shift_ref[0], own_ref, other_ref)

    width = rows.shape[1]
    out_ref[:, :width] = spread_rows(index_ref[...], rows[...])
    if groups is None:
        return
    shares, of_rows = groups
    across = shares * TILE_ROWS // of_rows
    members = refs[0].shape[0] // of_rows
    blocks = [
        (keep, got, pl.ds(start, LANES))
        for keep, got in (refs[0:2], refs[2:4])
        for start in range(0, keep.shape[1], LANES)
    ]
    for number, (keep, got, lanes) in enumerate(blocks):
        start = width + number // across * LANES
        for f in range(members):
            source = pl.ds(pl.multiple_of(f * of_rows + step * TILE_ROWS, TILE_ROWS), TILE_ROWS)
            to = (number % across * members + f) * TILE_ROWS
            out_ref[to : to + TILE_ROWS, start : start + LANES] = (
                keep[source, lanes] + got[source, lanes]
            ).astype(BF16)


def spread_pair(shift, index, pair, name, parts=(), groups=None, after=()):
    slots = index.shape[1]
    source, width = pair[0].shape
    blocks = groups[1] // TILE_ROWS if parts else 4
    wide = width + sum(part.shape[1] for part in parts[::2]) * LANES // width
    block = slots // blocks
    return pl.pallas_call(
        functools.partial(spread_pair_kernel, groups),
        grid=(blocks,),
        in_specs=[SMEM, pl.BlockSpec((1, block), lambda i: (0, i))]
        + [whole((source, width))] * 2
        + [whole(part.shape) for part in parts]
        + [ANY] * len(after),
        out_specs=pl.BlockSpec((block, wide), lambda i: (i, 0)),
        out_shape=jax.ShapeDtypeStruct((slots, wide), BF16),
        scratch_shapes=[pltpu.VMEM((source, width), BF16)],
        compiler_params=params(),
        cost_estimate=lasting(6),
        name=name,
    )(shift, index, *pair, *parts, *after)


def add_tiles_kernel(tiles_ref, gain_ref, *refs):
    out_ref = refs[-1]
    slots, lanes = tiles_ref.shape
    pairs = tiles_ref[...].astype(F32).reshape(slots // TILE_ROWS // 2, 2, TILE_ROWS, lanes)
    sums = jnp.sum(pairs, axis=0)
    gain = jnp.concatenate([gain_ref[...], jnp.zeros((TILE_ROWS - 8, LANES), F32)], axis=0)
    line = jnp.concatenate([sums[0], sums[1], gain], axis=1)
    out_ref[...] = jnp.broadcast_to(line[None], out_ref.shape)


def add_tiles(got, gain, width, shares, after):
    slots, wide = got.shape
    more = wide - width
    shape = (shares, TILE_ROWS, 2 * more + LANES)
    return pl.pallas_call(
        add_tiles_kernel,
        grid=(1,),
        in_specs=[pl.BlockSpec((slots, more), lambda i: (0, width // more)), whole(gain.shape)]
        + [ANY] * len(after),
        out_specs=whole(shape),
        out_shape=jax.ShapeDtypeStruct(shape, F32),
        compiler_params=params(),
        cost_estimate=lasting(2),
        name="add_tiles",
    )(got, gain, *after)


def settle_kernel(groups, columns, member_ref, tiles_ref, in_ref, out_ref, gain_ref):
    shares, of_rows = groups
    across = shares * TILE_ROWS // of_rows
    width = out_ref.shape[1]
    half = width // 2
    each = (tiles_ref.shape[2] - LANES) // LANES // 2
    for share in range(shares):
        rows = pl.ds(share // across * TILE_ROWS, TILE_ROWS)
        for core in range(2):
            for k in range(each):
                lane = (core * each + k) * LANES
                tile = tiles_ref[share, :, lane : lane + LANES]
                column = (k * across + share % across) * LANES
                group = column // columns[0]
                column = column - group * columns[0] + core * columns[group]
                part, start = column // half, column % half
                if part < 3:
                    start += part * width + group * half
                    in_ref[rows, start : start + LANES] = tile
                else:
                    start = column - 3 * half
                    out_ref[rows, start : start + LANES] = tile
    gains = jnp.sum(tiles_ref[:, :8, 2 * each * LANES :], axis=0)
    a_line = LANES // of_rows
    mine = iota(gains.shape, 0) == lax.div(member_ref[0], a_line)
    line = jnp.sum(jnp.where(mine, gains, 0.0), axis=0, keepdims=True)
    gain_ref[...] = line[:, :of_rows]
    for piece in range(1, a_line):
        @pl.when(lax.rem(member_ref[0], a_line) == piece)
        def _():
            gain_ref[...] = line[:, piece * of_rows : (piece + 1) * of_rows]


def settle(member, tiles, groups, columns, width):
    of_rows = groups[1]
    shapes = [(of_rows, 3 * width), (of_rows, width), (1, of_rows)]
    return pl.pallas_call(
        functools.partial(settle_kernel, groups, columns),
        grid=(1,),
        in_specs=[SMEM, whole(tiles.shape)],
        out_specs=[whole(shape) for shape in shapes],
        out_shape=[jax.ShapeDtypeStruct(shape, F32) for shape in shapes],
        compiler_params=params(),
        cost_estimate=lasting(2),
        name="settle",
    )(member, tiles)


def gate_kernel(*refs):
    pass


def gate(array, *after):
    return pl.pallas_call(
        gate_kernel,
        in_specs=[ANY] * (1 + len(after)),
        out_specs=ANY,
        out_shape=jax.ShapeDtypeStruct(array.shape, array.dtype),
        input_output_aliases={0: 0},
        compiler_params=pltpu.CompilerParams(has_side_effects=True),
        name="gate",
    )(array, *after)


def joined(shift, own_ref, other_ref):
    row = iota(own_ref.shape, 0)
    return jnp.where(row < PATCH - shift, own_ref[...], other_ref[...])


def attend(key_x, query_x, value, probs_ref, out_ref, step):
    heads, head_width, length = value.shape
    scale = head_width ** (-0.5) * LOG2E
    for start in range(0, length, FORWARD_CHUNK):
        cols = pl.ds(start, FORWARD_CHUNK)
        scores = [nn(jnp.transpose(key_x[h]), query_x[h, :, cols]) for h in range(heads)]
        for h in range(heads):
            top = jnp.max(scores[h], axis=0, keepdims=True)
            weights = jnp.exp2((scores[h] - top) * scale)
            probs = weights * (1.0 / jnp.sum(weights, axis=0, keepdims=True))
            rounded = probs.astype(BF16)
            probs_ref[h, :, cols] = probs.astype(PROBS)
            out_ref[step * heads + h, :, cols] = nn(value[h], rounded).astype(BF16)


def forward_first_kernel(
    shift_ref,
    wrap_ref,
    own_ref,
    other_ref,
    in_ref,
    gain_ref,
    probs_ref,
    hidden_ref,
    normed_ref,
    inverse_ref,
    query_x,
    key_x,
    values_ref,
    attended_ref,
):
    step = pl.program_id(0)
    heads, head_width, length = values_ref.shape
    width = heads * head_width
    extra = query_x.shape[1] - head_width

    @pl.when(step == 0)
    def _():
        rows = joined(shift_ref[0], own_ref, other_ref)
        values_in = jnp.transpose(rows.astype(F32))
        center = values_in - jnp.mean(values_in, axis=0, keepdims=True)
        inverse = lax.rsqrt(jnp.mean(center * center, axis=0, keepdims=True) + EPS)
        normed = center * inverse
        normed_ref[...] = normed
        inverse_ref[...] = inverse
        hidden = (normed * gain_ref[:, :1].astype(F32)).astype(BF16)
        hidden_ref[...] = hidden
        for part, ref in enumerate((query_x, key_x, values_ref)):
            columns = in_ref[:, part * width : (part + 1) * width]
            made = nn(jnp.transpose(columns), hidden).astype(BF16)
            ref[:, :head_width, :] = made.reshape(heads, head_width, length)
        side = iota((extra, length), 1) >= PATCH - shift_ref[0]
        line = iota((extra, length), 0)
        query_side = jnp.where(((line == 0) & ~side) | ((line == 1) & side), 1.0, 0.0)
        key_side = jnp.where(((line == 0) & side) | ((line == 1) & ~side), FAR, 0.0)
        key_side = jnp.where(wrap_ref[0] > 0, key_side, 0.0)
        for h in range(heads):
            query_x[h, head_width:, :] = query_side.astype(BF16)
            key_x[h, head_width:, :] = key_side.astype(BF16)

    count = probs_ref.shape[0]
    mine = pl.ds(step * count, count)
    attend(key_x.at[mine], query_x.at[mine], values_ref.at[mine], probs_ref, attended_ref, step)


def forward_last_kernel(
    shift_ref,
    own_ref,
    other_ref,
    out_ref,
    query_x,
    key_x,
    value_ref,
    first_ref,
    probs_ref,
    attended_ref,
    block_ref,
):
    step = pl.program_id(0)
    length, width = own_ref.shape
    attend(key_x, query_x, value_ref, probs_ref, attended_ref, step)

    @pl.when(step == pl.num_programs(0) - 1)
    def _():
        rows = joined(shift_ref[0], own_ref, other_ref)
        attended = jnp.concatenate(
            [r[...].reshape(width // 2, length) for r in (first_ref, attended_ref)], axis=0
        )
        added = nn(jnp.transpose(out_ref[...]), attended)
        block_ref[...] = (rows.astype(F32) + jnp.transpose(added)).astype(BF16)


def per_step(shape, first):
    return pl.BlockSpec(shape, lambda i: (i + first, 0, 0))


def forward(shift, wrap, pair, weights):
    length, width = pair[0].shape
    head_width = width // HEADS
    some = HEADS // 2
    count = FORWARD_HEADS
    extended = (HEADS, head_width + 16, length)
    split = (HEADS, head_width, length)
    first_split = (some, head_width, length)
    rows_specs = [whole((length, width))] * 2
    probs_a, hidden, normed, inverse, query_x, key_x, values, attended_a = pl.pallas_call(
        forward_first_kernel,
        grid=(some // count,),
        in_specs=[SMEM, SMEM]
        + rows_specs
        + [
            pl.BlockSpec((width, 3 * width), lambda h: (0, 0)),
            pl.BlockSpec((width, GAIN_COLS), lambda h: (0, 4 * width // GAIN_COLS)),
        ],
        out_specs=[
            per_step((count, length, length), 0),
            whole((width, length)),
            whole((width, length)),
            whole((1, length)),
            whole(extended),
            whole(extended),
            whole(split),
            whole(first_split),
        ],
        out_shape=[
            jax.ShapeDtypeStruct((some, length, length), PROBS),
            jax.ShapeDtypeStruct((width, length), BF16),
            jax.ShapeDtypeStruct((width, length), F32),
            jax.ShapeDtypeStruct((1, length), F32),
            jax.ShapeDtypeStruct(extended, BF16),
            jax.ShapeDtypeStruct(extended, BF16),
            jax.ShapeDtypeStruct(split, BF16),
            jax.ShapeDtypeStruct(first_split, BF16),
        ],
        compiler_params=params(),
        cost_estimate=lasting(25),
        name="forward_first",
    )(shift, wrap, *pair, weights, weights)
    skip = some // count
    probs_b, attended_b, block = pl.pallas_call(
        forward_last_kernel,
        grid=(some // count,),
        in_specs=[SMEM]
        + rows_specs
        + [
            pl.BlockSpec((width, width), lambda h: (0, 3)),
            per_step((count,) + extended[1:], skip),
            per_step((count,) + extended[1:], skip),
            per_step((count,) + split[1:], skip),
            whole(first_split),
        ],
        out_specs=[
            per_step((count, length, length), 0),
            whole(first_split),
            whole((length, width)),
        ],
        out_shape=[
            jax.ShapeDtypeStruct((some, length, length), PROBS),
            jax.ShapeDtypeStruct(first_split, BF16),
            jax.ShapeDtypeStruct((length, width), BF16),
        ],
        compiler_params=params(),
        cost_estimate=lasting(20),
        name="forward_last",
    )(shift, *pair, weights, query_x, key_x, values, attended_a)
    return block, (probs_a, probs_b), (query_x, key_x, values), (attended_a, attended_b), (
        hidden,
        normed,
        inverse,
    )


def attend_back(probs_ref, query_x, key_x, values_ref, attended_ref, upstream_ref, grads_ref, step):
    heads, head_width, length = values_ref.shape
    scale = head_width ** (-0.5)
    for h in range(heads):
        query, key, value = query_x[h, :head_width, :], key_x[h, :head_width, :], values_ref[h]
        upstream = upstream_ref[h]
        value_rows = jnp.transpose(value)
        offset = jnp.sum(
            upstream.astype(F32) * attended_ref[h].astype(F32), axis=0, keepdims=True
        )
        head = step * heads + h
        key_grad = value_grad = 0.0
        for start in range(0, length, BACKWARD_CHUNK):
            cols = slice(start, start + BACKWARD_CHUNK)
            probs = probs_ref[h, :, cols]
            along = nn(value_rows, upstream[:, cols])
            slopes = (probs.astype(F32) * (along - offset[:, cols]) * scale).astype(BF16)
            grads_ref[0, head, :, cols] = nn(key, slopes).astype(BF16)
            key_grad = key_grad + nt(query[:, cols], slopes)
            value_grad = value_grad + nt(upstream[:, cols], probs.astype(BF16))
        grads_ref[1, head] = key_grad.astype(BF16)
        grads_ref[2, head] = value_grad.astype(BF16)


def backward_first_kernel(
    shift_ref,
    own_ref,
    other_ref,
    out_ref,
    probs_ref,
    query_x,
    key_x,
    values_ref,
    attended_ref,
    hidden_ref,
    attended_a_ref,
    attended_b_ref,
    core_ref,
    cot_ref,
    upstream_b_ref,
    grads_ref,
    keep_ref,
    send_ref,
    upstream_a,
):
    step = pl.program_id(0)
    some, head_width, length = upstream_a.shape
    count = probs_ref.shape[0]

    @pl.when(step == 0)
    def _():
        rows = joined(shift_ref[0], own_ref, other_ref)
        cot_ref[...] = rows
        upstream = nt(out_ref[...], rows).astype(BF16).reshape(2, some, head_width, length)
        upstream_a[...] = upstream[0]
        upstream_b_ref[...] = upstream[1]

    attend_back(
        probs_ref,
        query_x,
        key_x,
        values_ref,
        attended_ref,
        upstream_a.at[pl.ds(step * count, count)],
        grads_ref,
        step,
    )

    @pl.when(step == pl.num_programs(0) - 1)
    def _():
        width = cot_ref.shape[1]
        part_in = nt(hidden_ref[...], grads_ref[...].reshape(3 * width // 2, length))
        part_out = [
            nn(out[...].reshape(width // 2, length), cot_ref[...])
            for out in (attended_a_ref, attended_b_ref)
        ]
        parts = jnp.concatenate([part_in, jnp.concatenate(part_out, axis=0)], axis=1)
        keep_and_send(core_ref[0], parts, keep_ref, send_ref)


def keep_and_send(core, parts, keep_ref, send_ref):
    half = parts.shape[1] // 2
    first, second = parts[:, :half], parts[:, half:]
    keep_ref[...] = jnp.where(core == 0, first, second)
    send_ref[...] = jnp.where(core == 0, second, first)


def backward_last_kernel(
    in_ref,
    gain_ref,
    probs_ref,
    hidden_ref,
    normed_ref,
    inverse_ref,
    query_x,
    key_x,
    values_ref,
    attended_ref,
    upstream_ref,
    first_ref,
    cot_ref,
    core_ref,
    *refs,
):
    grad_ref, keep_ref, send_ref, gain_out, grads = refs[-5:]
    step = pl.program_id(0)
    length, width = cot_ref.shape
    half = width // 2
    attend_back(
        probs_ref, query_x, key_x, values_ref, attended_ref, upstream_ref, grads, step
    )

    @pl.when(step == pl.num_programs(0) - 1)
    def _():
        grad_hidden = 0.0
        for group, ref in enumerate((first_ref, grads)):
            for part in range(3):
                first = part * width + group * half
                grad_hidden = grad_hidden + nn(
                    in_ref[:, first : first + half], ref[part].reshape(half, length)
                )
        parts = nt(hidden_ref[...], grads[...].reshape(3 * half, length))
        keep_and_send(core_ref[0], parts, keep_ref, send_ref)
        normed = normed_ref[...]
        part_gain = jnp.sum(grad_hidden * normed, axis=1, keepdims=True)
        part_gain = jnp.transpose(jnp.broadcast_to(part_gain, (width, LANES)))[:1, :]
        lines = [part_gain[:, start : start + LANES] for start in range(0, width, LANES)]
        lines.append(jnp.zeros((8 - len(lines), LANES), F32))
        gain_out[...] = jnp.concatenate(lines, axis=0)
        scaled = grad_hidden * gain_ref[:, :1].astype(F32)
        middle = jnp.mean(scaled, axis=0, keepdims=True)
        slope = jnp.mean(scaled * normed, axis=0, keepdims=True)
        change = inverse_ref[...] * (scaled - middle - normed * slope)
        grad_ref[...] = (cot_ref[...].astype(F32) + jnp.transpose(change)).astype(BF16)


def backward_first(shift, pair, weights, probs, split, attended, hidden, core):
    length, width = pair[0].shape
    head_width = width // HEADS
    some = HEADS // 2
    count = BACKWARD_HEADS
    group = (some, head_width, length)
    extended = (count, head_width + 16, length)
    return pl.pallas_call(
        backward_first_kernel,
        grid=(some // count,),
        in_specs=[
            SMEM,
            whole((length, width)),
            whole((length, width)),
            pl.BlockSpec((width, width), lambda h: (0, 3)),
            per_step((count, length, length), 0),
            per_step(extended, 0),
            per_step(extended, 0),
            per_step((count, head_width, length), 0),
            per_step((count, head_width, length), 0),
            whole((width, length)),
            whole(group),
            whole(group),
            SMEM,
        ],
        out_specs=[
            whole((length, width)),
            whole(group),
            whole((3,) + group),
            whole((width, 5 * width // 4)),
            whole((width, 5 * width // 4)),
        ],
        out_shape=[
            jax.ShapeDtypeStruct((length, width), BF16),
            jax.ShapeDtypeStruct(group, BF16),
            jax.ShapeDtypeStruct((3,) + group, BF16),
            jax.ShapeDtypeStruct((width, 5 * width // 4), F32),
            jax.ShapeDtypeStruct((width, 5 * width // 4), F32),
        ],
        scratch_shapes=[pltpu.VMEM(group, BF16)],
        compiler_params=params(),
        cost_estimate=lasting(25),
        name="backward_first",
    )(shift, *pair, weights, probs, *split, attended[0], hidden, *attended, core)


def backward_last(weights, probs, rows, split, attended, upstream, first, cot, core, after):
    length, width = cot.shape
    head_width = width // HEADS
    some = HEADS // 2
    count = BACKWARD_HEADS
    skip = some // count
    group = (some, head_width, length)
    extended = (count, head_width + 16, length)
    one = (count, head_width, length)
    return pl.pallas_call(
        backward_last_kernel,
        grid=(some // count,),
        in_specs=[
            pl.BlockSpec((width, 3 * width), lambda h: (0, 0)),
            pl.BlockSpec((width, GAIN_COLS), lambda h: (0, 4 * width // GAIN_COLS)),
            per_step((count, length, length), 0),
            whole((width, length)),
            whole((width, length)),
            whole((1, length)),
            per_step(extended, skip),
            per_step(extended, skip),
            per_step(one, skip),
            per_step(one, 0),
            per_step(one, 0),
            whole((3,) + group),
            whole((length, width)),
            SMEM,
        ]
        + [ANY] * len(after),
        out_specs=[
            whole((length, width)),
            whole((width, 3 * width // 4)),
            whole((width, 3 * width // 4)),
            whole((8, LANES)),
        ],
        out_shape=[
            jax.ShapeDtypeStruct((length, width), BF16),
            jax.ShapeDtypeStruct((width, 3 * width // 4), F32),
            jax.ShapeDtypeStruct((width, 3 * width // 4), F32),
            jax.ShapeDtypeStruct((8, LANES), F32),
        ],
        scratch_shapes=[pltpu.VMEM((3,) + group, BF16)],
        compiler_params=params(),
        cost_estimate=lasting(25),
        name="backward_last",
    )(
        weights,
        weights,
        probs,
        *rows,
        *split,
        attended[1],
        upstream,
        first,
        cot,
        core,
        *after,
    )


def exchange(rows, devices):
    moved = lax.all_to_all(
        rows.reshape(devices, rows.shape[0] // devices, rows.shape[1]),
        BOTH,
        split_axis=0,
        concat_axis=0,
        tiled=True,
    )
    return moved.reshape(rows.shape)


def with_ahead(rows, devices):
    pairs = [((i + 1) % devices, i) for i in range(devices)]
    return rows, lax.ppermute(rows, BOTH, pairs)


def with_behind(rows, devices):
    pairs = [(i, (i + 1) % devices) for i in range(devices)]
    return rows, lax.ppermute(rows, BOTH, pairs)


def other_core(array):
    pairs = [(i, i ^ 1) for i in range(lax.axis_size("fsdp"))]
    return lax.ppermute(array, "fsdp", pairs)


def over_fsdp(terms):
    count, far = lax.axis_size("fsdp"), 1
    while far < count:
        terms = terms + lax.ppermute(terms, "fsdp", [(i, i ^ far) for i in range(count)])
        far *= 2
    return terms


def body(
    points,
    cotangent,
    destination,
    curve_slot,
    point_counts,
    shift_offset,
    project_in,
    project_out,
    norm_gain,
):
    devices = lax.axis_size(BOTH)
    groups = lax.axis_size("dp")
    arrived, width = points.shape
    share = project_in.shape[0]
    device = lax.axis_index(BOTH)
    wrap = (device == devices - 1).astype(jnp.int32).reshape(1)

    send_points, target = send_first(
        shift_offset,
        point_counts,
        destination.reshape(1, arrived),
        curve_slot.reshape(1, arrived),
        points,
        devices,
    )
    got_points = exchange(send_points, devices)
    packed = pack(project_in, project_out, norm_gain, (target,))
    weights = lax.all_gather(packed, "fsdp", axis=0, tiled=True)
    send_cot = pick(target, cotangent, arrived, "send_cot")
    own_points, place = land_first(shift_offset, got_points, width, (send_cot,))
    points_pair = with_ahead(own_points, devices)
    got_cot = exchange(gate(send_cot, points_pair[1]), devices)

    block, (probs_a, probs_b), split, attended, (hidden, normed, inverse) = forward(
        shift_offset, wrap, points_pair, weights
    )
    own_cot = pick(place, got_cot, PATCH, "land_cot", (probs_a,), PATCH)
    cot_pair = with_ahead(own_cot, devices)
    block_pair = with_behind(block, devices)

    member = lax.axis_index("fsdp").astype(jnp.int32)
    core = (member % 2).reshape(1)
    cot, upstream, first_grads, first_keep, first_send = backward_first(
        shift_offset, cot_pair, weights, probs_a, split, attended, hidden, core
    )
    spread_block = spread_pair(shift_offset, place, block_pair, "back_block", after=(first_grads,))
    back_block = exchange(spread_block, devices)
    grad, last_keep, last_send, part_gain = backward_last(
        weights,
        probs_b,
        (hidden, normed, inverse),
        split,
        attended,
        upstream,
        first_grads,
        cot,
        core,
        (spread_block,),
    )
    grad_pair = with_behind(grad, devices)
    dealt = (groups, share)
    parts = (first_keep, other_core(first_send), last_keep, other_core(last_send))
    gain_terms = over_fsdp(part_gain)
    spread_grad = spread_pair(
        shift_offset, place, grad_pair, "back_grad", parts, dealt, (back_block, gain_terms)
    )
    back_grad = exchange(spread_grad, devices)
    block_out = spread(target, back_block, width, "block_out", (spread_grad,))
    sums = add_tiles(back_grad, gain_terms, width, groups, (block_out,))
    tiles = lax.all_to_all(sums, "dp", split_axis=0, concat_axis=0, tiled=True)
    point_grad = spread(target, back_grad, width, "point_grad", (sums,))
    columns = (first_keep.shape[1], last_keep.shape[1])
    grad_in, grad_out, grad_gain = settle(member.reshape(1), tiles, dealt, columns, width)
    return block_out, point_grad, grad_in, grad_out, grad_gain.reshape(share)


def solution(mesh):
    in_specs = (
        P(BOTH, None),
        P(BOTH, None),
        P(BOTH),
        P(BOTH),
        P(BOTH),
        P(),
        P("fsdp", None),
        P("fsdp", None),
        P("fsdp"),
    )
    out_specs = (
        P(BOTH, None),
        P(BOTH, None),
        P("fsdp", None),
        P("fsdp", None),
        P("fsdp"),
    )
    return jax.shard_map(body, mesh=mesh, in_specs=in_specs, out_specs=out_specs, check_vma=False)
```

time: 405 us -> 332 us (0.82)
  local copies, waits for them, and re-layouts: 22.9 us -> 1.82 us
  blocking collectives: 20.3 us -> 0 us
  Pallas kernels: 178 us -> 161 us
  starting transfers between devices: 62.5 us -> 53 us
  waiting for transfers between devices: 104 us -> 98.7 us
    reduce_scatter x1 -> x0, waiting for transfers between devices: 26.7 us -> none  [body(): shares = lax.psum_scatter(parts, 'fsdp', scatter_dimension=0, tiled=True)]
    ppermute x8 -> x9, waiting for transfers between devices: 6.82 us -> 27.1 us  [the longest x2 12.6 us: with_ahead(): return (rows, lax.ppermute(rows, BOTH, pairs))]
    all_to_all x1 -> x0, blocking collectives: 20.3 us -> none  [body(): lax.all_to_all(marks, BOTH, split_axis=0, concat_axis=0, tiled=True)]
    ppermute x8 -> x9, starting transfers between devices: 22.5 us -> 8.63 us  [the longest x2 3.85 us: with_ahead(): return (rows, lax.ppermute(rows, BOTH, pairs))]
    all_to_all x4, starting transfers between devices: 27.5 us -> 40.7 us  [exchange(): lax.all_to_all(rows.reshape(devices, rows.shape[0] // devices, rows.shape...]
    pallas_call x6 -> x12, Pallas kernels: 145 us -> 134 us  [the longest x1 27.8 us: backward_first(): pl.pallas_call(backward_first_kernel, grid=(some // count,), in_specs=[SM...]
    all_to_all x2 -> x1, starting transfers between devices: 12.4 us -> 3.59 us  [body(): tiles = lax.all_to_all(sums, 'dp', split_axis=0, concat_axis=0, tiled=True)]
    slice x7 -> x0, local copies, waits for them, and re-layouts: 6.67 us -> none  [the longest x2 3.5 us: neighbours(): rows[half:]]
  transfers between devices with their start and end apart: 16 -> 15, of which waited for: 6 -> 9; matrix products, arithmetic and copies ran while one was open for 3% -> 0% of each run, Pallas kernels for 28% -> 39%
where the time goes in v2:
time: 332 us; the launch traced here: 331 us
  Pallas kernels  161 us (48%)
  waiting for transfers between devices  98.7 us (30%)
  starting transfers between devices  53 us (16%)
  between operations  15.4 us (5%)
    all_to_all x4, waiting for transfers between devices, exchange(): lax.all_to_all(rows.reshape(devices, rows.shape[0] // devices, rows.shape...  66.5 us
    all_to_all x4, starting transfers between devices, exchange(): lax.all_to_all(rows.reshape(devices, rows.shape[0] // devices, rows.shape...  40.7 us
    pallas_call x1, Pallas kernels, backward_first(): pl.pallas_call(backward_first_kernel, grid=(some // count,), in_specs=[SM...  27.8 us
    pallas_call x1, Pallas kernels, backward_last(): pl.pallas_call(backward_last_kernel, grid=(some // count,), in_specs=[pl....  27.4 us
    pallas_call x1, Pallas kernels, forward(): pl.pallas_call(forward_first_kernel, grid=(some // count,), in_specs=[SME...  23.6 us
    pallas_call x1, Pallas kernels, forward(): pl.pallas_call(forward_last_kernel, grid=(some // count,), in_specs=[SMEM...  20.8 us
    pallas_call x2, Pallas kernels, spread(): pl.pallas_call(spread_kernel, grid=(slots // block,), in_specs=[pl.BlockS...  15.3 us
    pallas_call x2, Pallas kernels, spread_pair(): pl.pallas_call(functools.partial(spread_pair_kernel, groups), grid=(block...  12.7 us
  transfers between devices with their start and end apart: 15, of which 9 were waited for; matrix products, arithmetic and copies ran while one was open for 0% of the time, Pallas kernels for 39%

profile of v2, /device:TPU:0, one launch (start us, length us, event | category | flops | bytes accessed | tf_op | source)
XLA Modules:
  0.0 331.4 jit_solution(10700829008659560571)
XLA Ops:
  8.5 10.2 %send_points.1 = (bf16[2048,640]{1,0:T(8,128)(2,1)}, s32[1,2048]{1,0:T(1,128)}) custom-call(s32[1]{0:T(128)S(6)} %copy.17.shift_ref, s32[1]{0:T(128)S(6)} %copy.16.count_ref, s32[1,2048]{1,0:T(1,128)} %bitcast.19, s32[1,2048]{1,0:T(1,128)} %bitcast.20, bf16[2048,512]{1,0:T(8,128)(2,1)} %rows_ref.2), custom_call_target="tpu_custom_call" | custom-call | flops 8999999488 | tf_op jit(solution)/shard_map/send_points/pallas_call | solution.py:104
  18.6 11.6 %all-to-all-start = ((bf16[128,16,640]{2,1,0:T(8,128)(2,1)}), bf16[128,16,640]{2,1,0:T(8,128)(2,1)}, u32[]{:S(2)}, u32[]{:S(2)}) async-start(bf16[128,16,640]{2,1,0:T(8,128)(2,1)} %bitcast.17), calls=%async_computation | async-start | bytes 5242880 | tf_op jit(solution)/shard_map/all_to_all | solution.py:808
  32.1 7.5 %send_cot.1.refs_0_ = bf16[2048,512]{1,0:T(8,128)(2,1)} custom-call(s32[1,2048]{1,0:T(1,128)} %get-tuple-element.32.index_ref.refs_0_, bf16[2048,512]{1,0:T(8,128)(2,1)} %rows_ref.3), custom_call_target="tpu_custom_call" | custom-call | flops 8000000000 | tf_op jit(solution)/shard_map/send_cot/pallas_call | solution.py:127
  39.5 26.5 %all-to-all-done = bf16[128,16,640]{2,1,0:T(8,128)(2,1)} async-done(((bf16[128,16,640]{2,1,0:T(8,128)(2,1)}), bf16[128,16,640]{2,1,0:T(8,128)(2,1)}, u32[]{:S(2)}, u32[]{:S(2)}) %all-to-all-start) | async-done | bytes 2621472 | tf_op jit(solution)/shard_map/all_to_all | solution.py:808
  66.0 5.4 %land_points.1 = (bf16[1024,512]{1,0:T(8,128)(2,1)}, s32[1,2048]{1,0:T(1,128)}) custom-call(s32[1]{0:T(128)S(6)} %copy.17.shift_ref, bf16[2048,640]{1,0:T(8,128)(2,1)} %bitcast.3.marks_ref.rows_ref, bf16[2048,640]{1,0:T(8,128)(2,1)} %bitcast.3.marks_ref.rows_ref, bf16[2048,512]{1,0:T(8,128)(2,1)} %send_cot.1.refs_0_), custom_call_target="tpu_custom_call" | custom-call | flops 7000000000 | tf_op jit(solution)/shard_map/land_points/pallas_call | solution.py:165
  71.4 3.1 collective-permute-start
  74.6 12.6 %collective-permute-done.other_ref.refs_1_ = bf16[1024,512]{1,0:T(8,128)(2,1)S(1)} collective-permute-done((bf16[1024,512]{1,0:T(8,128)(2,1)}, bf16[1024,512]{1,0:T(8,128)(2,1)S(1)}, u32[]{:S(2)}, u32[]{:S(2)}) %collective-permute-start) | collective-permute-done | bytes 1048608 | tf_op jit(solution)/shard_map/ppermute | solution.py:820
  88.2 9.9 %all-to-all-start.1 = ((bf16[128,16,512]{2,1,0:T(8,128)(2,1)}), bf16[128,16,512]{2,1,0:T(8,128)(2,1)}, u32[]{:S(2)}, u32[]{:S(2)}) async-start(bf16[128,16,512]{2,1,0:T(8,128)(2,1)} %bitcast.15), calls=%async_computation.1 | async-start | bytes 4194304 | tf_op jit(solution)/shard_map/all_to_all | solution.py:808
  98.1 23.6 %forward_first.1 = (f32[8,1024,1024]{2,1,0:T(8,128)}, bf16[512,1024]{1,0:T(8,128)(2,1)}, f32[512,1024]{1,0:T(8,128)}, f32[1,1024]{1,0:T(1,128)}, bf16[16,48,1024...) custom-call(s32[1]{0:T(128)S(6)} %copy.17.shift_ref, ...), custom_call_target="tpu_custom_call" | custom-call | flops 24999999488 | tf_op jit(solution)/shard_map/forward_first/pallas_call | solution.py:498
  121.7 6.2 %all-to-all-done.1 = bf16[128,16,512]{2,1,0:T(8,128)(2,1)} async-done(((bf16[128,16,512]{2,1,0:T(8,128)(2,1)}), bf16[128,16,512]{2,1,0:T(8,128)(2,1)}, u32[]{:S(2)}, u32[]{:S(2)}) %all-to-all-start.1) | async-done | bytes 2097184 | tf_op jit(solution)/shard_map/all_to_all | solution.py:808
  127.9 4.9 %land_cot.1.own_ref = bf16[1024,512]{1,0:T(8,128)(2,1)} custom-call(s32[1,2048]{1,0:T(1,128)} %get-tuple-element.34.index_ref, bf16[2048,512]{1,0:T(8,128)(2,1)} %bitcast.7.rows_ref, f32[8,1024,1024]{2,1,0:T(8,128)} %get-tuple-element.41.refs_0_.probs_ref), custom_call_target="tpu_custom_call" | custom-call | flops 8000000000 | tf_op jit(solution)/shard_map/land_cot/pallas_call | solution.py:127
  133.5 20.8 %forward_last.1 = (f32[8,1024,1024]{2,1,0:T(8,128)}, bf16[8,32,1024]{2,1,0:T(8,128)(2,1)}, bf16[1024,512]{1,0:T(8,128)(2,1)}) custom-call(s32[1]{0:T(128)S(6)} %copy.17.shift_ref, bf16[1024,512]{1,0:T(8,128)(2,1)} %get-tuple-element.35.own_ref, bf16[1024,512]{1,0:T(8,128)(2,1)} %copy-done, ...), custom_call_target="tpu_custom_call" | custom-call | flops 20000000000 | tf_op jit(solution)/shard_map/forward_last/pallas_call | solution.py:532
  154.5 27.8 %backward_first.1 = (bf16[1024,512]{1,0:T(8,128)(2,1)}, bf16[8,32,1024]{2,1,0:T(8,128)(2,1)}, bf16[3,8,32,1024]{3,2,1,0:T(8,128)(2,1)}, f32[512,640]{1,0:T(8,128)}, f32[512,640]{1,0:T(8,128)}) custom-call(s32[1]{0:T(128)S(6)} %copy.17.shift_ref, bf16[1024,512]{1,0:T(8,128)(2,1)} %land_cot.1.own_ref, bf16[1024,512]{1,0:T(8,128)(2,1)} %collective-permute-done.2.other_ref, ...), custom_call_target="tpu_custom_call" | custom-call | flops 24999999488 | tf_op jit(solution)/shard_map/backward_first/pallas_call | solution.py:708
  182.3 5.6 %back_block.1.refs_0_ = bf16[2048,512]{1,0:T(8,128)(2,1)} custom-call(s32[1]{0:T(128)S(6)} %copy.17.shift_ref, s32[1,2048]{1,0:T(1,128)} %get-tuple-element.34.index_ref, bf16[1024,512]{1,0:T(8,128)(2,1)} %get-tuple-element.40.own_ref, bf16[1024,512]{1,0:T(8,128)(2,1)} %collective-permute-done.1.other_ref, ...), custom_call_target="tpu_custom_call" | custom-call | flops 6000000000 | tf_op jit(solution)/shard_map/back_block/pallas_call | solution.py:281
  187.9 9.6 %all-to-all-start.2 = ((bf16[128,16,512]{2,1,0:T(8,128)(2,1)}), bf16[128,16,512]{2,1,0:T(8,128)(2,1)}, u32[]{:S(2)}, u32[]{:S(2)}) async-start(bf16[128,16,512]{2,1,0:T(8,128)(2,1)} %bitcast.18), calls=%async_computation.2 | async-start | bytes 4194304 | tf_op jit(solution)/shard_map/all_to_all | solution.py:808
  197.6 27.4 %backward_last.1 = (bf16[1024,512]{1,0:T(8,128)(2,1)}, f32[512,384]{1,0:T(8,128)}, f32[512,384]{1,0:T(8,128)}, f32[8,128]{1,0:T(8,128)}) custom-call(bf16[512,2176]{1,0:T(8,128)(2,1)} %all-gather.2.cloned.1.call-done.in_ref.gain_ref.out_ref, bf16[512,2176]{1,0:T(8,128)(2,1)} %all-gather.2.cloned.1.call-done.in_ref.gain_ref.out_ref, ...), custom_call_target="tpu_custom_call" | custom-call | flops 24999999488 | tf_op jit(solution)/shard_map/backward_last/pallas_call | solution.py:756
  239.3 5.9 %collective-permute-done.3.other_ref = bf16[1024,512]{1,0:T(8,128)(2,1)} collective-permute-done((bf16[1024,512]{1,0:T(8,128)(2,1)}, bf16[1024,512]{1,0:T(8,128)(2,1)}, u32[]{:S(2)}, u32[]{:S(2)}) %collective-permute-start.3) | collective-permute-done | bytes 1048608 | tf_op jit(solution)/shard_map/ppermute | solution.py:825
  245.2 7.1 %back_grad.1.refs_0_ = bf16[2048,768]{1,0:T(8,128)(2,1)} custom-call(s32[1]{0:T(128)S(6)} %copy.17.shift_ref, s32[1,2048]{1,0:T(1,128)} %get-tuple-element.34.index_ref, bf16[1024,512]{1,0:T(8,128)(2,1)} %get-tuple-element.50.own_ref, bf16[1024,512]{1,0:T(8,128)(2,1)} %collective-permute-done.3.other_ref, f32[512,640]{1,0:T(8,128)} %get-tuple-element.51.refs_0_, ...), custom_call_target="tpu_custom_call" | custom-call | flops 6000000000 | tf_op jit(solution)/shard_map/back_grad/pallas_call | solution.py:281
  252.3 9.6 %all-to-all-start.3 = ((bf16[128,16,768]{2,1,0:T(8,128)(2,1)}), bf16[128,16,768]{2,1,0:T(8,128)(2,1)}, u32[]{:S(2)}, u32[]{:S(2)}) async-start(bf16[128,16,768]{2,1,0:T(8,128)(2,1)} %bitcast.16), calls=%async_computation.3 | async-start | bytes 6291456 | tf_op jit(solution)/shard_map/all_to_all | solution.py:808
  261.9 7.6 %block_out.1.refs_0_ = bf16[2048,512]{1,0:T(8,128)(2,1)} custom-call(s32[1,2048]{1,0:T(1,128)} %get-tuple-element.32.index_ref.refs_0_, bf16[2048,512]{1,0:T(8,128)(2,1)} %bitcast.10.refs_4_.rows_ref, bf16[2048,768]{1,0:T(8,128)(2,1)} %back_grad.1.refs_0_), custom_call_target="tpu_custom_call" | custom-call | flops 8000000000 | tf_op jit(solution)/shard_map/block_out/pallas_call | solution.py:232
  269.6 33.7 %all-to-all-done.3 = bf16[128,16,768]{2,1,0:T(8,128)(2,1)} async-done(((bf16[128,16,768]{2,1,0:T(8,128)(2,1)}), bf16[128,16,768]{2,1,0:T(8,128)(2,1)}, u32[]{:S(2)}, u32[]{:S(2)}) %all-to-all-start.3) | async-done | bytes 3145760 | tf_op jit(solution)/shard_map/all_to_all | solution.py:808
  305.5 3.6 %all-to-all-start.4 = ((f32[16,16,640]{2,1,0:T(8,128)}), f32[16,16,640]{2,1,0:T(8,128)S(1)}, u32[]{:S(2)}, u32[]{:S(2)}) async-start(f32[16,16,640]{2,1,0:T(8,128)} %add_tiles.1.refs_0_), calls=%async_computation.4 | async-start | bytes 1310720 | tf_op jit(solution)/shard_map/all_to_all | solution.py:911
  309.1 7.6 %point_grad.1 = bf16[2048,512]{1,0:T(8,128)(2,1)} custom-call(s32[1,2048]{1,0:T(1,128)} %get-tuple-element.32.index_ref.refs_0_, bf16[2048,768]{1,0:T(8,128)(2,1)} %bitcast.12.tiles_ref.rows_ref, f32[16,16,640]{2,1,0:T(8,128)} %add_tiles.1.refs_0_), custom_call_target="tpu_custom_call" | custom-call | flops 8000000000 | tf_op jit(solution)/shard_map/point_grad/pallas_call | solution.py:232
  316.8 5.1 %all-to-all-done.4.tiles_ref = f32[16,16,640]{2,1,0:T(8,128)S(1)} async-done(((f32[16,16,640]{2,1,0:T(8,128)}), f32[16,16,640]{2,1,0:T(8,128)S(1)}, u32[]{:S(2)}, u32[]{:S(2)}) %all-to-all-start.4) | async-done | bytes 655392 | tf_op jit(solution)/shard_map/all_to_all | solution.py:911
  (32 shorter events, 23.1 us)
Async XLA Ops:
  18.6 47.4 %all-to-all-start = ((bf16[128,16,640]{2,1,0:T(8,128)(2,1)}), bf16[128,16,640]{2,1,0:T(8,128)(2,1)}, u32[]{:S(2)}, u32[]{:S(2)}) async-start(bf16[128,16,640]{2,1,0:T(8,128)(2,1)} %bitcast.17), calls=%async_computation | async-start | bytes 5242880 | tf_op jit(solution)/shard_map/all_to_all | solution.py:808
  30.2 67.9 %all-gather.2.cloned.1.call-start = ((), (), s32[]{:S(2)}) async-start(), calls=%async_computation.5 | async-start | bytes 2506752 | tf_op jit(solution)/shard_map/all_gather | solution.py:869
  71.4 15.8 %collective-permute-start = (bf16[1024,512]{1,0:T(8,128)(2,1)}, bf16[1024,512]{1,0:T(8,128)(2,1)S(1)}, u32[]{:S(2)}, u32[]{:S(2)}) collective-permute-start(bf16[1024,512]{1,0:T(8,128)(2,1)} %get-tuple-element.35.own_ref), channel_id=1, source_target_pairs={{1,0},{2,1},{3,2},{4,3},{5,4},{6,5},{7,6},{8,7},{9,8},{10,9},{11,1... | collective-permute-start | bytes 3145736 | tf_op jit(solution)/shard_map/ppermute | solution.py:820
  87.2 1.0 copy-start
  88.2 39.7 %all-to-all-start.1 = ((bf16[128,16,512]{2,1,0:T(8,128)(2,1)}), bf16[128,16,512]{2,1,0:T(8,128)(2,1)}, u32[]{:S(2)}, u32[]{:S(2)}) async-start(bf16[128,16,512]{2,1,0:T(8,128)(2,1)} %bitcast.15), calls=%async_computation.1 | async-start | bytes 4194304 | tf_op jit(solution)/shard_map/all_to_all | solution.py:808
  132.8 21.7 %collective-permute-start.2 = (bf16[1024,512]{1,0:T(8,128)(2,1)}, bf16[1024,512]{1,0:T(8,128)(2,1)}, u32[]{:S(2)}, u32[]{:S(2)}) collective-permute-start(bf16[1024,512]{1,0:T(8,128)(2,1)} %land_cot.1.own_ref), channel_id=1, source_target_pairs={{1,0},{2,1},{3,2},{4,3},{5,4},{6,5},{7,6},{8,7},{9,8},{10,9},{11,1... | collective-permute-start | bytes 3145736 | tf_op jit(solution)/shard_map/ppermute | solution.py:820
  154.3 28.0 %collective-permute-start.1 = (bf16[1024,512]{1,0:T(8,128)(2,1)}, bf16[1024,512]{1,0:T(8,128)(2,1)}, u32[]{:S(2)}, u32[]{:S(2)}) collective-permute-start(bf16[1024,512]{1,0:T(8,128)(2,1)} %get-tuple-element.40.own_ref), channel_id=1, source_target_pairs={{0,1},{1,2},{2,3},{3,4},{4,5},{5,6},{6,7},{7,8},{8,9},{9,10},{10,1... | collective-permute-start | bytes 3145736 | tf_op jit(solution)/shard_map/ppermute | solution.py:825
  187.9 57.3 %all-to-all-start.2 = ((bf16[128,16,512]{2,1,0:T(8,128)(2,1)}), bf16[128,16,512]{2,1,0:T(8,128)(2,1)}, u32[]{:S(2)}, u32[]{:S(2)}) async-start(bf16[128,16,512]{2,1,0:T(8,128)(2,1)} %bitcast.18), calls=%async_computation.2 | async-start | bytes 4194304 | tf_op jit(solution)/shard_map/all_to_all | solution.py:808
  197.5 47.7 %collective-permute-start.4 = (f32[512,640]{1,0:T(8,128)}, f32[512,640]{1,0:T(8,128)}, u32[]{:S(2)}, u32[]{:S(2)}) collective-permute-start(f32[512,640]{1,0:T(8,128)} %get-tuple-element.52), channel_id=1, source_target_pairs={{0,1},{1,0},{2,3},{3,2},{4,5},{5,4},{6,7},{7,6},{8,9},{9,8},{10,11... | collective-permute-start | bytes 3932168 | tf_op jit(solution)/shard_map/ppermute | solution.py:830
  225.0 20.2 %collective-permute-start.3 = (bf16[1024,512]{1,0:T(8,128)(2,1)}, bf16[1024,512]{1,0:T(8,128)(2,1)}, u32[]{:S(2)}, u32[]{:S(2)}) collective-permute-start(bf16[1024,512]{1,0:T(8,128)(2,1)} %get-tuple-element.50.own_ref), channel_id=1, source_target_pairs={{0,1},{1,2},{2,3},{3,4},{4,5},{5,6},{6,7},{7,8},{8,9},{9,10},{10,1... | collective-permute-start | bytes 3145736 | tf_op jit(solution)/shard_map/ppermute | solution.py:825
  225.5 13.7 %collective-permute-start.5 = (f32[512,384]{1,0:T(8,128)}, f32[512,384]{1,0:T(8,128)S(1)}, u32[]{:S(2)}, u32[]{:S(2)}) collective-permute-start(f32[512,384]{1,0:T(8,128)} %get-tuple-element.54), channel_id=1, source_target_pairs={{0,1},{1,0},{2,3},{3,2},{4,5},{5,4},{6,7},{7,6},{8,9},{9,8},{10,11... | collective-permute-start | bytes 2359304 | tf_op jit(solution)/shard_map/ppermute | solution.py:830
  226.2 3.0 collective-permute-start.6
  229.8 3.6 %collective-permute-start.7 = (f32[8,128]{1,0:T(8,128)S(1)}, f32[8,128]{1,0:T(8,128)S(1)}, u32[]{:S(2)}, u32[]{:S(2)}) collective-permute-start(f32[8,128]{1,0:T(8,128)S(1)} %add.18), channel_id=1, source_target_pairs={{0,2},{1,3},{2,0},{3,1},{4,6},{5,7},{6,4},{7,5},{8,10},{9,11},{10,... | collective-permute-start | bytes 12296 | tf_op jit(solution)/shard_map/ppermute | solution.py:836
  233.5 5.2 %collective-permute-start.8 = (f32[8,128]{1,0:T(8,128)S(1)}, f32[8,128]{1,0:T(8,128)S(1)}, u32[]{:S(2)}, u32[]{:S(2)}) collective-permute-start(f32[8,128]{1,0:T(8,128)S(1)} %add.19), channel_id=1, source_target_pairs={{0,4},{1,5},{2,6},{3,7},{4,0},{5,1},{6,2},{7,3},{8,12},{9,13},{10,... | collective-permute-start | bytes 12296 | tf_op jit(solution)/shard_map/ppermute | solution.py:836
  239.3 5.9 %copy-start.2 = (f32[512,384]{1,0:T(8,128)}, f32[512,384]{1,0:T(8,128)S(1)}, u32[]{:S(2)}) copy-start(f32[512,384]{1,0:T(8,128)S(1)} %collective-permute-done.5.refs_3_) | copy-start | bytes 2359300
  252.3 51.0 %all-to-all-start.3 = ((bf16[128,16,768]{2,1,0:T(8,128)(2,1)}), bf16[128,16,768]{2,1,0:T(8,128)(2,1)}, u32[]{:S(2)}, u32[]{:S(2)}) async-start(bf16[128,16,768]{2,1,0:T(8,128)(2,1)} %bitcast.16), calls=%async_computation.3 | async-start | bytes 6291456 | tf_op jit(solution)/shard_map/all_to_all | solution.py:808
  305.5 16.3 %all-to-all-start.4 = ((f32[16,16,640]{2,1,0:T(8,128)}), f32[16,16,640]{2,1,0:T(8,128)S(1)}, u32[]{:S(2)}, u32[]{:S(2)}) async-start(f32[16,16,640]{2,1,0:T(8,128)} %add_tiles.1.refs_0_), calls=%async_computation.4 | async-start | bytes 1310720 | tf_op jit(solution)/shard_map/all_to_all | solution.py:911
  321.8 0.8 copy-start.1
Sparse Core Ops, SparseCore 0:
  33.3 39.5 all-gather.1

commit v3 on v2

--- a/solution.py
+++ b/solution.py
@@ -66,6 +66,13 @@
     return nn(chosen, rows).astype(BF16)
 
 
+def seat(shard):
+    core, along_y = shard & 1, (shard >> 1) & 3
+    along_z, along_x = (shard >> 3) & 3, shard >> 5
+    y, z = (along_y - along_z) & 3, (along_z - along_x) & 3
+    return (((along_x << 2) + z << 2) + y << 1) + core
+
+
 def slot_targets(count, dest_ref, target_ref, devices):
     arrived = dest_ref.shape[1]
     capacity = arrived // devices
@@ -74,7 +81,7 @@
     base = jnp.zeros((devices, 1), F32)
     for start in range(0, arrived, chunk):
         cols = pl.ds(start, chunk)
-        dest = dest_ref[:, cols]
+        dest = seat(dest_ref[:, cols])
         valid = iota((1, chunk), 1) + start < count
         here = jnp.where((iota((devices, chunk), 0) == dest) & valid, 1.0, 0.0)
         ahead = nn(here.astype(BF16), before) + base
@@ -83,7 +90,8 @@
         target_ref[:, cols] = jnp.where(valid, dest * capacity + rank, -1)
 
 
-def send_first_kernel(devices, shift_ref, count_ref, dest_ref, slot_ref, rows_ref, send_ref, target_ref):
+def send_first_kernel(devices, shift_ref, count_ref, dest_ref, slot_ref, rows_ref, *refs):
+    send_ref, target_ref = refs[-2:]
     step = pl.program_id(0)
 
     @pl.when(step == 0)
@@ -98,13 +106,14 @@
     send_ref[:, width:] = nt(chosen, jnp.broadcast_to(code, (MARK_COLS, arrived)).astype(BF16)).astype(BF16)
 
 
-def send_first(shift, count, dest, slot, rows, devices, block=512):
+def send_first(shift, count, dest, slot, rows, devices, after, block=512):
     arrived, width = rows.shape
     wide = width + MARK_COLS
     return pl.pallas_call(
         functools.partial(send_first_kernel, devices),
         grid=(arrived // block,),
-        in_specs=[SMEM, SMEM, whole((1, arrived)), whole((1, arrived)), whole((arrived, width))],
+        in_specs=[SMEM, SMEM, whole((1, arrived)), whole((1, arrived)), whole((arrived, width))]
+        + [ANY] * len(after),
         out_specs=[pl.BlockSpec((block, wide), lambda i: (i, 0)), whole((1, arrived))],
         out_shape=[
             jax.ShapeDtypeStruct((arrived, wide), BF16),
@@ -113,7 +122,7 @@
         compiler_params=params(),
         cost_estimate=lasting(9),
         name="send_points",
-    )(shift, count, dest, slot, rows)
+    )(shift, count, dest, slot, rows, *after)
 
 
 def pick_kernel(index_ref, rows_ref, *refs):
@@ -154,14 +163,21 @@
         place_ref[:, start : start + chunk] = jnp.where(here > 0.0, place, -1)
 
 
+def halves_out(first, second, index_row, rows):
+    half = first.shape[0]
+    first[...] = pick_rows(index_row, rows, 0, half)
+    second[...] = pick_rows(index_row, rows, half, half)
+
+
 def land_first_kernel(shift_ref, marks_ref, rows_ref, *refs):
-    own_ref, place_ref = refs[-2:]
+    first_ref, second_ref, place_ref = refs[-3:]
     places(shift_ref[0], marks_ref, place_ref)
-    own_ref[...] = pick_rows(place_ref[...], rows_ref[...], 0, PATCH)
+    halves_out(first_ref, second_ref, place_ref[...], rows_ref[...])
 
 
 def land_first(shift, got, width, after):
     slots, wide = got.shape
+    half = PATCH // 2
     return pl.pallas_call(
         land_first_kernel,
         grid=(1,),
@@ -171,9 +187,10 @@
             pl.BlockSpec((slots, width), lambda i: (0, 0)),
         ]
         + [ANY] * len(after),
-        out_specs=[whole((PATCH, width)), whole((1, slots))],
+        out_specs=[whole((half, width)), whole((half, width)), whole((1, slots))],
         out_shape=[
-            jax.ShapeDtypeStruct((PATCH, width), BF16),
+            jax.ShapeDtypeStruct((half, width), BF16),
+            jax.ShapeDtypeStruct((half, width), BF16),
             jax.ShapeDtypeStruct((1, slots), jnp.int32),
         ],
         compiler_params=params(),
@@ -182,8 +199,27 @@
     )(shift, got, got, *after)
 
 
-def pack_kernel(in_ref, out_ref, gain_ref, *refs):
-    packed_ref = refs[-1]
+def land_second_kernel(place_ref, rows_ref, *refs):
+    first_ref, second_ref = refs[-2:]
+    halves_out(first_ref, second_ref, place_ref[...], rows_ref[...])
+
+
+def land_second(place, got, after):
+    slots, width = got.shape
+    half = PATCH // 2
+    return pl.pallas_call(
+        land_second_kernel,
+        grid=(1,),
+        in_specs=[whole((1, slots)), whole((slots, width))] + [ANY] * len(after),
+        out_specs=[whole((half, width)), whole((half, width))],
+        out_shape=[jax.ShapeDtypeStruct((half, width), BF16)] * 2,
+        compiler_params=params(),
+        cost_estimate=lasting(5),
+        name="land_cot",
+    )(place, got, *after)
+
+
+def pack_kernel(in_ref, out_ref, gain_ref, packed_ref):
     inner, outer = in_ref.shape[1], out_ref.shape[1]
     packed_ref[:, :inner] = in_ref[...]
     packed_ref[:, inner : inner + outer] = out_ref[...]
@@ -191,20 +227,19 @@
     packed_ref[:, inner + outer :] = column.astype(BF16)
 
 
-def pack(project_in, project_out, gain, after):
+def pack(project_in, project_out, gain):
     share = project_in.shape[0]
     columns = project_in.shape[1] + project_out.shape[1] + GAIN_COLS
     return pl.pallas_call(
         pack_kernel,
         grid=(1,),
-        in_specs=[whole(project_in.shape), whole(project_out.shape), whole((1, share))]
-        + [ANY] * len(after),
+        in_specs=[whole(project_in.shape), whole(project_out.shape), whole((1, share))],
         out_specs=whole((share, columns)),
         out_shape=jax.ShapeDtypeStruct((share, columns), BF16),
         compiler_params=params(),
         cost_estimate=lasting(1),
         name="pack_weights",
-    )(project_in, project_out, gain.reshape(1, share), *after)
+    )(project_in, project_out, gain.reshape(1, share))
 
 
 def column_of(row):
@@ -242,13 +277,13 @@
     )(index, rows, *after)
 
 
-def spread_pair_kernel(groups, shift_ref, index_ref, own_ref, other_ref, *refs):
+def spread_pair_kernel(groups, shift_ref, index_ref, first_rows, second_rows, top_ref, bottom_ref, *refs):
     out_ref, rows = refs[-2:]
     step = pl.program_id(0)
 
     @pl.when(step == 0)
     def _():
-        rows[...] = joined(shift_ref[0], own_ref, other_ref)
+        rows[...] = joined(shift_ref[0], first_rows, second_rows, top_ref, bottom_ref)
 
     width = rows.shape[1]
     out_ref[:, :width] = spread_rows(index_ref[...], rows[...])
@@ -274,7 +309,7 @@
 
 def spread_pair(shift, index, pair, name, parts=(), groups=None, after=()):
     slots = index.shape[1]
-    source, width = pair[0].shape
+    half, width = pair[0].shape
     blocks = groups[1] // TILE_ROWS if parts else 4
     wide = width + sum(part.shape[1] for part in parts[::2]) * LANES // width
     block = slots // blocks
@@ -282,12 +317,12 @@
         functools.partial(spread_pair_kernel, groups),
         grid=(blocks,),
         in_specs=[SMEM, pl.BlockSpec((1, block), lambda i: (0, i))]
-        + [whole((source, width))] * 2
+        + [whole((half, width))] * 4
         + [whole(part.shape) for part in parts]
         + [ANY] * len(after),
         out_specs=pl.BlockSpec((block, wide), lambda i: (i, 0)),
         out_shape=jax.ShapeDtypeStruct((slots, wide), BF16),
-        scratch_shapes=[pltpu.VMEM((source, width), BF16)],
+        scratch_shapes=[pltpu.VMEM((2 * half, width), BF16)],
         compiler_params=params(),
         cost_estimate=lasting(6),
         name=name,
@@ -369,25 +404,13 @@
     )(member, tiles)
 
 
-def gate_kernel(*refs):
-    pass
-
-
-def gate(array, *after):
-    return pl.pallas_call(
-        gate_kernel,
-        in_specs=[ANY] * (1 + len(after)),
-        out_specs=ANY,
-        out_shape=jax.ShapeDtypeStruct(array.shape, array.dtype),
-        input_output_aliases={0: 0},
-        compiler_params=pltpu.CompilerParams(has_side_effects=True),
-        name="gate",
-    )(array, *after)
-
-
-def joined(shift, own_ref, other_ref):
-    row = iota(own_ref.shape, 0)
-    return jnp.where(row < PATCH - shift, own_ref[...], other_ref[...])
+def joined(shift, first_ref, second_ref, top_ref, bottom_ref):
+    half, width = top_ref.shape
+    edge = PATCH - shift
+    row = iota((half, width), 0)
+    first = jnp.where((2 * shift > PATCH) & (row < edge), top_ref[...], first_ref[...])
+    second = jnp.where((2 * shift <= PATCH) & (row + half >= edge), bottom_ref[...], second_ref[...])
+    return jnp.concatenate([first, second], axis=0)
 
 
 def attend(key_x, query_x, value, probs_ref, out_ref, step):
@@ -408,8 +431,10 @@
 def forward_first_kernel(
     shift_ref,
     wrap_ref,
-    own_ref,
-    other_ref,
+    first_rows,
+    second_rows,
+    top_ref,
+    bottom_ref,
     in_ref,
     gain_ref,
     probs_ref,
@@ -428,7 +453,7 @@
 
     @pl.when(step == 0)
     def _():
-        rows = joined(shift_ref[0], own_ref, other_ref)
+        rows = joined(shift_ref[0], first_rows, second_rows, top_ref, bottom_ref)
         values_in = jnp.transpose(rows.astype(F32))
         center = values_in - jnp.mean(values_in, axis=0, keepdims=True)
         inverse = lax.rsqrt(jnp.mean(center * center, axis=0, keepdims=True) + EPS)
@@ -457,8 +482,10 @@
 
 def forward_last_kernel(
     shift_ref,
-    own_ref,
-    other_ref,
+    first_rows,
+    second_rows,
+    top_ref,
+    bottom_ref,
     out_ref,
     query_x,
     key_x,
@@ -466,20 +493,23 @@
     first_ref,
     probs_ref,
     attended_ref,
-    block_ref,
+    block_first,
+    block_second,
 ):
     step = pl.program_id(0)
-    length, width = own_ref.shape
+    length, width = 2 * top_ref.shape[0], top_ref.shape[1]
     attend(key_x, query_x, value_ref, probs_ref, attended_ref, step)
 
     @pl.when(step == pl.num_programs(0) - 1)
     def _():
-        rows = joined(shift_ref[0], own_ref, other_ref)
+        rows = joined(shift_ref[0], first_rows, second_rows, top_ref, bottom_ref)
         attended = jnp.concatenate(
             [r[...].reshape(width // 2, length) for r in (first_ref, attended_ref)], axis=0
         )
         added = nn(jnp.transpose(out_ref[...]), attended)
-        block_ref[...] = (rows.astype(F32) + jnp.transpose(added)).astype(BF16)
+        block = (rows.astype(F32) + jnp.transpose(added)).astype(BF16)
+        block_first[...] = block[: length // 2]
+        block_second[...] = block[length // 2 :]
 
 
 def per_step(shape, first):
@@ -487,14 +517,15 @@
 
 
 def forward(shift, wrap, pair, weights):
-    length, width = pair[0].shape
+    half, width = pair[0].shape
+    length = 2 * half
     head_width = width // HEADS
     some = HEADS // 2
     count = FORWARD_HEADS
     extended = (HEADS, head_width + 16, length)
     split = (HEADS, head_width, length)
     first_split = (some, head_width, length)
-    rows_specs = [whole((length, width))] * 2
+    rows_specs = [whole((half, width))] * 4
     probs_a, hidden, normed, inverse, query_x, key_x, values, attended_a = pl.pallas_call(
         forward_first_kernel,
         grid=(some // count,),
@@ -529,7 +560,7 @@
         name="forward_first",
     )(shift, wrap, *pair, weights, weights)
     skip = some // count
-    probs_b, attended_b, block = pl.pallas_call(
+    probs_b, attended_b, *block = pl.pallas_call(
         forward_last_kernel,
         grid=(some // count,),
         in_specs=[SMEM]
@@ -544,12 +575,14 @@
         out_specs=[
             per_step((count, length, length), 0),
             whole(first_split),
-            whole((length, width)),
+            whole((half, width)),
+            whole((half, width)),
         ],
         out_shape=[
             jax.ShapeDtypeStruct((some, length, length), PROBS),
             jax.ShapeDtypeStruct(first_split, BF16),
-            jax.ShapeDtypeStruct((length, width), BF16),
+            jax.ShapeDtypeStruct((half, width), BF16),
+            jax.ShapeDtypeStruct((half, width), BF16),
         ],
         compiler_params=params(),
         cost_estimate=lasting(20),
@@ -588,8 +621,10 @@
 
 def backward_first_kernel(
     shift_ref,
-    own_ref,
-    other_ref,
+    first_rows,
+    second_rows,
+    top_ref,
+    bottom_ref,
     out_ref,
     probs_ref,
     query_x,
@@ -613,7 +648,7 @@
 
     @pl.when(step == 0)
     def _():
-        rows = joined(shift_ref[0], own_ref, other_ref)
+        rows = joined(shift_ref[0], first_rows, second_rows, top_ref, bottom_ref)
         cot_ref[...] = rows
         upstream = nt(out_ref[...], rows).astype(BF16).reshape(2, some, head_width, length)
         upstream_a[...] = upstream[0]
@@ -666,7 +701,7 @@
     core_ref,
     *refs,
 ):
-    grad_ref, keep_ref, send_ref, gain_out, grads = refs[-5:]
+    grad_first, grad_second, keep_ref, send_ref, gain_out, grads = refs[-6:]
     step = pl.program_id(0)
     length, width = cot_ref.shape
     half = width // 2
@@ -695,11 +730,14 @@
         middle = jnp.mean(scaled, axis=0, keepdims=True)
         slope = jnp.mean(scaled * normed, axis=0, keepdims=True)
         change = inverse_ref[...] * (scaled - middle - normed * slope)
-        grad_ref[...] = (cot_ref[...].astype(F32) + jnp.transpose(change)).astype(BF16)
+        grad = (cot_ref[...].astype(F32) + jnp.transpose(change)).astype(BF16)
+        grad_first[...] = grad[: length // 2]
+        grad_second[...] = grad[length // 2 :]
 
 
 def backward_first(shift, pair, weights, probs, split, attended, hidden, core):
-    length, width = pair[0].shape
+    half, width = pair[0].shape
+    length = 2 * half
     head_width = width // HEADS
     some = HEADS // 2
     count = BACKWARD_HEADS
@@ -710,8 +748,10 @@
         grid=(some // count,),
         in_specs=[
             SMEM,
-            whole((length, width)),
-            whole((length, width)),
+            whole((half, width)),
+            whole((half, width)),
+            whole((half, width)),
+            whole((half, width)),
             pl.BlockSpec((width, width), lambda h: (0, 3)),
             per_step((count, length, length), 0),
             per_step(extended, 0),
@@ -774,13 +814,15 @@
         ]
         + [ANY] * len(after),
         out_specs=[
-            whole((length, width)),
+            whole((length // 2, width)),
+            whole((length // 2, width)),
             whole((width, 3 * width // 4)),
             whole((width, 3 * width // 4)),
             whole((8, LANES)),
         ],
         out_shape=[
-            jax.ShapeDtypeStruct((length, width), BF16),
+            jax.ShapeDtypeStruct((length // 2, width), BF16),
+            jax.ShapeDtypeStruct((length // 2, width), BF16),
             jax.ShapeDtypeStruct((width, 3 * width // 4), F32),
             jax.ShapeDtypeStruct((width, 3 * width // 4), F32),
             jax.ShapeDtypeStruct((8, LANES), F32),
@@ -815,14 +857,18 @@
     return moved.reshape(rows.shape)
 
 
-def with_ahead(rows, devices):
-    pairs = [((i + 1) % devices, i) for i in range(devices)]
-    return rows, lax.ppermute(rows, BOTH, pairs)
-
-
-def with_behind(rows, devices):
-    pairs = [(i, (i + 1) % devices) for i in range(devices)]
-    return rows, lax.ppermute(rows, BOTH, pairs)
+def with_neighbours(first, second):
+    devices = lax.axis_size(BOTH)
+    ahead = [(seat(i), seat((i + 1) % devices)) for i in range(devices)]
+    behind = [(j, i) for i, j in ahead]
+    return first, second, lax.ppermute(first, BOTH, ahead), lax.ppermute(second, BOTH, behind)
+
+
+def with_neighbours_back(first, second):
+    devices = lax.axis_size(BOTH)
+    ahead = [(seat(i), seat((i + 1) % devices)) for i in range(devices)]
+    behind = [(j, i) for i, j in ahead]
+    return first, second, lax.ppermute(first, BOTH, behind), lax.ppermute(second, BOTH, ahead)
 
 
 def other_core(array):
@@ -830,12 +876,54 @@
     return lax.ppermute(array, "fsdp", pairs)
 
 
-def over_fsdp(terms):
-    count, far = lax.axis_size("fsdp"), 1
+def over_chips(terms):
+    count, far = lax.axis_size("fsdp"), 2
     while far < count:
         terms = terms + lax.ppermute(terms, "fsdp", [(i, i ^ far) for i in range(count)])
         far *= 2
     return terms
+
+
+def curve_work(shift_offset, got_points, send_cot, weights):
+    devices, groups = lax.axis_size(BOTH), lax.axis_size("dp")
+    width, share = send_cot.shape[1], weights.shape[0] // lax.axis_size("fsdp")
+    edge_device = jnp.where(2 * shift_offset <= PATCH, seat(devices - 1), seat(0))
+    wrap = (lax.axis_index(BOTH) == edge_device).astype(jnp.int32)
+    core = (lax.axis_index("fsdp") % 2).astype(jnp.int32).reshape(1)
+
+    *own_points, place = land_first(shift_offset, got_points, width, (send_cot,))
+    points_pair = with_neighbours(*own_points)
+    got_cot = exchange(send_cot, devices)
+    block, (probs_a, probs_b), split, attended, (hidden, normed, inverse) = forward(
+        shift_offset, wrap, points_pair, weights
+    )
+    cot_pair = with_neighbours(*land_second(place, got_cot, (probs_a,)))
+    block_pair = with_neighbours_back(*block)
+
+    cot, upstream, first_grads, first_keep, first_send = backward_first(
+        shift_offset, cot_pair, weights, probs_a, split, attended, hidden, core
+    )
+    spread_block = spread_pair(shift_offset, place, block_pair, "back_block", after=(first_grads,))
+    back_block = exchange(spread_block, devices)
+    *grad, last_keep, last_send, part_gain = backward_last(
+        weights,
+        probs_b,
+        (hidden, normed, inverse),
+        split,
+        attended,
+        upstream,
+        first_grads,
+        cot,
+        core,
+        (spread_block,),
+    )
+    grad_pair = with_neighbours_back(*grad)
+    parts = (first_keep, other_core(first_send), last_keep, other_core(last_send))
+    gain_terms = over_chips(part_gain)
+    spread_grad = spread_pair(
+        shift_offset, place, grad_pair, "back_grad", parts, (groups, share), (back_block, gain_terms)
+    )
+    return spread_grad, back_block, gain_terms + other_core(gain_terms)
 
 
 def body(
@@ -849,13 +937,11 @@
     project_out,
     norm_gain,
 ):
-    devices = lax.axis_size(BOTH)
-    groups = lax.axis_size("dp")
+    devices, groups = lax.axis_size(BOTH), lax.axis_size("dp")
     arrived, width = points.shape
     share = project_in.shape[0]
-    device = lax.axis_index(BOTH)
-    wrap = (device == devices - 1).astype(jnp.int32).reshape(1)
-
+    packed = pack(project_in, project_out, norm_gain)
+    weights = lax.all_gather(packed, "fsdp", axis=0, tiled=True)
     send_points, target = send_first(
         shift_offset,
         point_counts,
@@ -863,55 +949,19 @@
         curve_slot.reshape(1, arrived),
         points,
         devices,
+        (packed,),
     )
     got_points = exchange(send_points, devices)
-    packed = pack(project_in, project_out, norm_gain, (target,))
-    weights = lax.all_gather(packed, "fsdp", axis=0, tiled=True)
     send_cot = pick(target, cotangent, arrived, "send_cot")
-    own_points, place = land_first(shift_offset, got_points, width, (send_cot,))
-    points_pair = with_ahead(own_points, devices)
-    got_cot = exchange(gate(send_cot, points_pair[1]), devices)
-
-    block, (probs_a, probs_b), split, attended, (hidden, normed, inverse) = forward(
-        shift_offset, wrap, points_pair, weights
-    )
-    own_cot = pick(place, got_cot, PATCH, "land_cot", (probs_a,), PATCH)
-    cot_pair = with_ahead(own_cot, devices)
-    block_pair = with_behind(block, devices)
-
-    member = lax.axis_index("fsdp").astype(jnp.int32)
-    core = (member % 2).reshape(1)
-    cot, upstream, first_grads, first_keep, first_send = backward_first(
-        shift_offset, cot_pair, weights, probs_a, split, attended, hidden, core
-    )
-    spread_block = spread_pair(shift_offset, place, block_pair, "back_block", after=(first_grads,))
-    back_block = exchange(spread_block, devices)
-    grad, last_keep, last_send, part_gain = backward_last(
-        weights,
-        probs_b,
-        (hidden, normed, inverse),
-        split,
-        attended,
-        upstream,
-        first_grads,
-        cot,
-        core,
-        (spread_block,),
-    )
-    grad_pair = with_behind(grad, devices)
-    dealt = (groups, share)
-    parts = (first_keep, other_core(first_send), last_keep, other_core(last_send))
-    gain_terms = over_fsdp(part_gain)
-    spread_grad = spread_pair(
-        shift_offset, place, grad_pair, "back_grad", parts, dealt, (back_block, gain_terms)
-    )
+    spread_grad, back_block, gain_terms = curve_work(shift_offset, got_points, send_cot, weights)
     back_grad = exchange(spread_grad, devices)
     block_out = spread(target, back_block, width, "block_out", (spread_grad,))
     sums = add_tiles(back_grad, gain_terms, width, groups, (block_out,))
     tiles = lax.all_to_all(sums, "dp", split_axis=0, concat_axis=0, tiled=True)
     point_grad = spread(target, back_grad, width, "point_grad", (sums,))
-    columns = (first_keep.shape[1], last_keep.shape[1])
-    grad_in, grad_out, grad_gain = settle(member.reshape(1), tiles, dealt, columns, width)
+    columns = (5 * width // 4, 3 * width // 4)
+    member = lax.axis_index("fsdp").astype(jnp.int32).reshape(1)
+    grad_in, grad_out, grad_gain = settle(member, tiles, (groups, share), columns, width)
     return block_out, point_grad, grad_in, grad_out, grad_gain.reshape(share)
 
 

time: 332 us -> 320 us (0.964)
  waiting for transfers between devices: 98.7 us -> 83.2 us
    ppermute x7 -> x10, waiting for transfers between devices: 27.1 us -> 16.8 us  [the longest x2 9.95 us: over_chips(): lax.ppermute(terms, 'fsdp', [(i, i ^ far) for i in range(count)])]
    all_to_all x4, waiting for transfers between devices: 66.5 us -> 60.1 us  [exchange(): lax.all_to_all(rows.reshape(devices, rows.shape[0] // devices, rows.shape...]
    pallas_call x2 -> x1, Pallas kernels: 12.3 us -> 7.5 us  [pick(): pl.pallas_call(pick_kernel, grid=(out_rows // block,), in_specs=[whole((1...]
    pallas_call x1, Pallas kernels: 0.01 us -> 4.75 us  [land_second(): pl.pallas_call(land_second_kernel, grid=(1,), in_specs=[whole((1, slots))...]
    ppermute x7 -> x10, starting transfers between devices: 7.9 us -> 12 us  [the longest x2 6.86 us: with_neighbours(): lax.ppermute(second, BOTH, behind)]
    all_to_all x4, starting transfers between devices: 40.7 us -> 37.1 us  [exchange(): lax.all_to_all(rows.reshape(devices, rows.shape[0] // devices, rows.shape...]
  transfers between devices with their start and end apart: 15 -> 19, of which waited for: 9 -> 8; matrix products, arithmetic and copies ran while one was open for 0% -> 1% of each run, Pallas kernels for 39% -> 43%
where the time goes in v3:
time: 320 us; the launch traced here: 319 us
  Pallas kernels  161 us (50%)
  waiting for transfers between devices  83.2 us (26%)
  starting transfers between devices  53.5 us (17%)
  between operations  15.5 us (5%)
  local copies, waits for them, and re-layouts  3.53 us (1%)
    all_to_all x4, waiting for transfers between devices, exchange(): lax.all_to_all(rows.reshape(devices, rows.shape[0] // devices, rows.shape...  60.1 us
    all_to_all x4, starting transfers between devices, exchange(): lax.all_to_all(rows.reshape(devices, rows.shape[0] // devices, rows.shape...  37.1 us
    pallas_call x1, Pallas kernels, backward_first(): pl.pallas_call(backward_first_kernel, grid=(some // count,), in_specs=[SM...  27.8 us
    pallas_call x1, Pallas kernels, backward_last(): pl.pallas_call(backward_last_kernel, grid=(some // count,), in_specs=[pl....  27.4 us
    pallas_call x1, Pallas kernels, forward(): pl.pallas_call(forward_first_kernel, grid=(some // count,), in_specs=[SME...  23.7 us
    pallas_call x1, Pallas kernels, forward(): pl.pallas_call(forward_last_kernel, grid=(some // count,), in_specs=[SMEM...  21 us
    pallas_call x2, Pallas kernels, spread(): pl.pallas_call(spread_kernel, grid=(slots // block,), in_specs=[pl.BlockS...  15.3 us
    pallas_call x2, Pallas kernels, spread_pair(): pl.pallas_call(functools.partial(spread_pair_kernel, groups), grid=(block...  12.8 us
  transfers between devices with their start and end apart: 19, of which 8 were waited for; matrix products, arithmetic and copies ran while one was open for 1% of the time, Pallas kernels for 43%

profile of v3, /device:TPU:0, one launch (start us, length us, event | category | flops | bytes accessed | tf_op | source)
XLA Modules:
  0.0 318.9 jit_solution(17924488715966202763)
XLA Ops:
  10.3 10.2 %send_points.1 = (bf16[2048,640]{1,0:T(8,128)(2,1)}, s32[1,2048]{1,0:T(1,128)}) custom-call(s32[1]{0:T(128)S(6)} %copy.15.shift_ref, s32[1]{0:T(128)S(6)} %copy.14.count_ref, s32[1,2048]{1,0:T(1,128)} %bitcast.19, s32[1,2048]{1,0:T(1,128)} %bitcast.20, bf16[2048,512]{1,0:T(8,128)(2,1)} %rows_ref.2, bf16[64,2176]{1,0:T(8,128)(2,1)} %pack_weights.1.refs_0_), custom_call_target="tpu_custom_call" | custom-call | flops 8999999488 | tf_op jit(solution)/shard_map/send_points/pallas_call | solution.py:112
  20.5 11.6 %all-to-all-start = ((bf16[128,16,640]{2,1,0:T(8,128)(2,1)}), bf16[128,16,640]{2,1,0:T(8,128)(2,1)}, u32[]{:S(2)}, u32[]{:S(2)}) async-start(bf16[128,16,640]{2,1,0:T(8,128)(2,1)} %bitcast.16), calls=%async_computation | async-start | bytes 5242880 | tf_op jit(solution)/shard_map/all_to_all | solution.py:850
  32.1 7.5 %send_cot.1.refs_0_ = bf16[2048,512]{1,0:T(8,128)(2,1)} custom-call(s32[1,2048]{1,0:T(1,128)} %get-tuple-element.37.index_ref, bf16[2048,512]{1,0:T(8,128)(2,1)} %rows_ref.3), custom_call_target="tpu_custom_call" | custom-call | flops 8000000000 | tf_op jit(solution)/shard_map/send_cot/pallas_call | solution.py:136
  39.6 28.2 %all-to-all-done = bf16[128,16,640]{2,1,0:T(8,128)(2,1)} async-done(((bf16[128,16,640]{2,1,0:T(8,128)(2,1)}), bf16[128,16,640]{2,1,0:T(8,128)(2,1)}, u32[]{:S(2)}, u32[]{:S(2)}) %all-to-all-start) | async-done | bytes 2621472 | tf_op jit(solution)/shard_map/all_to_all | solution.py:850
  67.8 5.2 %land_points.1 = (bf16[512,512]{1,0:T(8,128)(2,1)}, bf16[512,512]{1,0:T(8,128)(2,1)}, s32[1,2048]{1,0:T(1,128)}) custom-call(s32[1]{0:T(128)S(6)} %copy.15.shift_ref, bf16[2048,640]{1,0:T(8,128)(2,1)} %bitcast.4.marks_ref.rows_ref, bf16[2048,640]{1,0:T(8,128)(2,1)} %bitcast.4.marks_ref.rows_ref, bf16[2048,512]{1,0:T(8,128)(2,1)} %send_cot.1.refs_0_), custom_call_target="tpu_custom_call" | custom-call | flops 7000000000 | tf_op jit(solution)/shard_map/land_points/pallas_call | solution.py:181
  73.0 3.0 collective-permute-start.1
  75.9 6.0 %all-to-all-start.1 = ((bf16[128,16,512]{2,1,0:T(8,128)(2,1)}), bf16[128,16,512]{2,1,0:T(8,128)(2,1)}, u32[]{:S(2)}, u32[]{:S(2)}) async-start(bf16[128,16,512]{2,1,0:T(8,128)(2,1)} %bitcast.17), calls=%async_computation.1 | async-start | bytes 4194304 | tf_op jit(solution)/shard_map/all_to_all | solution.py:850
  83.0 5.8 %collective-permute-done.1.bottom_ref = bf16[512,512]{1,0:T(8,128)(2,1)} collective-permute-done((bf16[512,512]{1,0:T(8,128)(2,1)}, bf16[512,512]{1,0:T(8,128)(2,1)}, u32[]{:S(2)}, u32[]{:S(2)}) %collective-permute-start.1) | collective-permute-done | bytes 524320 | tf_op jit(solution)/shard_map/ppermute | solution.py:864
  88.8 23.7 %forward_first.1 = (f32[8,1024,1024]{2,1,0:T(8,128)}, bf16[512,1024]{1,0:T(8,128)(2,1)}, f32[512,1024]{1,0:T(8,128)}, f32[1,1024]{1,0:T(1,128)}, bf16[16,48,1024...) custom-call(s32[1]{0:T(128)S(6)} %copy.15.shift_ref, ...), custom_call_target="tpu_custom_call" | custom-call | flops 24999999488 | tf_op jit(solution)/shard_map/forward_first/pallas_call | solution.py:529
  112.5 4.7 %land_cot.1 = (bf16[512,512]{1,0:T(8,128)(2,1)}, bf16[512,512]{1,0:T(8,128)(2,1)}) custom-call(s32[1,2048]{1,0:T(1,128)} %get-tuple-element.39.place_ref.index_ref, bf16[2048,512]{1,0:T(8,128)(2,1)} %bitcast.7.rows_ref, f32[8,1024,1024]{2,1,0:T(8,128)} %get-tuple-element.48.refs_0_.probs_ref), custom_call_target="tpu_custom_call" | custom-call | flops 5000000000 | tf_op jit(solution)/shard_map/land_cot/pallas_call | solution.py:210
  117.2 3.9 %collective-permute-start.5 = (bf16[512,512]{1,0:T(8,128)(2,1)}, bf16[512,512]{1,0:T(8,128)(2,1)}, u32[]{:S(2)}, u32[]{:S(2)}) collective-permute-start(bf16[512,512]{1,0:T(8,128)(2,1)} %get-tuple-element.50.second_rows), channel_id=1, source_target_pairs={{1,0},{2,1},{3,2},{4,3},{5,4},{6,5},{7,6},{14,7},{15,14},{8,15},{9... | collective-permute-start | bytes 1572872 | tf_op jit(solution)/shard_map/ppermute | solution.py:864
  121.1 21.0 %forward_last.1 = (f32[8,1024,1024]{2,1,0:T(8,128)}, bf16[8,32,1024]{2,1,0:T(8,128)(2,1)}, bf16[512,512]{1,0:T(8,128)(2,1)}, bf16[512,512]{1,0:T(8,128)(2,1)}) custom-call(s32[1]{0:T(128)S(6)} %copy.15.shift_ref, bf16[512,512]{1,0:T(8,128)(2,1)} %get-tuple-element.40.first_rows, bf16[512,512]{1,0:T(8,128)(2,1)} %get-tuple-element.41.second_rows, ...), custom_call_target="tpu_custom_call" | custom-call | flops 20000000000 | tf_op jit(solution)/shard_map/forward_last/pallas_call | solution.py:563
  143.7 27.8 %backward_first.1 = (bf16[1024,512]{1,0:T(8,128)(2,1)}, bf16[8,32,1024]{2,1,0:T(8,128)(2,1)}, bf16[3,8,32,1024]{3,2,1,0:T(8,128)(2,1)}, f32[512,640]{1,0:T(8,128)}, f32[512,640]{1,0:T(8,128)}) custom-call(s32[1]{0:T(128)S(6)} %copy.15.shift_ref, bf16[512,512]{1,0:T(8,128)(2,1)} %get-tuple-element.49.first_rows, ...), custom_call_target="tpu_custom_call" | custom-call | flops 24999999488 | tf_op jit(solution)/shard_map/backward_first/pallas_call | solution.py:746
  171.5 5.7 %back_block.1.refs_0_ = bf16[2048,512]{1,0:T(8,128)(2,1)} custom-call(s32[1]{0:T(128)S(6)} %copy.15.shift_ref, s32[1,2048]{1,0:T(1,128)} %get-tuple-element.39.place_ref.index_ref, bf16[512,512]{1,0:T(8,128)(2,1)} %get-tuple-element.46.first_rows, bf16[512,512]{1,0:T(8,128)(2,1)} %get-tuple-element.47.second_rows, ...), custom_call_target="tpu_custom_call" | custom-call | flops 6000000000 | tf_op jit(solution)/shard_map/back_block/pallas_call | solution.py:316
  177.2 9.3 %all-to-all-start.2 = ((bf16[128,16,512]{2,1,0:T(8,128)(2,1)}), bf16[128,16,512]{2,1,0:T(8,128)(2,1)}, u32[]{:S(2)}, u32[]{:S(2)}) async-start(bf16[128,16,512]{2,1,0:T(8,128)(2,1)} %bitcast.18), calls=%async_computation.2 | async-start | bytes 4194304 | tf_op jit(solution)/shard_map/all_to_all | solution.py:850
  186.6 27.4 %backward_last.1 = (bf16[512,512]{1,0:T(8,128)(2,1)}, bf16[512,512]{1,0:T(8,128)(2,1)}, f32[512,384]{1,0:T(8,128)}, f32[512,384]{1,0:T(8,128)}, f32[8,128]{1,0:T(8,128)}) custom-call(bf16[512,2176]{1,0:T(8,128)(2,1)} %all-gather.2.cloned.1.call-done.in_ref.gain_ref.out_ref, bf16[512,2176]{1,0:T(8,128)(2,1)} %all-gather.2.cloned.1.call-done.in_ref.gain_ref.out_ref, ...), custom_call_target="tpu_custom_call" | custom-call | flops 24999999488 | tf_op jit(solution)/shard_map/backward_last/pallas_call | solution.py:796
  216.4 7.3 %collective-permute-done.10 = f32[8,128]{1,0:T(8,128)S(1)} collective-permute-done((f32[8,128]{1,0:T(8,128)}, f32[8,128]{1,0:T(8,128)S(1)}, u32[]{:S(2)}, u32[]{:S(2)}) %collective-permute-start.10) | collective-permute-done | bytes 4128 | tf_op jit(solution)/shard_map/ppermute | solution.py:882
  232.0 7.1 %back_grad.1.refs_0_ = bf16[2048,768]{1,0:T(8,128)(2,1)} custom-call(s32[1]{0:T(128)S(6)} %copy.15.shift_ref, s32[1,2048]{1,0:T(1,128)} %get-tuple-element.39.place_ref.index_ref, bf16[512,512]{1,0:T(8,128)(2,1)} %get-tuple-element.59.first_rows, bf16[512,512]{1,0:T(8,128)(2,1)} %get-tuple-element.60.second_rows, bf16[512,512]{1,0:T(8,128)(2,1)} %copy-done.4, ...), custom_call_target="tpu_custom_call" | custom-call | flops 6000000000 | tf_op jit(solution)/shard_map/back_grad/pallas_call | solution.py:316
  239.1 10.2 %all-to-all-start.3 = ((bf16[128,16,768]{2,1,0:T(8,128)(2,1)}), bf16[128,16,768]{2,1,0:T(8,128)(2,1)}, u32[]{:S(2)}, u32[]{:S(2)}) async-start(bf16[128,16,768]{2,1,0:T(8,128)(2,1)} %bitcast.15), calls=%async_computation.3 | async-start | bytes 6291456 | tf_op jit(solution)/shard_map/all_to_all | solution.py:850
  251.2 7.6 %block_out.1.refs_0_ = bf16[2048,512]{1,0:T(8,128)(2,1)} custom-call(s32[1,2048]{1,0:T(1,128)} %get-tuple-element.37.index_ref, bf16[2048,512]{1,0:T(8,128)(2,1)} %bitcast.10.refs_4_.rows_ref, bf16[2048,768]{1,0:T(8,128)(2,1)} %back_grad.1.refs_0_), custom_call_target="tpu_custom_call" | custom-call | flops 8000000000 | tf_op jit(solution)/shard_map/block_out/pallas_call | solution.py:267
  258.8 31.9 %all-to-all-done.3 = bf16[128,16,768]{2,1,0:T(8,128)(2,1)} async-done(((bf16[128,16,768]{2,1,0:T(8,128)(2,1)}), bf16[128,16,768]{2,1,0:T(8,128)(2,1)}, u32[]{:S(2)}, u32[]{:S(2)}) %all-to-all-start.3) | async-done | bytes 3145760 | tf_op jit(solution)/shard_map/all_to_all | solution.py:850
  293.0 3.6 %all-to-all-start.4 = ((f32[16,16,640]{2,1,0:T(8,128)}), f32[16,16,640]{2,1,0:T(8,128)S(1)}, u32[]{:S(2)}, u32[]{:S(2)}) async-start(f32[16,16,640]{2,1,0:T(8,128)} %add_tiles.1.refs_0_), calls=%async_computation.4 | async-start | bytes 1310720 | tf_op jit(solution)/shard_map/all_to_all | solution.py:960
  296.6 7.6 %point_grad.1 = bf16[2048,512]{1,0:T(8,128)(2,1)} custom-call(s32[1,2048]{1,0:T(1,128)} %get-tuple-element.37.index_ref, bf16[2048,768]{1,0:T(8,128)(2,1)} %bitcast.12.tiles_ref.rows_ref, f32[16,16,640]{2,1,0:T(8,128)} %add_tiles.1.refs_0_), custom_call_target="tpu_custom_call" | custom-call | flops 8000000000 | tf_op jit(solution)/shard_map/point_grad/pallas_call | solution.py:267
  304.2 5.1 %all-to-all-done.4.tiles_ref = f32[16,16,640]{2,1,0:T(8,128)S(1)} async-done(((f32[16,16,640]{2,1,0:T(8,128)}), f32[16,16,640]{2,1,0:T(8,128)S(1)}, u32[]{:S(2)}, u32[]{:S(2)}) %all-to-all-start.4) | async-done | bytes 655392 | tf_op jit(solution)/shard_map/all_to_all | solution.py:960
  (47 shorter events, 22.2 us)
Async XLA Ops:
  7.2 81.6 %all-gather.2.cloned.1.call-start = ((), (), s32[]{:S(2)}) async-start(), calls=%async_computation.5 | async-start | bytes 2506752 | tf_op jit(solution)/shard_map/all_gather | solution.py:944
  20.5 47.3 %all-to-all-start = ((bf16[128,16,640]{2,1,0:T(8,128)(2,1)}), bf16[128,16,640]{2,1,0:T(8,128)(2,1)}, u32[]{:S(2)}, u32[]{:S(2)}) async-start(bf16[128,16,640]{2,1,0:T(8,128)(2,1)} %bitcast.16), calls=%async_computation | async-start | bytes 5242880 | tf_op jit(solution)/shard_map/all_to_all | solution.py:850
  73.0 10.0 %collective-permute-start = (bf16[512,512]{1,0:T(8,128)(2,1)}, bf16[512,512]{1,0:T(8,128)(2,1)S(1)}, u32[]{:S(2)}, u32[]{:S(2)}) collective-permute-start(bf16[512,512]{1,0:T(8,128)(2,1)} %get-tuple-element.40.first_rows), channel_id=1, source_target_pairs={{0,1},{1,2},{2,3},{3,4},{4,5},{5,6},{6,7},{7,14},{14,15},{15,8},{8... | collective-permute-start | bytes 1572872 | tf_op jit(solution)/shard_map/ppermute | solution.py:864
  73.0 15.8 %collective-permute-start.1 = (bf16[512,512]{1,0:T(8,128)(2,1)}, bf16[512,512]{1,0:T(8,128)(2,1)}, u32[]{:S(2)}, u32[]{:S(2)}) collective-permute-start(bf16[512,512]{1,0:T(8,128)(2,1)} %get-tuple-element.41.second_rows), channel_id=1, source_target_pairs={{1,0},{2,1},{3,2},{4,3},{5,4},{6,5},{7,6},{14,7},{15,14},{8,15},{9... | collective-permute-start | bytes 1572872 | tf_op jit(solution)/shard_map/ppermute | solution.py:864
  75.9 36.5 %all-to-all-start.1 = ((bf16[128,16,512]{2,1,0:T(8,128)(2,1)}), bf16[128,16,512]{2,1,0:T(8,128)(2,1)}, u32[]{:S(2)}, u32[]{:S(2)}) async-start(bf16[128,16,512]{2,1,0:T(8,128)(2,1)} %bitcast.17), calls=%async_computation.1 | async-start | bytes 4194304 | tf_op jit(solution)/shard_map/all_to_all | solution.py:850
  83.0 5.8 %copy-start.3 = (bf16[512,512]{1,0:T(8,128)(2,1)}, bf16[512,512]{1,0:T(8,128)(2,1)S(1)}, u32[]{:S(2)}) copy-start(bf16[512,512]{1,0:T(8,128)(2,1)S(1)} %collective-permute-done.top_ref) | copy-start | bytes 1572868
  117.2 25.7 %collective-permute-start.4 = (bf16[512,512]{1,0:T(8,128)(2,1)}, bf16[512,512]{1,0:T(8,128)(2,1)S(1)}, u32[]{:S(2)}, u32[]{:S(2)}) collective-permute-start(bf16[512,512]{1,0:T(8,128)(2,1)} %get-tuple-element.49.first_rows), channel_id=1, source_target_pairs={{0,1},{1,2},{2,3},{3,4},{4,5},{5,6},{6,7},{7,14},{14,15},{15,8},{8... | collective-permute-start | bytes 1572872 | tf_op jit(solution)/shard_map/ppermute | solution.py:864
  117.2 25.7 %collective-permute-start.5 = (bf16[512,512]{1,0:T(8,128)(2,1)}, bf16[512,512]{1,0:T(8,128)(2,1)}, u32[]{:S(2)}, u32[]{:S(2)}) collective-permute-start(bf16[512,512]{1,0:T(8,128)(2,1)} %get-tuple-element.50.second_rows), channel_id=1, source_target_pairs={{1,0},{2,1},{3,2},{4,3},{5,4},{6,5},{7,6},{14,7},{15,14},{8,15},{9... | collective-permute-start | bytes 1572872 | tf_op jit(solution)/shard_map/ppermute | solution.py:864
  142.1 29.4 %collective-permute-start.2 = (bf16[512,512]{1,0:T(8,128)(2,1)}, bf16[512,512]{1,0:T(8,128)(2,1)}, u32[]{:S(2)}, u32[]{:S(2)}) collective-permute-start(bf16[512,512]{1,0:T(8,128)(2,1)} %get-tuple-element.46.first_rows), channel_id=1, source_target_pairs={{1,0},{2,1},{3,2},{4,3},{5,4},{6,5},{7,6},{14,7},{15,14},{8,15},{9... | collective-permute-start | bytes 1572872 | tf_op jit(solution)/shard_map/ppermute | solution.py:871
  142.9 28.6 %collective-permute-start.3 = (bf16[512,512]{1,0:T(8,128)(2,1)}, bf16[512,512]{1,0:T(8,128)(2,1)}, u32[]{:S(2)}, u32[]{:S(2)}) collective-permute-start(bf16[512,512]{1,0:T(8,128)(2,1)} %get-tuple-element.47.second_rows), channel_id=1, source_target_pairs={{0,1},{1,2},{2,3},{3,4},{4,5},{5,6},{6,7},{7,14},{14,15},{15,8},{8... | collective-permute-start | bytes 1572872 | tf_op jit(solution)/shard_map/ppermute | solution.py:871
  177.2 53.9 %all-to-all-start.2 = ((bf16[128,16,512]{2,1,0:T(8,128)(2,1)}), bf16[128,16,512]{2,1,0:T(8,128)(2,1)}, u32[]{:S(2)}, u32[]{:S(2)}) async-start(bf16[128,16,512]{2,1,0:T(8,128)(2,1)} %bitcast.18), calls=%async_computation.2 | async-start | bytes 4194304 | tf_op jit(solution)/shard_map/all_to_all | solution.py:850
  186.5 44.6 %collective-permute-start.8 = (f32[512,640]{1,0:T(8,128)}, f32[512,640]{1,0:T(8,128)}, u32[]{:S(2)}, u32[]{:S(2)}) collective-permute-start(f32[512,640]{1,0:T(8,128)} %get-tuple-element.62), channel_id=1, source_target_pairs={{0,1},{1,0},{2,3},{3,2},{4,5},{5,4},{6,7},{7,6},{8,9},{9,8},{10,11... | collective-permute-start | bytes 3932168 | tf_op jit(solution)/shard_map/ppermute | solution.py:876
  214.0 16.1 %collective-permute-start.9 = (f32[512,384]{1,0:T(8,128)}, f32[512,384]{1,0:T(8,128)S(1)}, u32[]{:S(2)}, u32[]{:S(2)}) collective-permute-start(f32[512,384]{1,0:T(8,128)} %get-tuple-element.64), channel_id=1, source_target_pairs={{0,1},{1,0},{2,3},{3,2},{4,5},{5,4},{6,7},{7,6},{8,9},{9,8},{10,11... | collective-permute-start | bytes 2359304 | tf_op jit(solution)/shard_map/ppermute | solution.py:876
  214.5 15.5 %collective-permute-start.6 = (bf16[512,512]{1,0:T(8,128)(2,1)}, bf16[512,512]{1,0:T(8,128)(2,1)S(1)}, u32[]{:S(2)}, u32[]{:S(2)}) collective-permute-start(bf16[512,512]{1,0:T(8,128)(2,1)} %get-tuple-element.59.first_rows), channel_id=1, source_target_pairs={{1,0},{2,1},{3,2},{4,3},{5,4},{6,5},{7,6},{14,7},{15,14},{8,15},{9... | collective-permute-start | bytes 1572872 | tf_op jit(solution)/shard_map/ppermute | solution.py:871
  216.4 13.7 %collective-permute-start.7 = (bf16[512,512]{1,0:T(8,128)(2,1)}, bf16[512,512]{1,0:T(8,128)(2,1)S(1)}, u32[]{:S(2)}, u32[]{:S(2)}) collective-permute-start(bf16[512,512]{1,0:T(8,128)(2,1)} %get-tuple-element.60.second_rows), channel_id=1, source_target_pairs={{0,1},{1,2},{2,3},{3,4},{4,5},{5,6},{6,7},{7,14},{14,15},{15,8},{8... | collective-permute-start | bytes 1572872 | tf_op jit(solution)/shard_map/ppermute | solution.py:871
  216.4 7.3 %collective-permute-start.10 = (f32[8,128]{1,0:T(8,128)}, f32[8,128]{1,0:T(8,128)S(1)}, u32[]{:S(2)}, u32[]{:S(2)}) collective-permute-start(f32[8,128]{1,0:T(8,128)} %get-tuple-element.65), channel_id=1, source_target_pairs={{0,2},{1,3},{2,0},{3,1},{4,6},{5,7},{6,4},{7,5},{8,10},{9,11},{10,... | collective-permute-start | bytes 12296 | tf_op jit(solution)/shard_map/ppermute | solution.py:882
  224.4 5.1 %collective-permute-start.11 = (f32[8,128]{1,0:T(8,128)S(1)}, f32[8,128]{1,0:T(8,128)S(1)}, u32[]{:S(2)}, u32[]{:S(2)}) collective-permute-start(f32[8,128]{1,0:T(8,128)S(1)} %add.18), channel_id=1, source_target_pairs={{0,4},{1,5},{2,6},{3,7},{4,0},{5,1},{6,2},{7,3},{8,12},{9,13},{10,... | collective-permute-start | bytes 12296 | tf_op jit(solution)/shard_map/ppermute | solution.py:882
  230.1 1.0 copy-start.5
  231.1 0.9 copy-start.2
  239.1 10.3 %copy-start.1 = (f32[8,128]{1,0:T(8,128)S(1)}, f32[8,128]{1,0:T(8,128)}, u32[]{:S(2)}) copy-start(f32[8,128]{1,0:T(8,128)} %add.19.refs_5_) | copy-start | bytes 12292
  239.1 51.6 %all-to-all-start.3 = ((bf16[128,16,768]{2,1,0:T(8,128)(2,1)}), bf16[128,16,768]{2,1,0:T(8,128)(2,1)}, u32[]{:S(2)}, u32[]{:S(2)}) async-start(bf16[128,16,768]{2,1,0:T(8,128)(2,1)} %bitcast.15), calls=%async_computation.3 | async-start | bytes 6291456 | tf_op jit(solution)/shard_map/all_to_all | solution.py:850
  249.4 1.2 collective-permute-start.12
  293.0 16.3 %all-to-all-start.4 = ((f32[16,16,640]{2,1,0:T(8,128)}), f32[16,16,640]{2,1,0:T(8,128)S(1)}, u32[]{:S(2)}, u32[]{:S(2)}) async-start(f32[16,16,640]{2,1,0:T(8,128)} %add_tiles.1.refs_0_), calls=%async_computation.4 | async-start | bytes 1310720 | tf_op jit(solution)/shard_map/all_to_all | solution.py:960
  309.3 0.9 copy-start
  (2 other events, 1.6 us)
Sparse Core Ops, SparseCore 0:
  10.3 47.8 all-gather.1

commit v4 on v3

--- a/solution.py
+++ b/solution.py
@@ -404,6 +404,48 @@
     )(member, tiles)
 
 
+def turn_kernel(in_ref, out_ref, *refs):
+    turned_ref = refs[-1]
+    width = out_ref.shape[0]
+    for part in range(3):
+        columns = slice(part * width, (part + 1) * width)
+        turned_ref[columns, :] = jnp.transpose(in_ref[:, columns])
+    turned_ref[3 * width :, :] = jnp.transpose(out_ref[...])
+
+
+def turn(weights, width, after):
+    return pl.pallas_call(
+        turn_kernel,
+        grid=(1,),
+        in_specs=[
+            pl.BlockSpec((width, 3 * width), lambda i: (0, 0)),
+            pl.BlockSpec((width, width), lambda i: (0, 3)),
+        ]
+        + [ANY] * len(after),
+        out_specs=whole((4 * width, width)),
+        out_shape=jax.ShapeDtypeStruct((4 * width, width), BF16),
+        compiler_params=params(),
+        cost_estimate=lasting(2),
+        name="turn_weights",
+    )(weights, weights, *after)
+
+
+def gate_kernel(*refs):
+    pass
+
+
+def gate(array, *after):
+    return pl.pallas_call(
+        gate_kernel,
+        in_specs=[ANY] * (1 + len(after)),
+        out_specs=ANY,
+        out_shape=jax.ShapeDtypeStruct(array.shape, array.dtype),
+        input_output_aliases={0: 0},
+        compiler_params=pltpu.CompilerParams(has_side_effects=True),
+        name="gate",
+    )(array, *after)
+
+
 def joined(shift, first_ref, second_ref, top_ref, bottom_ref):
     half, width = top_ref.shape
     edge = PATCH - shift
@@ -463,8 +505,7 @@
         hidden = (normed * gain_ref[:, :1].astype(F32)).astype(BF16)
         hidden_ref[...] = hidden
         for part, ref in enumerate((query_x, key_x, values_ref)):
-            columns = in_ref[:, part * width : (part + 1) * width]
-            made = nn(jnp.transpose(columns), hidden).astype(BF16)
+            made = nn(in_ref[part * width : (part + 1) * width, :], hidden).astype(BF16)
             ref[:, :head_width, :] = made.reshape(heads, head_width, length)
         side = iota((extra, length), 1) >= PATCH - shift_ref[0]
         line = iota((extra, length), 0)
@@ -506,7 +547,7 @@
         attended = jnp.concatenate(
             [r[...].reshape(width // 2, length) for r in (first_ref, attended_ref)], axis=0
         )
-        added = nn(jnp.transpose(out_ref[...]), attended)
+        added = nn(out_ref[...], attended)
         block = (rows.astype(F32) + jnp.transpose(added)).astype(BF16)
         block_first[...] = block[: length // 2]
         block_second[...] = block[length // 2 :]
@@ -516,7 +557,7 @@
     return pl.BlockSpec(shape, lambda i: (i + first, 0, 0))
 
 
-def forward(shift, wrap, pair, weights):
+def forward(shift, wrap, pair, weights, turned):
     half, width = pair[0].shape
     length = 2 * half
     head_width = width // HEADS
@@ -532,7 +573,7 @@
         in_specs=[SMEM, SMEM]
         + rows_specs
         + [
-            pl.BlockSpec((width, 3 * width), lambda h: (0, 0)),
+            pl.BlockSpec((3 * width, width), lambda h: (0, 0)),
             pl.BlockSpec((width, GAIN_COLS), lambda h: (0, 4 * width // GAIN_COLS)),
         ],
         out_specs=[
@@ -558,7 +599,7 @@
         compiler_params=params(),
         cost_estimate=lasting(25),
         name="forward_first",
-    )(shift, wrap, *pair, weights, weights)
+    )(shift, wrap, *pair, turned, weights)
     skip = some // count
     probs_b, attended_b, *block = pl.pallas_call(
         forward_last_kernel,
@@ -566,7 +607,7 @@
         in_specs=[SMEM]
         + rows_specs
         + [
-            pl.BlockSpec((width, width), lambda h: (0, 3)),
+            pl.BlockSpec((width, width), lambda h: (3, 0)),
             per_step((count,) + extended[1:], skip),
             per_step((count,) + extended[1:], skip),
             per_step((count,) + split[1:], skip),
@@ -587,7 +628,7 @@
         compiler_params=params(),
         cost_estimate=lasting(20),
         name="forward_last",
-    )(shift, *pair, weights, query_x, key_x, values, attended_a)
+    )(shift, *pair, turned, query_x, key_x, values, attended_a)
     return block, (probs_a, probs_b), (query_x, key_x, values), (attended_a, attended_b), (
         hidden,
         normed,
@@ -893,9 +934,10 @@
 
     *own_points, place = land_first(shift_offset, got_points, width, (send_cot,))
     points_pair = with_neighbours(*own_points)
-    got_cot = exchange(send_cot, devices)
+    turned = turn(weights, width, (place,))
+    got_cot = exchange(gate(send_cot, turned), devices)
     block, (probs_a, probs_b), split, attended, (hidden, normed, inverse) = forward(
-        shift_offset, wrap, points_pair, weights
+        shift_offset, wrap, points_pair, weights, turned
     )
     cot_pair = with_neighbours(*land_second(place, got_cot, (probs_a,)))
     block_pair = with_neighbours_back(*block)

time: 320 us -> 318 us (level)
  starting transfers between devices: 53.5 us -> 49.1 us
  Pallas kernels: 161 us -> 165 us
    ppermute x2, waiting for transfers between devices: 5.79 us -> 0.01 us  [with_neighbours(): lax.ppermute(second, BOTH, behind)]
    all_to_all x4, waiting for transfers between devices: 60.1 us -> 65.5 us  [exchange(): lax.all_to_all(rows.reshape(devices, rows.shape[0] // devices, rows.shape...]
    pallas_call x0 -> x2, Pallas kernels: none -> 3.43 us  [the longest x1 3.43 us: turn(): pl.pallas_call(turn_kernel, grid=(1,), in_specs=[pl.BlockSpec((width, 3 *...]
    all_to_all x4, starting transfers between devices: 37.1 us -> 33.7 us  [exchange(): lax.all_to_all(rows.reshape(devices, rows.shape[0] // devices, rows.shape...]
  transfers between devices with their start and end apart: 19 -> 19, of which waited for: 8 -> 7; matrix products, arithmetic and copies ran while one was open for 1% -> 1% of each run, Pallas kernels for 43% -> 45%
where the time goes in v4:
time: 318 us; the launch traced here: 317 us
  Pallas kernels  165 us (52%)
  waiting for transfers between devices  81.7 us (26%)
  starting transfers between devices  49.1 us (15%)
  between operations  15.5 us (5%)
  local copies, waits for them, and re-layouts  4.34 us (1%)
    all_to_all x4, waiting for transfers between devices, exchange(): lax.all_to_all(rows.reshape(devices, rows.shape[0] // devices, rows.shape...  65.5 us
    all_to_all x4, starting transfers between devices, exchange(): lax.all_to_all(rows.reshape(devices, rows.shape[0] // devices, rows.shape...  33.7 us
    pallas_call x1, Pallas kernels, backward_first(): pl.pallas_call(backward_first_kernel, grid=(some // count,), in_specs=[SM...  27.9 us
    pallas_call x1, Pallas kernels, backward_last(): pl.pallas_call(backward_last_kernel, grid=(some // count,), in_specs=[pl....  27.4 us
    pallas_call x1, Pallas kernels, forward(): pl.pallas_call(forward_first_kernel, grid=(some // count,), in_specs=[SME...  23.6 us
    pallas_call x1, Pallas kernels, forward(): pl.pallas_call(forward_last_kernel, grid=(some // count,), in_specs=[SMEM...  20.9 us
    pallas_call x2, Pallas kernels, spread(): pl.pallas_call(spread_kernel, grid=(slots // block,), in_specs=[pl.BlockS...  15.3 us
    pallas_call x2, Pallas kernels, spread_pair(): pl.pallas_call(functools.partial(spread_pair_kernel, groups), grid=(block...  12.8 us
  transfers between devices with their start and end apart: 19, of which 7 were waited for; matrix products, arithmetic and copies ran while one was open for 1% of the time, Pallas kernels for 45%

profile of v4, /device:TPU:0, one launch (start us, length us, event | category | flops | bytes accessed | tf_op | source)
XLA Modules:
  0.0 317.3 jit_solution(3668654083306404012)
XLA Ops:
  10.3 10.2 %send_points.1 = (bf16[2048,640]{1,0:T(8,128)(2,1)}, s32[1,2048]{1,0:T(1,128)}) custom-call(s32[1]{0:T(128)S(6)} %copy.17.shift_ref, s32[1]{0:T(128)S(6)} %copy.16.count_ref, s32[1,2048]{1,0:T(1,128)} %bitcast.19, s32[1,2048]{1,0:T(1,128)} %bitcast.20, bf16[2048,512]{1,0:T(8,128)(2,1)} %rows_ref.2, bf16[64,2176]{1,0:T(8,128)(2,1)} %pack_weights.1.refs_0_), custom_call_target="tpu_custom_call" | custom-call | flops 8999999488 | tf_op jit(solution)/shard_map/send_points/pallas_call | solution.py:112
  20.5 11.6 %all-to-all-start = ((bf16[128,16,640]{2,1,0:T(8,128)(2,1)}), bf16[128,16,640]{2,1,0:T(8,128)(2,1)}, u32[]{:S(2)}, u32[]{:S(2)}) async-start(bf16[128,16,640]{2,1,0:T(8,128)(2,1)} %bitcast.17), calls=%async_computation | async-start | bytes 5242880 | tf_op jit(solution)/shard_map/all_to_all | solution.py:891
  32.1 7.5 %send_cot.1.refs_0_ = bf16[2048,512]{1,0:T(8,128)(2,1)} custom-call(s32[1,2048]{1,0:T(1,128)} %get-tuple-element.37.index_ref, bf16[2048,512]{1,0:T(8,128)(2,1)} %rows_ref.3), custom_call_target="tpu_custom_call" | custom-call | flops 8000000000 | tf_op jit(solution)/shard_map/send_cot/pallas_call | solution.py:136
  39.6 28.2 %all-to-all-done = bf16[128,16,640]{2,1,0:T(8,128)(2,1)} async-done(((bf16[128,16,640]{2,1,0:T(8,128)(2,1)}), bf16[128,16,640]{2,1,0:T(8,128)(2,1)}, u32[]{:S(2)}, u32[]{:S(2)}) %all-to-all-start) | async-done | bytes 2621472 | tf_op jit(solution)/shard_map/all_to_all | solution.py:891
  67.8 5.2 %land_points.1 = (bf16[512,512]{1,0:T(8,128)(2,1)}, bf16[512,512]{1,0:T(8,128)(2,1)}, s32[1,2048]{1,0:T(1,128)}) custom-call(s32[1]{0:T(128)S(6)} %copy.17.shift_ref, bf16[2048,640]{1,0:T(8,128)(2,1)} %bitcast.4.marks_ref.rows_ref, bf16[2048,640]{1,0:T(8,128)(2,1)} %bitcast.4.marks_ref.rows_ref, bf16[2048,512]{1,0:T(8,128)(2,1)} %send_cot.1.refs_0_), custom_call_target="tpu_custom_call" | custom-call | flops 7000000000 | tf_op jit(solution)/shard_map/land_points/pallas_call | solution.py:181
  73.0 3.0 collective-permute-start.1
  75.9 3.4 %turn_weights.1.in_ref.out_ref.refs_1_ = bf16[2048,512]{1,0:T(8,128)(2,1)} custom-call(bf16[512,2176]{1,0:T(8,128)(2,1)} %all-gather.2.cloned.1.call-done.in_ref.out_ref.gain_ref, bf16[512,2176]{1,0:T(8,128)(2,1)} %all-gather.2.cloned.1.call-done.in_ref.out_ref.gain_ref, s32[1,2048]{1,0:T(1,128)} %get-tuple-element.39.refs_0_.place_ref.index_ref), custom_call_target="tpu_custom_call" | custom-call | flops 2000000000 | tf_op jit(solution)/shard_map/turn_weights/pallas_call | solution.py:417
  79.4 6.0 %all-to-all-start.1 = ((bf16[128,16,512]{2,1,0:T(8,128)(2,1)}), bf16[128,16,512]{2,1,0:T(8,128)(2,1)}, u32[]{:S(2)}, u32[]{:S(2)}) async-start(bf16[128,16,512]{2,1,0:T(8,128)(2,1)} %bitcast.15), calls=%async_computation.1 | async-start | bytes 4194304 | tf_op jit(solution)/shard_map/all_to_all | solution.py:891
  86.2 23.6 %forward_first.1 = (f32[8,1024,1024]{2,1,0:T(8,128)}, bf16[512,1024]{1,0:T(8,128)(2,1)}, f32[512,1024]{1,0:T(8,128)}, f32[1,1024]{1,0:T(1,128)}, bf16[16,48,1024...) custom-call(s32[1]{0:T(128)S(6)} %copy.17.shift_ref, ...), custom_call_target="tpu_custom_call" | custom-call | flops 24999999488 | tf_op jit(solution)/shard_map/forward_first/pallas_call | solution.py:570
  109.7 5.4 %all-to-all-done.1 = bf16[128,16,512]{2,1,0:T(8,128)(2,1)} async-done(((bf16[128,16,512]{2,1,0:T(8,128)(2,1)}), bf16[128,16,512]{2,1,0:T(8,128)(2,1)}, u32[]{:S(2)}, u32[]{:S(2)}) %all-to-all-start.1) | async-done | bytes 2097184 | tf_op jit(solution)/shard_map/all_to_all | solution.py:891
  115.2 4.7 %land_cot.1 = (bf16[512,512]{1,0:T(8,128)(2,1)}, bf16[512,512]{1,0:T(8,128)(2,1)}) custom-call(s32[1,2048]{1,0:T(1,128)} %get-tuple-element.39.refs_0_.place_ref.index_ref, bf16[2048,512]{1,0:T(8,128)(2,1)} %bitcast.7.rows_ref, f32[8,1024,1024]{2,1,0:T(8,128)} %get-tuple-element.48.refs_0_.probs_ref), custom_call_target="tpu_custom_call" | custom-call | flops 5000000000 | tf_op jit(solution)/shard_map/land_cot/pallas_call | solution.py:210
  122.9 20.9 %forward_last.1 = (f32[8,1024,1024]{2,1,0:T(8,128)}, bf16[8,32,1024]{2,1,0:T(8,128)(2,1)}, bf16[512,512]{1,0:T(8,128)(2,1)}, bf16[512,512]{1,0:T(8,128)(2,1)}) custom-call(s32[1]{0:T(128)S(6)} %copy.17.shift_ref, bf16[512,512]{1,0:T(8,128)(2,1)} %get-tuple-element.40.first_rows, bf16[512,512]{1,0:T(8,128)(2,1)} %get-tuple-element.41.second_rows, ...), custom_call_target="tpu_custom_call" | custom-call | flops 20000000000 | tf_op jit(solution)/shard_map/forward_last/pallas_call | solution.py:604
  145.4 27.9 %backward_first.1 = (bf16[1024,512]{1,0:T(8,128)(2,1)}, bf16[8,32,1024]{2,1,0:T(8,128)(2,1)}, bf16[3,8,32,1024]{3,2,1,0:T(8,128)(2,1)}, f32[512,640]{1,0:T(8,128)}, f32[512,640]{1,0:T(8,128)}) custom-call(s32[1]{0:T(128)S(6)} %copy.17.shift_ref, bf16[512,512]{1,0:T(8,128)(2,1)} %get-tuple-element.49.first_rows, ...), custom_call_target="tpu_custom_call" | custom-call | flops 24999999488 | tf_op jit(solution)/shard_map/backward_first/pallas_call | solution.py:787
  173.3 5.7 %back_block.1.refs_0_ = bf16[2048,512]{1,0:T(8,128)(2,1)} custom-call(s32[1]{0:T(128)S(6)} %copy.17.shift_ref, s32[1,2048]{1,0:T(1,128)} %get-tuple-element.39.refs_0_.place_ref.index_ref, bf16[512,512]{1,0:T(8,128)(2,1)} %get-tuple-element.46.first_rows, bf16[512,512]{1,0:T(8,128)(2,1)} %get-tuple-element.47.second_rows, ...), custom_call_target="tpu_custom_call" | custom-call | flops 6000000000 | tf_op jit(solution)/shard_map/back_block/pallas_call | solution.py:316
  178.9 5.9 %all-to-all-start.2 = ((bf16[128,16,512]{2,1,0:T(8,128)(2,1)}), bf16[128,16,512]{2,1,0:T(8,128)(2,1)}, u32[]{:S(2)}, u32[]{:S(2)}) async-start(bf16[128,16,512]{2,1,0:T(8,128)(2,1)} %bitcast.18), calls=%async_computation.2 | async-start | bytes 4194304 | tf_op jit(solution)/shard_map/all_to_all | solution.py:891
  184.9 27.4 %backward_last.1 = (bf16[512,512]{1,0:T(8,128)(2,1)}, bf16[512,512]{1,0:T(8,128)(2,1)}, f32[512,384]{1,0:T(8,128)}, f32[512,384]{1,0:T(8,128)}, f32[8,128]{1,0:T(8,128)}) custom-call(bf16[512,2176]{1,0:T(8,128)(2,1)} %all-gather.2.cloned.1.call-done.in_ref.out_ref.gain_ref, bf16[512,2176]{1,0:T(8,128)(2,1)} %all-gather.2.cloned.1.call-done.in_ref.out_ref.gain_ref, ...), custom_call_target="tpu_custom_call" | custom-call | flops 24999999488 | tf_op jit(solution)/shard_map/backward_last/pallas_call | solution.py:837
  214.7 7.3 %collective-permute-done.10 = f32[8,128]{1,0:T(8,128)S(1)} collective-permute-done((f32[8,128]{1,0:T(8,128)}, f32[8,128]{1,0:T(8,128)S(1)}, u32[]{:S(2)}, u32[]{:S(2)}) %collective-permute-start.10) | collective-permute-done | bytes 4128 | tf_op jit(solution)/shard_map/ppermute | solution.py:923
  230.3 7.1 %back_grad.1.refs_0_ = bf16[2048,768]{1,0:T(8,128)(2,1)} custom-call(s32[1]{0:T(128)S(6)} %copy.17.shift_ref, s32[1,2048]{1,0:T(1,128)} %get-tuple-element.39.refs_0_.place_ref.index_ref, bf16[512,512]{1,0:T(8,128)(2,1)} %get-tuple-element.59.first_rows, bf16[512,512]{1,0:T(8,128)(2,1)} %get-tuple-element.60.second_rows, bf16[512,512]{1,0:T(8,128)(2,1)} %copy-done.4, ...), custom_call_target="tpu_custom_call" | custom-call | flops 6000000000 | tf_op jit(solution)/shard_map/back_grad/pallas_call | solution.py:316
  237.5 10.2 %all-to-all-start.3 = ((bf16[128,16,768]{2,1,0:T(8,128)(2,1)}), bf16[128,16,768]{2,1,0:T(8,128)(2,1)}, u32[]{:S(2)}, u32[]{:S(2)}) async-start(bf16[128,16,768]{2,1,0:T(8,128)(2,1)} %bitcast.16), calls=%async_computation.3 | async-start | bytes 6291456 | tf_op jit(solution)/shard_map/all_to_all | solution.py:891
  249.6 7.6 %block_out.1.refs_0_ = bf16[2048,512]{1,0:T(8,128)(2,1)} custom-call(s32[1,2048]{1,0:T(1,128)} %get-tuple-element.37.index_ref, bf16[2048,512]{1,0:T(8,128)(2,1)} %bitcast.10.refs_4_.rows_ref, bf16[2048,768]{1,0:T(8,128)(2,1)} %back_grad.1.refs_0_), custom_call_target="tpu_custom_call" | custom-call | flops 8000000000 | tf_op jit(solution)/shard_map/block_out/pallas_call | solution.py:267
  257.2 31.9 %all-to-all-done.3 = bf16[128,16,768]{2,1,0:T(8,128)(2,1)} async-done(((bf16[128,16,768]{2,1,0:T(8,128)(2,1)}), bf16[128,16,768]{2,1,0:T(8,128)(2,1)}, u32[]{:S(2)}, u32[]{:S(2)}) %all-to-all-start.3) | async-done | bytes 3145760 | tf_op jit(solution)/shard_map/all_to_all | solution.py:891
  291.3 3.6 %all-to-all-start.4 = ((f32[16,16,640]{2,1,0:T(8,128)}), f32[16,16,640]{2,1,0:T(8,128)S(1)}, u32[]{:S(2)}, u32[]{:S(2)}) async-start(f32[16,16,640]{2,1,0:T(8,128)} %add_tiles.1.refs_0_), calls=%async_computation.4 | async-start | bytes 1310720 | tf_op jit(solution)/shard_map/all_to_all | solution.py:1002
  294.9 7.6 %point_grad.1 = bf16[2048,512]{1,0:T(8,128)(2,1)} custom-call(s32[1,2048]{1,0:T(1,128)} %get-tuple-element.37.index_ref, bf16[2048,768]{1,0:T(8,128)(2,1)} %bitcast.12.tiles_ref.rows_ref, f32[16,16,640]{2,1,0:T(8,128)} %add_tiles.1.refs_0_), custom_call_target="tpu_custom_call" | custom-call | flops 8000000000 | tf_op jit(solution)/shard_map/point_grad/pallas_call | solution.py:267
  302.6 5.1 %all-to-all-done.4.tiles_ref = f32[16,16,640]{2,1,0:T(8,128)S(1)} async-done(((f32[16,16,640]{2,1,0:T(8,128)}), f32[16,16,640]{2,1,0:T(8,128)S(1)}, u32[]{:S(2)}, u32[]{:S(2)}) %all-to-all-start.4) | async-done | bytes 655392 | tf_op jit(solution)/shard_map/all_to_all | solution.py:1002
  (49 shorter events, 24.9 us)
Async XLA Ops:
  7.2 68.8 %all-gather.2.cloned.1.call-start = ((), (), s32[]{:S(2)}) async-start(), calls=%async_computation.5 | async-start | bytes 2506752 | tf_op jit(solution)/shard_map/all_gather | solution.py:986
  20.5 47.3 %all-to-all-start = ((bf16[128,16,640]{2,1,0:T(8,128)(2,1)}), bf16[128,16,640]{2,1,0:T(8,128)(2,1)}, u32[]{:S(2)}, u32[]{:S(2)}) async-start(bf16[128,16,640]{2,1,0:T(8,128)(2,1)} %bitcast.17), calls=%async_computation | async-start | bytes 5242880 | tf_op jit(solution)/shard_map/all_to_all | solution.py:891
  73.0 12.4 %collective-permute-start = (bf16[512,512]{1,0:T(8,128)(2,1)}, bf16[512,512]{1,0:T(8,128)(2,1)S(1)}, u32[]{:S(2)}, u32[]{:S(2)}) collective-permute-start(bf16[512,512]{1,0:T(8,128)(2,1)} %get-tuple-element.40.first_rows), channel_id=1, source_target_pairs={{0,1},{1,2},{2,3},{3,4},{4,5},{5,6},{6,7},{7,14},{14,15},{15,8},{8... | collective-permute-start | bytes 1572872 | tf_op jit(solution)/shard_map/ppermute | solution.py:905
  73.0 12.4 %collective-permute-start.1 = (bf16[512,512]{1,0:T(8,128)(2,1)}, bf16[512,512]{1,0:T(8,128)(2,1)}, u32[]{:S(2)}, u32[]{:S(2)}) collective-permute-start(bf16[512,512]{1,0:T(8,128)(2,1)} %get-tuple-element.41.second_rows), channel_id=1, source_target_pairs={{1,0},{2,1},{3,2},{4,3},{5,4},{6,5},{7,6},{14,7},{15,14},{8,15},{9... | collective-permute-start | bytes 1572872 | tf_op jit(solution)/shard_map/ppermute | solution.py:905
  79.4 35.8 %all-to-all-start.1 = ((bf16[128,16,512]{2,1,0:T(8,128)(2,1)}), bf16[128,16,512]{2,1,0:T(8,128)(2,1)}, u32[]{:S(2)}, u32[]{:S(2)}) async-start(bf16[128,16,512]{2,1,0:T(8,128)(2,1)} %bitcast.15), calls=%async_computation.1 | async-start | bytes 4194304 | tf_op jit(solution)/shard_map/all_to_all | solution.py:891
  85.3 0.8 copy-start.3
  119.9 24.6 %collective-permute-start.4 = (bf16[512,512]{1,0:T(8,128)(2,1)}, bf16[512,512]{1,0:T(8,128)(2,1)S(1)}, u32[]{:S(2)}, u32[]{:S(2)}) collective-permute-start(bf16[512,512]{1,0:T(8,128)(2,1)} %get-tuple-element.49.first_rows), channel_id=1, source_target_pairs={{0,1},{1,2},{2,3},{3,4},{4,5},{5,6},{6,7},{7,14},{14,15},{15,8},{8... | collective-permute-start | bytes 1572872 | tf_op jit(solution)/shard_map/ppermute | solution.py:905
  119.9 24.6 %collective-permute-start.5 = (bf16[512,512]{1,0:T(8,128)(2,1)}, bf16[512,512]{1,0:T(8,128)(2,1)}, u32[]{:S(2)}, u32[]{:S(2)}) collective-permute-start(bf16[512,512]{1,0:T(8,128)(2,1)} %get-tuple-element.50.second_rows), channel_id=1, source_target_pairs={{1,0},{2,1},{3,2},{4,3},{5,4},{6,5},{7,6},{14,7},{15,14},{8,15},{9... | collective-permute-start | bytes 1572872 | tf_op jit(solution)/shard_map/ppermute | solution.py:905
  143.7 29.5 %collective-permute-start.2 = (bf16[512,512]{1,0:T(8,128)(2,1)}, bf16[512,512]{1,0:T(8,128)(2,1)}, u32[]{:S(2)}, u32[]{:S(2)}) collective-permute-start(bf16[512,512]{1,0:T(8,128)(2,1)} %get-tuple-element.46.first_rows), channel_id=1, source_target_pairs={{1,0},{2,1},{3,2},{4,3},{5,4},{6,5},{7,6},{14,7},{15,14},{8,15},{9... | collective-permute-start | bytes 1572872 | tf_op jit(solution)/shard_map/ppermute | solution.py:912
  144.1 29.2 %collective-permute-start.3 = (bf16[512,512]{1,0:T(8,128)(2,1)}, bf16[512,512]{1,0:T(8,128)(2,1)}, u32[]{:S(2)}, u32[]{:S(2)}) collective-permute-start(bf16[512,512]{1,0:T(8,128)(2,1)} %get-tuple-element.47.second_rows), channel_id=1, source_target_pairs={{0,1},{1,2},{2,3},{3,4},{4,5},{5,6},{6,7},{7,14},{14,15},{15,8},{8... | collective-permute-start | bytes 1572872 | tf_op jit(solution)/shard_map/ppermute | solution.py:912
  178.9 50.5 %all-to-all-start.2 = ((bf16[128,16,512]{2,1,0:T(8,128)(2,1)}), bf16[128,16,512]{2,1,0:T(8,128)(2,1)}, u32[]{:S(2)}, u32[]{:S(2)}) async-start(bf16[128,16,512]{2,1,0:T(8,128)(2,1)} %bitcast.18), calls=%async_computation.2 | async-start | bytes 4194304 | tf_op jit(solution)/shard_map/all_to_all | solution.py:891
  184.9 44.6 %collective-permute-start.8 = (f32[512,640]{1,0:T(8,128)}, f32[512,640]{1,0:T(8,128)}, u32[]{:S(2)}, u32[]{:S(2)}) collective-permute-start(f32[512,640]{1,0:T(8,128)} %get-tuple-element.62), channel_id=1, source_target_pairs={{0,1},{1,0},{2,3},{3,2},{4,5},{5,4},{6,7},{7,6},{8,9},{9,8},{10,11... | collective-permute-start | bytes 3932168 | tf_op jit(solution)/shard_map/ppermute | solution.py:917
  212.3 16.1 %collective-permute-start.9 = (f32[512,384]{1,0:T(8,128)}, f32[512,384]{1,0:T(8,128)S(1)}, u32[]{:S(2)}, u32[]{:S(2)}) collective-permute-start(f32[512,384]{1,0:T(8,128)} %get-tuple-element.64), channel_id=1, source_target_pairs={{0,1},{1,0},{2,3},{3,2},{4,5},{5,4},{6,7},{7,6},{8,9},{9,8},{10,11... | collective-permute-start | bytes 2359304 | tf_op jit(solution)/shard_map/ppermute | solution.py:917
  212.9 15.6 %collective-permute-start.6 = (bf16[512,512]{1,0:T(8,128)(2,1)}, bf16[512,512]{1,0:T(8,128)(2,1)S(1)}, u32[]{:S(2)}, u32[]{:S(2)}) collective-permute-start(bf16[512,512]{1,0:T(8,128)(2,1)} %get-tuple-element.59.first_rows), channel_id=1, source_target_pairs={{1,0},{2,1},{3,2},{4,3},{5,4},{6,5},{7,6},{14,7},{15,14},{8,15},{9... | collective-permute-start | bytes 1572872 | tf_op jit(solution)/shard_map/ppermute | solution.py:912
  214.7 13.7 %collective-permute-start.7 = (bf16[512,512]{1,0:T(8,128)(2,1)}, bf16[512,512]{1,0:T(8,128)(2,1)S(1)}, u32[]{:S(2)}, u32[]{:S(2)}) collective-permute-start(bf16[512,512]{1,0:T(8,128)(2,1)} %get-tuple-element.60.second_rows), channel_id=1, source_target_pairs={{0,1},{1,2},{2,3},{3,4},{4,5},{5,6},{6,7},{7,14},{14,15},{15,8},{8... | collective-permute-start | bytes 1572872 | tf_op jit(solution)/shard_map/ppermute | solution.py:912
  214.7 7.3 %collective-permute-start.10 = (f32[8,128]{1,0:T(8,128)}, f32[8,128]{1,0:T(8,128)S(1)}, u32[]{:S(2)}, u32[]{:S(2)}) collective-permute-start(f32[8,128]{1,0:T(8,128)} %get-tuple-element.65), channel_id=1, source_target_pairs={{0,2},{1,3},{2,0},{3,1},{4,6},{5,7},{6,4},{7,5},{8,10},{9,11},{10,... | collective-permute-start | bytes 12296 | tf_op jit(solution)/shard_map/ppermute | solution.py:923
  222.7 5.1 %collective-permute-start.11 = (f32[8,128]{1,0:T(8,128)S(1)}, f32[8,128]{1,0:T(8,128)S(1)}, u32[]{:S(2)}, u32[]{:S(2)}) collective-permute-start(f32[8,128]{1,0:T(8,128)S(1)} %add.18), channel_id=1, source_target_pairs={{0,4},{1,5},{2,6},{3,7},{4,0},{5,1},{6,2},{7,3},{8,12},{9,13},{10,... | collective-permute-start | bytes 12296 | tf_op jit(solution)/shard_map/ppermute | solution.py:923
  228.5 1.0 copy-start.5
  229.5 0.9 copy-start.2
  237.5 10.2 %copy-start.1 = (f32[8,128]{1,0:T(8,128)S(1)}, f32[8,128]{1,0:T(8,128)}, u32[]{:S(2)}) copy-start(f32[8,128]{1,0:T(8,128)} %add.19.refs_5_) | copy-start | bytes 12292
  237.5 51.6 %all-to-all-start.3 = ((bf16[128,16,768]{2,1,0:T(8,128)(2,1)}), bf16[128,16,768]{2,1,0:T(8,128)(2,1)}, u32[]{:S(2)}, u32[]{:S(2)}) async-start(bf16[128,16,768]{2,1,0:T(8,128)(2,1)} %bitcast.16), calls=%async_computation.3 | async-start | bytes 6291456 | tf_op jit(solution)/shard_map/all_to_all | solution.py:891
  247.7 1.2 collective-permute-start.12
  291.3 16.3 %all-to-all-start.4 = ((f32[16,16,640]{2,1,0:T(8,128)}), f32[16,16,640]{2,1,0:T(8,128)S(1)}, u32[]{:S(2)}, u32[]{:S(2)}) async-start(f32[16,16,640]{2,1,0:T(8,128)} %add_tiles.1.refs_0_), calls=%async_computation.4 | async-start | bytes 1310720 | tf_op jit(solution)/shard_map/all_to_all | solution.py:1002
  307.6 0.9 copy-start
  (2 other events, 1.6 us)
Sparse Core Ops, SparseCore 0:
  10.3 47.8 all-gather.1
